TPU v7x, 32 devices: a whole 2x2x4 slice. The times are simulated.
32 devices in a mesh: mem: 4 (over x, core), lev: 8 (over z, y).
Axes of the slice: x: 2, y: 2, z: 4, core: 2. Of those that a mesh axis runs over, the one named last changes fastest.
Arguments:
- control: float32 [4, 128, 128, 256], P('mem', 'lev'), may hold values from -6 to 6
- diffusivity: float32 [128, 128, 256], P('lev'), may hold values from 0.02 to 0.24
- perturb: float32 [4, 49152, 128], P('mem', 'lev'), may hold values from -6 to 6
- vertical_filter: float32 [128, 128], replicated, may hold values from -0.5 to 0.5
- sub_widths: int32 [8], replicated, may hold values from 1 to 6144, 32768 in all
- obs_raw: int32 [8, 6144], P('lev'), may hold values from 0 to 1048575
- obs_counts: int32 [8], replicated, may hold values from 1 to 6144, 43008 in all
- obs_rinv: float32 [8, 6144, 128], P('lev'), may hold values from 0.3 to 3
Outputs:
- ensemble_term: float32 [4, 128, 128, 256], P('mem', 'lev')
Inputs may be any that keep to these rules, and one draw needn't show every extreme that they name: `sub_widths`: the widths sum to 32768; the largest is exactly 6144. `obs_counts`: the counts sum to 43008; the largest is exactly 6144.
All inputs are finite; a program needn't handle non-finite values.
Results may differ from a plain program's by a relative error of at most 0.00011.
Values sent between devices are 32-bit elements; how exact they have to be, the bound alone decides.
No kernel may reach another device: no remote copies, remote signals or barrier semaphores. Data moves between devices by JAX's collectives and lax.ppermute only.
A program may use at most 192 MiB of HBM per device.

v0:
```python
import math

import jax
import jax.numpy as jnp
from jax import lax
from jax.sharding import PartitionSpec as P

STEPS = 4


def diffuse(values, diffusivity):
    face_x = 0.5 * (diffusivity[..., 1:, :] + diffusivity[..., :-1, :])
    face_y = 0.5 * (diffusivity[..., :, 1:] + diffusivity[..., :, :-1])
    leading = [(0, 0)] * (values.ndim - 2)
    for repeat in range(STEPS):
        flux_x = face_x * (values[..., 1:, :] - values[..., :-1, :])
        flux_y = face_y * (values[..., :, 1:] - values[..., :, :-1])
        padded_x = jnp.pad(flux_x, leading + [(1, 1), (0, 0)])
        padded_y = jnp.pad(flux_y, leading + [(0, 0), (1, 1)])
        values = (
            values
            + (padded_x[..., 1:, :] - padded_x[..., :-1, :])
            + (padded_y[..., :, 1:] - padded_y[..., :, :-1])
        )
    return values


def slot_weights(slots, live, weights, capacity):
    block = math.gcd(capacity, 512)
    masked = jnp.where(live[:, None], weights, jnp.zeros_like(weights))

    def one_block(first):
        rows_here = first + jnp.arange(block, dtype=jnp.int32)
        onehot = (rows_here[:, None] == slots[None, :]).astype(jnp.float32)
        return jnp.dot(onehot, masked, precision=lax.Precision.HIGHEST)

    firsts = jnp.arange(capacity // block, dtype=jnp.int32) * block
    return lax.map(one_block, firsts).reshape(capacity, weights.shape[1])


def body(control, diffusivity, perturb, vertical_filter, sub_widths, obs_raw, obs_counts, obs_rinv):
    members, levels_here, size_x, size_y = control.shape
    columns = size_x * size_y
    capacity = perturb.shape[1]
    groups = sub_widths.shape[0]
    highest = lax.Precision.HIGHEST
    starts = jnp.cumsum(sub_widths) - sub_widths
    smooth = diffuse(control, diffusivity).reshape(members, levels_here, columns)
    padded = jnp.pad(smooth, ((0, 0), (0, 0), (0, capacity)), mode="edge")
    pieces = lax.map(lambda first: lax.dynamic_slice_in_dim(padded, first, capacity, 2), starts)
    outgoing = jnp.transpose(pieces, (1, 0, 3, 2)).reshape(members, groups * capacity, levels_here)
    column_form = lax.all_to_all(outgoing, "lev", split_axis=1, concat_axis=2, tiled=True)
    filtered = jnp.einsum("msk,lk->msl", column_form, vertical_filter, precision=highest)
    partial_sum = jnp.sum(perturb * filtered, axis=0)
    position = lax.axis_index("lev")
    width = sub_widths[position]
    count = obs_counts[position]
    slots = obs_raw[0] % width
    live = jnp.arange(obs_raw.shape[1], dtype=jnp.int32) < count
    obs_weight = slot_weights(slots, live, obs_rinv[0], capacity)
    increment = lax.psum(partial_sum, "mem")
    adjoint_obs = increment * obs_weight
    back_filtered = jnp.einsum(
        "msl,lk->msk", perturb * adjoint_obs[None], vertical_filter, precision=highest
    )
    returned = lax.all_to_all(back_filtered, "lev", split_axis=2, concat_axis=1, tiled=True)
    blocks = jnp.transpose(returned.reshape(members, groups, capacity, levels_here), (1, 0, 3, 2))
    offsets = jnp.arange(capacity, dtype=jnp.int32)

    def place(index, grid):
        kept = jnp.where(
            offsets[None, None, :] < sub_widths[index], blocks[index], jnp.zeros_like(blocks[index])
        )
        first = starts[index]
        current = lax.dynamic_slice_in_dim(grid, first, capacity, 2)
        return lax.dynamic_update_slice_in_dim(grid, current + kept, first, 2)

    grid = lax.fori_loop(
        0, groups, place, jnp.zeros((members, levels_here, columns + capacity), jnp.float32)
    )
    grid = grid[:, :, :columns].reshape(members, levels_here, size_x, size_y)
    return diffuse(grid, diffusivity)


def solution(mesh):
    return jax.shard_map(
        body,
        mesh=mesh,
        in_specs=(
            P("mem", "lev", None, None),
            P("lev", None, None),
            P("mem", "lev", None),
            P(),
            P(),
            P("lev", None),
            P(),
            P("lev", None, None),
        ),
        out_specs=P("mem", "lev", None, None),
        check_vma=False,
    )
```

profile of v0, /device:TPU:0, one launch (start us, length us, event | category | flops | bytes accessed | tf_op | source)
XLA Modules:
  0.0 790.4 jit_solution(2831878907063190374)
XLA Ops:
  34.3 35.7 %while.34 = (s32[]{:T(128)}, f32[8,1,16,6144]{3,2,1,0:T(8,128)}, s32[8]{0:T(128)S(1)}, f32[1,16,38912]{2,1,0:T(8,128)}, s32[]{:T(128)}, /*index=5*/s32[]{:T(128)}, s32[]{:T(128)}) while((s32[]{:T(128)}, f32[8,1,16,6144]{3,2,1,0:T(8,128)}, s32[8]{0:T(128)S(1)}, f32[1,16,38912]{2,1,0:T(8,128)}, s32[]{:T(128)}, /*index=5*/s32[]{:T(128)}, ...), condition=%wide.region_2.3_spmd, body=%wide.region_1.2_spmd.sunk | while | flops 5 | bytes 787071 | solution.py:50
  70.0 13.4 %copy.24 = f32[1,8,6144,16]{3,2,1,0:T(8,128)} copy(f32[1,8,6144,16]{2,3,0,1:T(8,128)} %bitcast.109) | data formatting | bytes 6291456 | tf_op jit(solution)/shard_map/reshape | solution.py:51
  83.9 218.7 %reduce.2 = f32[49152,16]{1,0:T(8,128)} reduce(f32[49152,1,16]{2,1,0:T(1,128)} %bitcast.100, f32[]{:T(128)} %broadcast.115), dimensions={1}, to_apply=%bitcast.77.reduce_sub_computation | reduce | bytes 6291460
  302.6 14.9 %reshape.121 = f32[8,1,98304]{2,1,0:T(1,128)} reshape(f32[49152,16]{1,0:T(8,128)} %reduce.2) | data formatting | bytes 6291456
  336.3 59.5 %all-to-all-done = f32[8,1,98304]{2,1,0:T(1,128)} async-done(((f32[8,1,98304]{2,1,0:T(1,128)}), f32[8,1,98304]{2,1,0:T(1,128)}, u32[]{:S(2)}, u32[]{:S(2)}) %all-to-all-start) | async-done | bytes 3145760 | tf_op jit(solution)/shard_map/all_to_all | solution.py:52
  395.8 11.6 %reduce.3 = f32[8,98304]{1,0:T(8,128)} reduce(f32[8,1,98304]{2,1,0:T(1,128)} %all-to-all-done, f32[]{:T(128)} %broadcast.115), dimensions={1}, to_apply=%all_to_all.20.reduce_sub_computation | reduce | bytes 6291460 | tf_op jit(solution)/shard_map/all_to_all | solution.py:52
  407.4 72.0 %reshape.122 = f32[49152,1,16]{2,1,0:T(1,128)} reshape(f32[8,98304]{1,0:T(8,128)} %reduce.3) | data formatting | bytes 6291456
  479.4 14.7 %copy.25 = f32[1,8,6144,16]{2,1,3,0:T(8,128)} copy(f32[1,8,6144,16]{3,2,1,0:T(8,128)} %bitcast.101) | data formatting | bytes 6291456 | tf_op jit(solution)/shard_map/all_to_all | solution.py:52
  505.0 113.7 %while.35 = (s32[]{:T(128)}, f32[12,512,128]{2,1,0:T(8,128)}, s32[12]{0:T(128)S(1)}, s32[6144]{0:T(1024)S(1)}, f32[6144,128]{1,0:T(8,128)}, /*index=5*/s32[]{:T(128)}) while((s32[]{:T(128)}, f32[12,512,128]{2,1,0:T(8,128)}, s32[12]{0:T(128)S(1)}, s32[6144]{0:T(1024)S(1)}, f32[6144,128]{1,0:T(8,128)}, /*index=5*/s32[]{:T(128)}) %tuple.65), condition=%wide.region_5.6_spmd, body=%wide.region_4.5_spmd.sunk | while | flops 4834984448 | bytes 3437141 | solution.py:38
  506.5 8.2 %fusion.72 = f32[12,512,128]{2,1,0:T(8,128)} fusion(f32[12,512,128]{2,1,0:T(8,128)} %get-tuple-element.340, s32[]{:T(128)} %get-tuple-element.339, f32[6144,128]{1,0:T(8,128)} %get-tuple-element.349, s32[6144]{0:T(1024)S(1)} %get-tuple-element.348, s32[512]{0:T(512)S(1)} %iota_add_fusion.2), kind=kOutput, calls=%fused_computation.7.clone.1 | convolution fusion | flops 4834983936 | bytes 3435008 | tf_op jit(solution)/shard_map/while/body/eval_jaxpr/dot_general | solution.py:35
  515.9 8.2 %fusion.72 = f32[12,512,128]{2,1,0:T(8,128)} fusion(f32[12,512,128]{2,1,0:T(8,128)} %get-tuple-element.340, s32[]{:T(128)} %get-tuple-element.339, f32[6144,128]{1,0:T(8,128)} %get-tuple-element.349, s32[6144]{0:T(1024)S(1)} %get-tuple-element.348, s32[512]{0:T(512)S(1)} %iota_add_fusion.2), kind=kOutput, calls=%fused_computation.7.clone.1 | convolution fusion | flops 4834983936 | bytes 3435008 | tf_op jit(solution)/shard_map/while/body/eval_jaxpr/dot_general | solution.py:35
  525.3 8.2 %fusion.72 = f32[12,512,128]{2,1,0:T(8,128)} fusion(f32[12,512,128]{2,1,0:T(8,128)} %get-tuple-element.340, s32[]{:T(128)} %get-tuple-element.339, f32[6144,128]{1,0:T(8,128)} %get-tuple-element.349, s32[6144]{0:T(1024)S(1)} %get-tuple-element.348, s32[512]{0:T(512)S(1)} %iota_add_fusion.2), kind=kOutput, calls=%fused_computation.7.clone.1 | convolution fusion | flops 4834983936 | bytes 3435008 | tf_op jit(solution)/shard_map/while/body/eval_jaxpr/dot_general | solution.py:35
  534.8 8.2 %fusion.72 = f32[12,512,128]{2,1,0:T(8,128)} fusion(f32[12,512,128]{2,1,0:T(8,128)} %get-tuple-element.340, s32[]{:T(128)} %get-tuple-element.339, f32[6144,128]{1,0:T(8,128)} %get-tuple-element.349, s32[6144]{0:T(1024)S(1)} %get-tuple-element.348, s32[512]{0:T(512)S(1)} %iota_add_fusion.2), kind=kOutput, calls=%fused_computation.7.clone.1 | convolution fusion | flops 4834983936 | bytes 3435008 | tf_op jit(solution)/shard_map/while/body/eval_jaxpr/dot_general | solution.py:35
  544.2 8.5 %fusion.72 = f32[12,512,128]{2,1,0:T(8,128)} fusion(f32[12,512,128]{2,1,0:T(8,128)} %get-tuple-element.340, s32[]{:T(128)} %get-tuple-element.339, f32[6144,128]{1,0:T(8,128)} %get-tuple-element.349, s32[6144]{0:T(1024)S(1)} %get-tuple-element.348, s32[512]{0:T(512)S(1)} %iota_add_fusion.2), kind=kOutput, calls=%fused_computation.7.clone.1 | convolution fusion | flops 4834983936 | bytes 3435008 | tf_op jit(solution)/shard_map/while/body/eval_jaxpr/dot_general | solution.py:35
  554.0 8.3 %fusion.72 = f32[12,512,128]{2,1,0:T(8,128)} fusion(f32[12,512,128]{2,1,0:T(8,128)} %get-tuple-element.340, s32[]{:T(128)} %get-tuple-element.339, f32[6144,128]{1,0:T(8,128)} %get-tuple-element.349, s32[6144]{0:T(1024)S(1)} %get-tuple-element.348, s32[512]{0:T(512)S(1)} %iota_add_fusion.2), kind=kOutput, calls=%fused_computation.7.clone.1 | convolution fusion | flops 4834983936 | bytes 3435008 | tf_op jit(solution)/shard_map/while/body/eval_jaxpr/dot_general | solution.py:35
  563.5 8.2 %fusion.72 = f32[12,512,128]{2,1,0:T(8,128)} fusion(f32[12,512,128]{2,1,0:T(8,128)} %get-tuple-element.340, s32[]{:T(128)} %get-tuple-element.339, f32[6144,128]{1,0:T(8,128)} %get-tuple-element.349, s32[6144]{0:T(1024)S(1)} %get-tuple-element.348, s32[512]{0:T(512)S(1)} %iota_add_fusion.2), kind=kOutput, calls=%fused_computation.7.clone.1 | convolution fusion | flops 4834983936 | bytes 3435008 | tf_op jit(solution)/shard_map/while/body/eval_jaxpr/dot_general | solution.py:35
  572.9 8.2 %fusion.72 = f32[12,512,128]{2,1,0:T(8,128)} fusion(f32[12,512,128]{2,1,0:T(8,128)} %get-tuple-element.340, s32[]{:T(128)} %get-tuple-element.339, f32[6144,128]{1,0:T(8,128)} %get-tuple-element.349, s32[6144]{0:T(1024)S(1)} %get-tuple-element.348, s32[512]{0:T(512)S(1)} %iota_add_fusion.2), kind=kOutput, calls=%fused_computation.7.clone.1 | convolution fusion | flops 4834983936 | bytes 3435008 | tf_op jit(solution)/shard_map/while/body/eval_jaxpr/dot_general | solution.py:35
  582.3 8.2 %fusion.72 = f32[12,512,128]{2,1,0:T(8,128)} fusion(f32[12,512,128]{2,1,0:T(8,128)} %get-tuple-element.340, s32[]{:T(128)} %get-tuple-element.339, f32[6144,128]{1,0:T(8,128)} %get-tuple-element.349, s32[6144]{0:T(1024)S(1)} %get-tuple-element.348, s32[512]{0:T(512)S(1)} %iota_add_fusion.2), kind=kOutput, calls=%fused_computation.7.clone.1 | convolution fusion | flops 4834983936 | bytes 3435008 | tf_op jit(solution)/shard_map/while/body/eval_jaxpr/dot_general | solution.py:35
  591.7 8.2 %fusion.72 = f32[12,512,128]{2,1,0:T(8,128)} fusion(f32[12,512,128]{2,1,0:T(8,128)} %get-tuple-element.340, s32[]{:T(128)} %get-tuple-element.339, f32[6144,128]{1,0:T(8,128)} %get-tuple-element.349, s32[6144]{0:T(1024)S(1)} %get-tuple-element.348, s32[512]{0:T(512)S(1)} %iota_add_fusion.2), kind=kOutput, calls=%fused_computation.7.clone.1 | convolution fusion | flops 4834983936 | bytes 3435008 | tf_op jit(solution)/shard_map/while/body/eval_jaxpr/dot_general | solution.py:35
  601.1 8.2 %fusion.72 = f32[12,512,128]{2,1,0:T(8,128)} fusion(f32[12,512,128]{2,1,0:T(8,128)} %get-tuple-element.340, s32[]{:T(128)} %get-tuple-element.339, f32[6144,128]{1,0:T(8,128)} %get-tuple-element.349, s32[6144]{0:T(1024)S(1)} %get-tuple-element.348, s32[512]{0:T(512)S(1)} %iota_add_fusion.2), kind=kOutput, calls=%fused_computation.7.clone.1 | convolution fusion | flops 4834983936 | bytes 3435008 | tf_op jit(solution)/shard_map/while/body/eval_jaxpr/dot_general | solution.py:35
  610.6 8.2 %fusion.72 = f32[12,512,128]{2,1,0:T(8,128)} fusion(f32[12,512,128]{2,1,0:T(8,128)} %get-tuple-element.340, s32[]{:T(128)} %get-tuple-element.339, f32[6144,128]{1,0:T(8,128)} %get-tuple-element.349, s32[6144]{0:T(1024)S(1)} %get-tuple-element.348, s32[512]{0:T(512)S(1)} %iota_add_fusion.2), kind=kOutput, calls=%fused_computation.7.clone.1 | convolution fusion | flops 4834983936 | bytes 3435008 | tf_op jit(solution)/shard_map/while/body/eval_jaxpr/dot_general | solution.py:35
  626.8 7.7 copy.22
  639.2 69.9 %all-to-all-done.1 = f32[1,6144,128]{1,0,2:T(1,128)} async-done(((f32[1,6144,128]{1,0,2:T(1,128)}), f32[1,6144,128]{1,0,2:T(1,128)}, u32[]{:S(2)}, u32[]{:S(2)}) %all-to-all-start.1) | async-done | bytes 3145760 | tf_op jit(solution)/shard_map/all_to_all | solution.py:66
  715.3 55.6 %while.36 = (s32[]{:T(128)}, f32[1,16,38912]{2,1,0:T(8,128)}, s32[8]{0:T(128)S(1)}, s32[8]{0:T(128)S(1)}, f32[8,1,16,6144]{3,2,1,0:T(8,128)}, /*index=5*/s32[]{:T(128)}, s32[]{:T(128)}, s32[]{:T(128)}) while((s32[]{:T(128)}, f32[1,16,38912]{2,1,0:T(8,128)}, s32[8]{0:T(128)S(1)}, s32[8]{0:T(128)S(1)}, f32[8,1,16,6144]{3,2,1,0:T(8,128)}, ...), condition=%wide.region_7.8_spmd.clone, body=%wide.region_6.7_spmd.clone.sunk | while | flops 202757 | bytes 1978527 | solution.py:78
  (155 shorter events, 165.0 us)
Async XLA Ops:
  6.5 491.4 %copy-start = (f32[128,128]{1,0:T(8,128)S(1)}, f32[128,128]{1,0:T(8,128)}, u32[]{:S(2)}) copy-start(f32[128,128]{1,0:T(8,128)} %param.17) | copy-start | bytes 196612
  6.5 4.8 copy-start.4
  6.5 4.8 copy-start.5
  11.9 6.8 copy-start.1
  16.7 2.0 copy-start.3
  30.9 3.2 copy-start.10
  317.6 9.3 %copy-start.9 = (s32[8]{0:T(128)S(1)}, s32[8]{0:T(128)}, u32[]{:S(2)}) copy-start(s32[8]{0:T(128)} %param.20) | copy-start | bytes 100
  317.6 10.6 %copy-start.8 = (s32[1,6144]{1,0:T(1,128)S(1)}, s32[1,6144]{1,0:T(1,128)}, u32[]{:S(2)}) copy-start(s32[1,6144]{1,0:T(1,128)} %param.19) | copy-start | bytes 73732
  317.6 78.2 %all-to-all-start = ((f32[8,1,98304]{2,1,0:T(1,128)}), f32[8,1,98304]{2,1,0:T(1,128)}, u32[]{:S(2)}, u32[]{:S(2)}) async-start(f32[8,1,98304]{2,1,0:T(1,128)} %reshape.121), calls=%async_computation | async-start | bytes 6291456 | tf_op jit(solution)/shard_map/all_to_all | solution.py:52
  325.0 293.8 %all-reduce.18.cloned.1.call-start = ((), (), s32[]{:S(2)}) async-start(), calls=%async_computation.2 | async-start | bytes 6291456 | tf_op jit(solution)/shard_map/psum | solution.py:61
  494.1 3.9 copy-start.6
  618.7 3.7 copy-start.7
  634.5 74.6 %all-to-all-start.1 = ((f32[1,6144,128]{1,0,2:T(1,128)}), f32[1,6144,128]{1,0,2:T(1,128)}, u32[]{:S(2)}, u32[]{:S(2)}) async-start(f32[1,6144,128]{1,0,2:T(1,128)} %copy.22), calls=%async_computation.1 | async-start | bytes 6291456 | tf_op jit(solution)/shard_map/all_to_all | solution.py:66
  773.3 1.6 copy-start.2
Sparse Core Ops, SparseCore 0:
  505.1 67.4 all-reduce.17
where the time goes:
time: 800 us; the launch traced here: 790 us
  other arithmetic  297 us (37%)
  local copies, waits for them, and re-layouts  197 us (25%)
  waiting for transfers between devices  129 us (16%)
  matrix products  110 us (14%)
  loops' own time  28.9 us (4%)
  between operations  15.4 us (2%)
  starting transfers between devices  12.1 us (2%)
    unnamed x1, other arithmetic  219 us
    dot_general x12, matrix products, one_block(): return jnp.dot(onehot, masked, precision=lax.Precision.HIGHEST)  98.6 us
    unnamed x27, local copies, waits for them, and re-layouts  94 us
    all_to_all x1, waiting for transfers between devices, body(): lax.all_to_all(back_filtered, 'lev', split_axis=2, concat_axis=1, tiled=T...  69.9 us
    all_to_all x1, waiting for transfers between devices, body(): lax.all_to_all(outgoing, 'lev', split_axis=1, concat_axis=2, tiled=True)  59.5 us
    all_to_all x2, local copies, waits for them, and re-layouts, body(): lax.all_to_all(outgoing, 'lev', split_axis=1, concat_axis=2, tiled=True)  18.6 us
    dynamic_update_slice x8, local copies, waits for them, and re-layouts, place(): return lax.dynamic_update_slice_in_dim(grid, current + kept, first, 2)  17.7 us
  transfers between devices with their start and end apart: 3, of which 2 were waited for; matrix products, arithmetic and copies ran while one was open for 16% of the time, Pallas kernels for 0%

commit v1 on v0

v1 whole, which is shorter than its diff:
```python
import functools

import jax
import jax.numpy as jnp
from jax import lax
from jax.experimental import pallas as pl
from jax.experimental.pallas import tpu as pltpu
from jax.sharding import PartitionSpec as P

STEPS = 4
PARTS = 3
LANES = 128
GROUP = 8
F32 = jnp.float32
BF16 = jnp.bfloat16


def flip_pairs(size, bit):
    return [(i, i ^ bit) for i in range(size)]


def transpose_in(src, dst, size_x):
    def step(b, _):
        first = pl.multiple_of(b * 8, 8)
        dst[pl.ds(first, 8)] = jnp.swapaxes(src[:, pl.ds(first, 8), :], 0, 1)
        return 0

    lax.fori_loop(0, size_x // 8, step, 0, unroll=2)


def faces(diff, kx, ky, size_x, size_y):
    lane = lax.broadcasted_iota(jnp.int32, (GROUP, size_y), 1)

    def step(x, here):
        following = diff[jnp.minimum(x + 1, size_x - 1)]
        kx[x] = jnp.where(x < size_x - 1, 0.5 * (here + following), 0.0)
        ahead = pltpu.roll(here, size_y - 1, 1)
        ky[x] = jnp.where(lane < size_y - 1, 0.5 * (here + ahead), 0.0)
        return following

    lax.fori_loop(0, size_x, step, diff[0], unroll=4)


def sweep(read, write, kx, ky, size_x, size_y):
    def step(x, carry):
        here, flux_before = carry
        following = read(jnp.minimum(x + 1, size_x - 1))
        flux_x = kx[x] * (following - here)
        flux_y = ky[x] * (pltpu.roll(here, size_y - 1, 1) - here)
        write(x, here + (flux_x - flux_before) + (flux_y - pltpu.roll(flux_y, 1, 1)))
        return following, flux_x

    first = read(0)
    lax.fori_loop(0, size_x, step, (first, jnp.zeros_like(first)), unroll=8)


def forward_kernel(size_x, size_y, groups, capacity, starts, info, control, diffusivity, diff_out, *rest):
    outs = rest[: groups * PARTS]
    grid, flat, kx, ky = rest[groups * PARTS :]
    columns = size_x * size_y
    part = capacity // PARTS
    transpose_in(diffusivity, diff_out, size_x)
    faces(diff_out, kx, ky, size_x, size_y)
    transpose_in(control.at[0], grid, size_x)

    def read(x):
        return grid[x]

    def write(x, value):
        grid[x] = value

    def write_flat(x, value):
        flat[:, pl.ds(pl.multiple_of(x * size_y, size_y), size_y)] = value

    for repeat in range(STEPS - 1):
        sweep(read, write, kx, ky, size_x, size_y)
    sweep(read, write_flat, kx, ky, size_x, size_y)
    flat[:, columns:] = jnp.zeros((GROUP, flat.shape[1] - columns), F32)

    lane = lax.broadcasted_iota(jnp.int32, (GROUP, LANES), 1)
    me = info[0]
    tiles = part // LANES
    for d in range(groups):
        start = starts[jnp.bitwise_xor(me, d)]
        base = start // LANES
        shift = start - base * LANES
        back = lax.rem(LANES - shift, LANES)
        low = lane < LANES - shift
        for c in range(PARTS):
            out = outs[c * groups + d]
            begin = base + c * tiles

            def load(t):
                at = pl.multiple_of((begin + t) * LANES, LANES)
                return pltpu.roll(flat[:, pl.ds(at, LANES)], back, 1)

            now = load(0)
            for t in range(tiles):
                later = load(t + 1)
                out[:, t * LANES : (t + 1) * LANES] = jnp.where(low, now, later)
                now = later


def split3(value):
    high = value.astype(BF16)
    return high, (value - high.astype(F32)).astype(BF16)


def dot3(a, b, dims):
    ah, al = split3(a)
    bh, bl = split3(b)
    dot = functools.partial(lax.dot_general, dimension_numbers=(dims, ((), ())), preferred_element_type=F32)
    return dot(ah, bh) + (dot(ah, bl) + dot(al, bh))


def observation_kernel(rows_here, obs_cap, info, slots, rinv, out, split):
    step = pl.program_id(0)

    @pl.when(step == 0)
    def _():
        values = rinv[0]
        high = values.astype(BF16)
        split[:, :LANES] = high
        split[:, LANES:] = (values - high.astype(F32)).astype(BF16)

    first = info[2] + step * rows_here
    block = 512
    row = first + lax.broadcasted_iota(jnp.int32, (rows_here, block), 0)

    def add(b, total):
        at = pl.multiple_of(b * block, block)
        hit = row == slots[:, pl.ds(at, block)]
        onehot = jnp.where(hit, 1.0, 0.0).astype(BF16)
        return total + jnp.dot(onehot, split[pl.ds(at, block), :], preferred_element_type=F32)

    total = lax.fori_loop(0, obs_cap // block, add, jnp.zeros((rows_here, 2 * LANES), F32))
    out[...] = total[:, :LANES] + total[:, LANES:]


def filter_kernel(groups, info, vfilter, perturb, *rest):
    pieces = rest[:groups]
    keep, send = rest[groups:]
    half = keep.shape[0]
    width = 256
    mine = info[1]
    for which, out in ((mine, keep), (1 - mine, send)):

        def step(b, _):
            at = pl.multiple_of(which * half + b * width, width)
            slab = jnp.concatenate([piece[:, pl.ds(at, width)] for piece in pieces], axis=0)
            filtered = dot3(slab.T, vfilter[...], ((1,), (1,)))
            out[pl.ds(pl.multiple_of(b * width, width), width), :] = (
                perturb[0, pl.ds(at, width), :] * filtered
            )
            return 0

        lax.fori_loop(0, half // width, step, 0, unroll=2)


def back_kernel(groups, info, vfilter, perturb, adj_mine, adj_other, *pieces):
    half = adj_mine.shape[0]
    width = 256
    levels = pieces[0].shape[0]
    mine = info[1]
    for which, adj in ((mine, adj_mine), (1 - mine, adj_other)):

        def step(b, _):
            at = pl.multiple_of(which * half + b * width, width)
            weighted = perturb[0, pl.ds(at, width), :] * adj[pl.ds(pl.multiple_of(b * width, width), width), :]
            result = dot3(vfilter[...], weighted, ((0,), (1,)))
            for d in range(groups):
                pieces[d][:, pl.ds(at, width)] = result[d * levels : (d + 1) * levels]
            return 0

        lax.fori_loop(0, half // width, step, 0, unroll=2)


def backward_kernel(size_x, size_y, groups, capacity, starts, info, diff, *rest):
    ins = rest[: groups * PARTS]
    out, staging, flat, grid, kx, ky, sem = rest[groups * PARTS :]
    part = capacity // PARTS
    me = info[0]
    step_id = pl.program_id(0)
    level = pl.multiple_of(step_id * GROUP, GROUP)
    copies = []
    for c in range(PARTS):
        for d in range(groups):
            copies.append(
                pltpu.make_async_copy(
                    ins[c * groups + d].at[pl.ds(level, GROUP), :],
                    staging.at[jnp.bitwise_xor(me, d), :, pl.ds(c * part, part)],
                    sem.at[c * groups + d],
                )
            )
    for copy in copies:
        copy.start()
    faces(diff, kx, ky, size_x, size_y)
    for copy in copies:
        copy.wait()

    lane = lax.broadcasted_iota(jnp.int32, (GROUP, LANES), 1)
    tiles = capacity // LANES
    some = 8

    def place(j, _):
        start = starts[j]
        base = start // LANES
        shift = start - base * LANES
        high = lane >= shift

        def several(b, before):
            for t in range(some):
                at = pl.multiple_of((b * some + t) * LANES, LANES)
                to = pl.multiple_of((base + b * some + t) * LANES, LANES)
                here = pltpu.roll(staging[j, :, pl.ds(at, LANES)], shift, 1)
                flat[:, pl.ds(to, LANES)] = jnp.where(high, here, before)
                before = here
            return before

        existing = flat[:, pl.ds(pl.multiple_of(base * LANES, LANES), LANES)]
        last = lax.fori_loop(0, tiles // some, several, existing)
        flat[:, pl.ds(pl.multiple_of((base + tiles) * LANES, LANES), LANES)] = last
        return 0

    lax.fori_loop(0, groups, place, 0)

    def read_flat(x):
        return flat[:, pl.ds(pl.multiple_of(x * size_y, size_y), size_y)]

    def read(x):
        return grid[x]

    def write(x, value):
        grid[x] = value

    sweep(read_flat, write, kx, ky, size_x, size_y)
    for repeat in range(STEPS - 1):
        sweep(read, write, kx, ky, size_x, size_y)

    def back(b, _):
        first = pl.multiple_of(b * 8, 8)
        out[0, :, pl.ds(first, 8), :] = jnp.swapaxes(grid[pl.ds(first, 8)], 0, 1)
        return 0

    lax.fori_loop(0, size_x // 8, back, 0, unroll=2)


def body(control, diffusivity, perturb, vertical_filter, sub_widths, obs_raw, obs_counts, obs_rinv):
    members, levels_here, size_x, size_y = control.shape
    columns = size_x * size_y
    capacity = perturb.shape[1]
    levels = perturb.shape[2]
    groups = sub_widths.shape[0]
    obs_cap = obs_raw.shape[1]
    part = capacity // PARTS
    half = part // 2
    n_mem = lax.axis_size("mem")
    me = lax.axis_index("lev")
    mem = lax.axis_index("mem")
    core = mem % 2
    starts = (jnp.cumsum(sub_widths) - sub_widths).astype(jnp.int32)
    info = jnp.stack([me, core]).astype(jnp.int32)
    smem = pl.BlockSpec(memory_space=pltpu.SMEM)
    params = pltpu.CompilerParams(vmem_limit_bytes=56 << 20)
    flat_width = columns + capacity + LANES
    piece_shape = jax.ShapeDtypeStruct((levels_here, part), F32)
    steps = levels_here // GROUP

    results = pl.pallas_call(
        functools.partial(forward_kernel, size_x, size_y, groups, capacity),
        grid=(steps,),
        in_specs=[
            smem,
            smem,
            pl.BlockSpec((1, GROUP, size_x, size_y), lambda g: (0, g, 0, 0)),
            pl.BlockSpec((GROUP, size_x, size_y), lambda g: (g, 0, 0)),
        ],
        out_specs=[pl.BlockSpec((size_x, GROUP, size_y), lambda g: (0, g, 0))]
        + [pl.BlockSpec((GROUP, part), lambda g: (g, 0))] * (groups * PARTS),
        out_shape=[jax.ShapeDtypeStruct((size_x, levels_here, size_y), F32)] + [piece_shape] * (groups * PARTS),
        scratch_shapes=[
            pltpu.VMEM((size_x, GROUP, size_y), F32),
            pltpu.VMEM((GROUP, flat_width), F32),
            pltpu.VMEM((size_x, GROUP, size_y), F32),
            pltpu.VMEM((size_x, GROUP, size_y), F32),
        ],
        compiler_params=params,
        name="smooth_and_cut",
    )(starts, info, control, diffusivity)
    diff = results[0]
    outgoing = results[1:]

    width = sub_widths[me]
    live = jnp.arange(obs_cap, dtype=jnp.int32) < obs_counts[me]
    slots = jnp.where(live, obs_raw[0] % width, -1)[None, :]
    order = jnp.bitwise_xor(me, jnp.arange(groups))
    vfilter = vertical_filter.reshape(levels, groups, levels_here)[:, order, :].reshape(levels, levels)

    rows_here = 256
    adjoint_pieces = []
    for c in range(PARTS):
        row0 = c * part + core * half
        w_info = jnp.stack([me, core, row0]).astype(jnp.int32)
        obs_weight = pl.pallas_call(
            functools.partial(observation_kernel, rows_here, obs_cap),
            grid=(half // rows_here,),
            in_specs=[
                smem,
                pl.BlockSpec((1, obs_cap), lambda g: (0, 0)),
                pl.BlockSpec((1, obs_cap, levels), lambda g: (0, 0, 0)),
            ],
            out_specs=pl.BlockSpec((rows_here, levels), lambda g: (g, 0)),
            out_shape=jax.ShapeDtypeStruct((half, levels), F32),
            scratch_shapes=[pltpu.VMEM((obs_cap, 2 * levels), BF16)],
            compiler_params=params,
            cost_estimate=pl.CostEstimate(
                flops=4 * half * obs_cap * levels, bytes_accessed=4 * obs_cap * levels, transcendentals=0
            ),
            name="observation_weights",
        )(w_info, slots, obs_rinv)

        pieces = [outgoing[c * groups]]
        for d in range(1, groups):
            pieces.append(lax.ppermute(outgoing[c * groups + d], "lev", flip_pairs(groups, d)))
        whole = pl.BlockSpec((levels_here, part), lambda g: (0, 0))
        chunk = pl.BlockSpec((1, part, levels), lambda g, c=c: (0, c, 0))
        square = pl.BlockSpec((levels, levels), lambda g: (0, 0))
        half_block = pl.BlockSpec((half, levels), lambda g: (0, 0))
        half_shape = jax.ShapeDtypeStruct((half, levels), F32)
        cost = pl.CostEstimate(
            flops=6 * part * levels * levels, bytes_accessed=12 * part * levels, transcendentals=0
        )
        keep, send = pl.pallas_call(
            functools.partial(filter_kernel, groups),
            grid=(1,),
            in_specs=[smem, square, chunk] + [whole] * groups,
            out_specs=[half_block, half_block],
            out_shape=[half_shape, half_shape],
            compiler_params=params,
            cost_estimate=cost,
            name="filter_forward",
        )(info, vfilter, perturb, *pieces)
        total = keep + lax.ppermute(send, "mem", flip_pairs(n_mem, 1))
        bit = 2
        while bit < n_mem:
            total = total + lax.ppermute(total, "mem", flip_pairs(n_mem, bit))
            bit *= 2
        adj_mine = total * obs_weight
        adj_other = lax.ppermute(adj_mine, "mem", flip_pairs(n_mem, 1))
        back = pl.pallas_call(
            functools.partial(back_kernel, groups),
            grid=(1,),
            in_specs=[smem, square, chunk, half_block, half_block],
            out_specs=[whole] * groups,
            out_shape=[piece_shape] * groups,
            compiler_params=params,
            cost_estimate=cost,
            name="filter_backward",
        )(info, vfilter, perturb, adj_mine, adj_other)
        adjoint_pieces.append(back[0])
        for d in range(1, groups):
            adjoint_pieces.append(lax.ppermute(back[d], "lev", flip_pairs(groups, d)))

    return pl.pallas_call(
        functools.partial(backward_kernel, size_x, size_y, groups, capacity),
        grid=(steps,),
        in_specs=[
            smem,
            smem,
            pl.BlockSpec((size_x, GROUP, size_y), lambda g: (0, g, 0)),
        ]
        + [pl.BlockSpec(memory_space=pl.ANY)] * (groups * PARTS),
        out_specs=pl.BlockSpec((1, GROUP, size_x, size_y), lambda g: (0, g, 0, 0)),
        out_shape=jax.ShapeDtypeStruct((members, levels_here, size_x, size_y), F32),
        scratch_shapes=[
            pltpu.VMEM((groups, GROUP, capacity), F32),
            pltpu.VMEM((GROUP, flat_width), F32),
            pltpu.VMEM((size_x, GROUP, size_y), F32),
            pltpu.VMEM((size_x, GROUP, size_y), F32),
            pltpu.VMEM((size_x, GROUP, size_y), F32),
            pltpu.SemaphoreType.DMA((groups * PARTS,)),
        ],
        compiler_params=params,
        name="place_and_smooth",
    )(starts, info, diff, *adjoint_pieces)


def solution(mesh):
    return jax.shard_map(
        body,
        mesh=mesh,
        in_specs=(
            P("mem", "lev", None, None),
            P("lev", None, None),
            P("mem", "lev", None),
            P(),
            P(),
            P("lev", None),
            P(),
            P("lev", None, None),
        ),
        out_specs=P("mem", "lev", None, None),
        check_vma=False,
    )
```

time: 800 us -> 374 us (0.47)
  other arithmetic: 297 us -> 8.16 us
  Pallas kernels: 0 us -> 214 us
  local copies, waits for them, and re-layouts: 197 us -> 5.14 us
  matrix products: 110 us -> 0 us
  starting transfers between devices: 12.1 us -> 88.8 us
  waiting for transfers between devices: 129 us -> 53.2 us
  loops' own time: 28.9 us -> 0 us
  between operations: 15.4 us -> 2.17 us
    unnamed x1 -> x0, other arithmetic: 219 us -> none
    pallas_call x0 -> x11, Pallas kernels: none -> 214 us  [the longest x1 76 us: body(): pl.pallas_call(functools.partial(backward_kernel, size_x, size_y, groups,...]
    all_to_all x2 -> x0, waiting for transfers between devices: 129 us -> none  [the longest x1 69.9 us: body(): lax.all_to_all(back_filtered, 'lev', split_axis=2, concat_axis=1, tiled=T...]
    dot_general x14 -> x0, matrix products: 110 us -> none  [the longest x12 98.6 us: one_block(): return jnp.dot(onehot, masked, precision=lax.Precision.HIGHEST)]
    unnamed x27 -> x139, local copies, waits for them, and re-layouts: 94 us -> 2.52 us
    ppermute x0 -> x51, starting transfers between devices: none -> 88.8 us  [the longest x21 46.4 us: body(): lax.ppermute(outgoing[c * groups + d], 'lev', flip_pairs(groups, d))]
    ppermute x0 -> x51, waiting for transfers between devices: none -> 53.2 us  [the longest x21 28.9 us: body(): adjoint_pieces.append(lax.ppermute(back[d], 'lev', flip_pairs(groups, d)))]
    dynamic_update_slice x16 -> x0, local copies, waits for them, and re-layouts: 33.3 us -> none  [the longest x8 17.7 us: place(): return lax.dynamic_update_slice_in_dim(grid, current + kept, first, 2)]
  transfers between devices with their start and end apart: 3 -> 51, of which waited for: 2 -> 9; matrix products, arithmetic and copies ran while one was open for 16% -> 2% of each run, Pallas kernels for 0% -> 18%
where the time goes in v1:
time: 374 us; the launch traced here: 372 us
  Pallas kernels  214 us (57%)
  starting transfers between devices  88.8 us (24%)
  waiting for transfers between devices  53.2 us (14%)
  other arithmetic  8.16 us (2%)
  local copies, waits for them, and re-layouts  5.14 us (1%)
    pallas_call x1, Pallas kernels, body(): pl.pallas_call(functools.partial(backward_kernel, size_x, size_y, groups,...  76 us
    pallas_call x1, Pallas kernels, body(): pl.pallas_call(functools.partial(forward_kernel, size_x, size_y, groups,...  70.6 us
    ppermute x21, starting transfers between devices, body(): lax.ppermute(outgoing[c * groups + d], 'lev', flip_pairs(groups, d))  46.4 us
    pallas_call x3, Pallas kernels, body(): pl.pallas_call(functools.partial(observation_kernel, rows_here, obs_cap),...  45.2 us
    ppermute x21, starting transfers between devices, body(): adjoint_pieces.append(lax.ppermute(back[d], 'lev', flip_pairs(groups, d)))  38 us
    ppermute x21, waiting for transfers between devices, body(): adjoint_pieces.append(lax.ppermute(back[d], 'lev', flip_pairs(groups, d)))  28.9 us
    ppermute x21, waiting for transfers between devices, body(): lax.ppermute(outgoing[c * groups + d], 'lev', flip_pairs(groups, d))  12.8 us
    ppermute x3, waiting for transfers between devices, body(): total = total + lax.ppermute(total, 'mem', flip_pairs(n_mem, bit))  11.5 us
  transfers between devices with their start and end apart: 51, of which 9 were waited for; matrix products, arithmetic and copies ran while one was open for 2% of the time, Pallas kernels for 18%

profile of v1, /device:TPU:0, one launch (start us, length us, event | category | flops | bytes accessed | tf_op | source)
XLA Modules:
  0.0 371.6 jit_solution(12492832351623456579)
XLA Ops:
  2.7 70.6 %smooth_and_cut.1 = (f32[128,16,256]{2,1,0:T(8,128)}, f32[16,2048]{1,0:T(8,128)}, f32[16,2048]{1,0:T(8,128)}, f32[16,2048]{1,0:T(8,128)}, f32[16,2048]{1,0:T(8,1...) custom-call(s32[8]{0:T(128)} %bitcast_subtract_fusion.starts, ...), custom_call_target="tpu_custom_call" | custom-call | tf_op jit(solution)/shard_map/smooth_and_cut/pallas_call | solution.py:269
  88.1 3.6 collective-permute-start.39
  94.8 5.7 %collective-permute-done.38.rest_5_ = f32[16,2048]{1,0:T(8,128)S(1)} collective-permute-done((f32[16,2048]{1,0:T(8,128)}, f32[16,2048]{1,0:T(8,128)S(1)}, u32[]{:S(2)}, u32[]{:S(2)}) %collective-permute-start.38) | collective-permute-done | bytes 131104 | tf_op jit(solution)/shard_map/ppermute | solution.py:324
  101.1 5.3 %collective-permute-start.20 = (f32[16,2048]{1,0:T(8,128)}, f32[16,2048]{1,0:T(8,128)S(1)}, u32[]{:S(2)}, u32[]{:S(2)}) collective-permute-start(f32[16,2048]{1,0:T(8,128)} %get-tuple-element.83), channel_id=1, source_target_pairs={{0,4},{1,5},{2,6},{3,7},{4,0},{5,1},{6,2},{7,3},{8,12},{9,13},{10,... | collective-permute-start | bytes 393224 | tf_op jit(solution)/shard_map/ppermute | solution.py:324
  106.4 8.1 %collective-permute-start.21 = (f32[16,2048]{1,0:T(8,128)}, f32[16,2048]{1,0:T(8,128)S(1)}, u32[]{:S(2)}, u32[]{:S(2)}) collective-permute-start(f32[16,2048]{1,0:T(8,128)} %get-tuple-element.84), channel_id=1, source_target_pairs={{0,5},{1,4},{2,7},{3,6},{4,1},{5,0},{6,3},{7,2},{8,13},{9,12},{10,... | collective-permute-start | bytes 393224 | tf_op jit(solution)/shard_map/ppermute | solution.py:324
  115.3 3.8 %filter_forward.5 = (f32[1024,128]{1,0:T(8,128)}, f32[1024,128]{1,0:T(8,128)}) custom-call(s32[2]{0:T(128)} %pad_add_fusion.info, f32[128,128]{1,0:T(8,128)} %copy.11.vfilter, f32[1,6144,128]{2,1,0:T(8,128)} %perturb.11, f32[16,2048]{1,0:T(8,128)} %get-tuple-element.97.rest_0_, f32[16,2048]{1,0:T(8,128)} %copy-done.33, f32[16,2048]{1,0:T(8,128)} %copy-done.34, ...), custom_call_target="tpu_custom_call" | custom-call | flops 201326592 | bytes 3145728 | tf_op jit(solution)/shard_map/filter_forward/pallas_call | solution.py:333
  119.1 5.2 %collective-permute-start = (f32[16,2048]{1,0:T(8,128)S(1)}, f32[16,2048]{1,0:T(8,128)S(1)}, u32[]{:S(2)}, u32[]{:S(2)}) collective-permute-start(f32[16,2048]{1,0:T(8,128)S(1)} %copy-done.62), channel_id=1, source_target_pairs={{0,1},{1,0},{2,3},{3,2},{4,5},{5,4},{6,7},{7,6},{8,9},{9,8},{10,11... | collective-permute-start | bytes 393224 | tf_op jit(solution)/shard_map/ppermute | solution.py:324
  129.1 15.1 %observation_weights.5 = f32[1024,128]{1,0:T(8,128)} custom-call(s32[3]{0:T(128)} %pad_add_fusion.4.info, s32[1,6144]{1,0:T(1,128)} %compare_select_fusion.slots, f32[1,6144,128]{2,1,0:T(8,128)} %rinv.5), custom_call_target="tpu_custom_call" | custom-call | flops 3221225472 | bytes 3145728 | tf_op jit(solution)/shard_map/observation_weights/pallas_call | solution.py:304
  144.2 3.8 %filter_forward.4 = (f32[1024,128]{1,0:T(8,128)}, f32[1024,128]{1,0:T(8,128)}) custom-call(s32[2]{0:T(128)} %pad_add_fusion.info, f32[128,128]{1,0:T(8,128)} %copy.11.vfilter, f32[1,6144,128]{2,1,0:T(8,128)} %perturb.11, f32[16,2048]{1,0:T(8,128)} %get-tuple-element.79.rest_0_, f32[16,2048]{1,0:T(8,128)} %copy-done.35, f32[16,2048]{1,0:T(8,128)} %copy-done.39, ...), custom_call_target="tpu_custom_call" | custom-call | flops 201326592 | bytes 3145728 | tf_op jit(solution)/shard_map/filter_forward/pallas_call | solution.py:333
  157.6 7.0 %collective-permute-done.4.rest_5_ = f32[16,2048]{1,0:T(8,128)S(1)} collective-permute-done((f32[16,2048]{1,0:T(8,128)S(1)}, f32[16,2048]{1,0:T(8,128)S(1)}, u32[]{:S(2)}, u32[]{:S(2)}) %collective-permute-start.4) | collective-permute-done | bytes 131104 | tf_op jit(solution)/shard_map/ppermute | solution.py:324
  165.4 3.8 %filter_forward.3 = (f32[1024,128]{1,0:T(8,128)}, f32[1024,128]{1,0:T(8,128)}) custom-call(s32[2]{0:T(128)} %pad_add_fusion.info, f32[128,128]{1,0:T(8,128)} %copy.11.vfilter, f32[1,6144,128]{2,1,0:T(8,128)} %perturb.11, f32[16,2048]{1,0:T(8,128)} %get-tuple-element.61.rest_0_, f32[16,2048]{1,0:T(8,128)} %copy-done.40, f32[16,2048]{1,0:T(8,128)} %copy-done.42, ...), custom_call_target="tpu_custom_call" | custom-call | flops 201326592 | bytes 3145728 | tf_op jit(solution)/shard_map/filter_forward/pallas_call | solution.py:333
  170.7 15.1 %observation_weights.4 = f32[1024,128]{1,0:T(8,128)} custom-call(s32[3]{0:T(128)} %pad_add_fusion.3.info, s32[1,6144]{1,0:T(1,128)} %compare_select_fusion.slots, f32[1,6144,128]{2,1,0:T(8,128)} %rinv.5), custom_call_target="tpu_custom_call" | custom-call | flops 3221225472 | bytes 3145728 | tf_op jit(solution)/shard_map/observation_weights/pallas_call | solution.py:304
  186.5 15.0 %observation_weights.3 = f32[1024,128]{1,0:T(8,128)} custom-call(s32[3]{0:T(128)} %pad_add_fusion.1.info, s32[1,6144]{1,0:T(1,128)} %compare_select_fusion.slots, f32[1,6144,128]{2,1,0:T(8,128)} %rinv.5), custom_call_target="tpu_custom_call" | custom-call | flops 3221225472 | bytes 3145728 | tf_op jit(solution)/shard_map/observation_weights/pallas_call | solution.py:304
  204.0 11.5 %collective-permute-done.8 = f32[1024,128]{1,0:T(8,128)S(1)} collective-permute-done((f32[1024,128]{1,0:T(8,128)S(1)}, f32[1024,128]{1,0:T(8,128)S(1)}, u32[]{:S(2)}, u32[]{:S(2)}) %collective-permute-start.8) | collective-permute-done | bytes 524320 | tf_op jit(solution)/shard_map/ppermute | solution.py:346
  216.6 3.7 filter_backward.5
  221.4 5.8 %collective-permute-start.45 = (f32[16,2048]{1,0:T(8,128)}, f32[16,2048]{1,0:T(8,128)S(1)}, u32[]{:S(2)}, u32[]{:S(2)}) collective-permute-start(f32[16,2048]{1,0:T(8,128)} %get-tuple-element.109), channel_id=1, source_target_pairs={{0,2},{1,3},{2,0},{3,1},{4,6},{5,7},{6,4},{7,5},{8,10},{9,11},{10,... | collective-permute-start | bytes 393224 | tf_op jit(solution)/shard_map/ppermute | solution.py:362
  232.6 3.7 filter_backward.4
  240.2 5.9 %collective-permute-done.47.rest_20_ = f32[16,2048]{1,0:T(8,128)S(1)} collective-permute-done((f32[16,2048]{1,0:T(8,128)}, f32[16,2048]{1,0:T(8,128)S(1)}, u32[]{:S(2)}, u32[]{:S(2)}) %collective-permute-start.47) | collective-permute-done | bytes 131104 | tf_op jit(solution)/shard_map/ppermute | solution.py:362
  246.1 3.7 collective-permute-done.48.rest_21_
  253.0 3.7 filter_backward.3
  263.3 5.7 %collective-permute-done.30.rest_12_ = f32[16,2048]{1,0:T(8,128)S(1)} collective-permute-done((f32[16,2048]{1,0:T(8,128)}, f32[16,2048]{1,0:T(8,128)S(1)}, u32[]{:S(2)}, u32[]{:S(2)}) %collective-permute-start.30) | collective-permute-done | bytes 131104 | tf_op jit(solution)/shard_map/ppermute | solution.py:362
  274.8 5.6 %collective-permute-start.14 = (f32[16,2048]{1,0:T(8,128)}, f32[16,2048]{1,0:T(8,128)S(1)}, u32[]{:S(2)}, u32[]{:S(2)}) collective-permute-start(f32[16,2048]{1,0:T(8,128)} %get-tuple-element.76), channel_id=1, source_target_pairs={{0,5},{1,4},{2,7},{3,6},{4,1},{5,0},{6,3},{7,2},{8,13},{9,12},{10,... | collective-permute-start | bytes 393224 | tf_op jit(solution)/shard_map/ppermute | solution.py:362
  284.5 6.9 %collective-permute-done.13.rest_4_ = f32[16,2048]{1,0:T(8,128)S(1)} collective-permute-done((f32[16,2048]{1,0:T(8,128)}, f32[16,2048]{1,0:T(8,128)S(1)}, u32[]{:S(2)}, u32[]{:S(2)}) %collective-permute-start.13) | collective-permute-done | bytes 131104 | tf_op jit(solution)/shard_map/ppermute | solution.py:362
  295.5 76.0 %place_and_smooth.1 = f32[1,16,128,256]{3,2,1,0:T(8,128)} custom-call(s32[8]{0:T(128)} %bitcast_subtract_fusion.starts, s32[2]{0:T(128)} %pad_add_fusion.info, f32[128,16,256]{2,1,0:T(8,128)} %get-tuple-element.60.diff, f32[16,2048]{1,0:T(8,128)} %get-tuple-element.71.rest_0_, f32[16,2048]{1,0:T(8,128)} %copy-done.26, f32[16,2048]{1,0:T(8,128)} %copy-done.27, ...), custom_call_target="tpu_custom_call" | custom-call | tf_op jit(solution)/shard_map/place_and_smooth/pallas_call | solution.py:364
  (247 shorter events, 75.2 us)
Async XLA Ops:
  80.8 19.7 %collective-permute-start.38 = (f32[16,2048]{1,0:T(8,128)}, f32[16,2048]{1,0:T(8,128)S(1)}, u32[]{:S(2)}, u32[]{:S(2)}) collective-permute-start(f32[16,2048]{1,0:T(8,128)} %get-tuple-element.102), channel_id=1, source_target_pairs={{0,5},{1,4},{2,7},{3,6},{4,1},{5,0},{6,3},{7,2},{8,13},{9,12},{10,... | collective-permute-start | bytes 393224 | tf_op jit(solution)/shard_map/ppermute | solution.py:324
  91.7 22.8 %collective-permute-start.17 = (f32[16,2048]{1,0:T(8,128)}, f32[16,2048]{1,0:T(8,128)S(1)}, u32[]{:S(2)}, u32[]{:S(2)}) collective-permute-start(f32[16,2048]{1,0:T(8,128)} %get-tuple-element.80), channel_id=1, source_target_pairs={{0,1},{1,0},{2,3},{3,2},{4,5},{5,4},{6,7},{7,6},{8,9},{9,8},{10,11... | collective-permute-start | bytes 393224 | tf_op jit(solution)/shard_map/ppermute | solution.py:324
  93.4 21.1 %collective-permute-start.18 = (f32[16,2048]{1,0:T(8,128)}, f32[16,2048]{1,0:T(8,128)S(1)}, u32[]{:S(2)}, u32[]{:S(2)}) collective-permute-start(f32[16,2048]{1,0:T(8,128)} %get-tuple-element.81), channel_id=1, source_target_pairs={{0,2},{1,3},{2,0},{3,1},{4,6},{5,7},{6,4},{7,5},{8,10},{9,11},{10,... | collective-permute-start | bytes 393224 | tf_op jit(solution)/shard_map/ppermute | solution.py:324
  100.5 18.6 %collective-permute-start.19 = (f32[16,2048]{1,0:T(8,128)}, f32[16,2048]{1,0:T(8,128)S(1)}, u32[]{:S(2)}, u32[]{:S(2)}) collective-permute-start(f32[16,2048]{1,0:T(8,128)} %get-tuple-element.82), channel_id=1, source_target_pairs={{0,3},{1,2},{2,1},{3,0},{4,7},{5,6},{6,5},{7,4},{8,11},{9,10},{10,... | collective-permute-start | bytes 393224 | tf_op jit(solution)/shard_map/ppermute | solution.py:324
  101.1 23.3 %collective-permute-start.20 = (f32[16,2048]{1,0:T(8,128)}, f32[16,2048]{1,0:T(8,128)S(1)}, u32[]{:S(2)}, u32[]{:S(2)}) collective-permute-start(f32[16,2048]{1,0:T(8,128)} %get-tuple-element.83), channel_id=1, source_target_pairs={{0,4},{1,5},{2,6},{3,7},{4,0},{5,1},{6,2},{7,3},{8,12},{9,13},{10,... | collective-permute-start | bytes 393224 | tf_op jit(solution)/shard_map/ppermute | solution.py:324
  106.4 18.0 %collective-permute-start.21 = (f32[16,2048]{1,0:T(8,128)}, f32[16,2048]{1,0:T(8,128)S(1)}, u32[]{:S(2)}, u32[]{:S(2)}) collective-permute-start(f32[16,2048]{1,0:T(8,128)} %get-tuple-element.84), channel_id=1, source_target_pairs={{0,5},{1,4},{2,7},{3,6},{4,1},{5,0},{6,3},{7,2},{8,13},{9,12},{10,... | collective-permute-start | bytes 393224 | tf_op jit(solution)/shard_map/ppermute | solution.py:324
  119.1 28.9 %collective-permute-start = (f32[16,2048]{1,0:T(8,128)S(1)}, f32[16,2048]{1,0:T(8,128)S(1)}, u32[]{:S(2)}, u32[]{:S(2)}) collective-permute-start(f32[16,2048]{1,0:T(8,128)S(1)} %copy-done.62), channel_id=1, source_target_pairs={{0,1},{1,0},{2,3},{3,2},{4,5},{5,4},{6,7},{7,6},{8,9},{9,8},{10,11... | collective-permute-start | bytes 393224 | tf_op jit(solution)/shard_map/ppermute | solution.py:324
  124.3 27.0 %collective-permute-start.1 = (f32[16,2048]{1,0:T(8,128)S(1)}, f32[16,2048]{1,0:T(8,128)S(1)}, u32[]{:S(2)}, u32[]{:S(2)}) collective-permute-start(f32[16,2048]{1,0:T(8,128)S(1)} %copy-done.61), channel_id=1, source_target_pairs={{0,2},{1,3},{2,0},{3,1},{4,6},{5,7},{6,4},{7,5},{8,10},{9,11},{10,... | collective-permute-start | bytes 393224 | tf_op jit(solution)/shard_map/ppermute | solution.py:324
  124.5 28.4 %collective-permute-start.2 = (f32[16,2048]{1,0:T(8,128)S(1)}, f32[16,2048]{1,0:T(8,128)S(1)}, u32[]{:S(2)}, u32[]{:S(2)}) collective-permute-start(f32[16,2048]{1,0:T(8,128)S(1)} %copy-done.60), channel_id=1, source_target_pairs={{0,3},{1,2},{2,1},{3,0},{4,7},{5,6},{6,5},{7,4},{8,11},{9,10},{10,... | collective-permute-start | bytes 393224 | tf_op jit(solution)/shard_map/ppermute | solution.py:324
  126.0 30.3 %collective-permute-start.3 = (f32[16,2048]{1,0:T(8,128)S(1)}, f32[16,2048]{1,0:T(8,128)S(1)}, u32[]{:S(2)}, u32[]{:S(2)}) collective-permute-start(f32[16,2048]{1,0:T(8,128)S(1)} %copy-done.59), channel_id=1, source_target_pairs={{0,4},{1,5},{2,6},{3,7},{4,0},{5,1},{6,2},{7,3},{8,12},{9,13},{10,... | collective-permute-start | bytes 393224 | tf_op jit(solution)/shard_map/ppermute | solution.py:324
  129.1 40.1 %collective-permute-start.41 = (f32[1024,128]{1,0:T(8,128)}, f32[1024,128]{1,0:T(8,128)S(1)}, u32[]{:S(2)}, u32[]{:S(2)}) collective-permute-start(f32[1024,128]{1,0:T(8,128)} %get-tuple-element.106), channel_id=1, source_target_pairs={{0,8},{8,0},{16,24},{24,16},{1,9},{9,1},{17,25},{25,17},{2,10},{10... | collective-permute-start | bytes 1572872 | tf_op jit(solution)/shard_map/ppermute | solution.py:343
  156.3 29.5 %collective-permute-start.24 = (f32[1024,128]{1,0:T(8,128)}, f32[1024,128]{1,0:T(8,128)S(1)}, u32[]{:S(2)}, u32[]{:S(2)}) collective-permute-start(f32[1024,128]{1,0:T(8,128)} %get-tuple-element.88), channel_id=1, source_target_pairs={{0,8},{8,0},{16,24},{24,16},{1,9},{9,1},{17,25},{25,17},{2,10},{10... | collective-permute-start | bytes 1572872 | tf_op jit(solution)/shard_map/ppermute | solution.py:343
  169.1 32.5 %collective-permute-start.7 = (f32[1024,128]{1,0:T(8,128)}, f32[1024,128]{1,0:T(8,128)S(1)}, u32[]{:S(2)}, u32[]{:S(2)}) collective-permute-start(f32[1024,128]{1,0:T(8,128)} %get-tuple-element.70), channel_id=1, source_target_pairs={{0,8},{8,0},{16,24},{24,16},{1,9},{9,1},{17,25},{25,17},{2,10},{10... | collective-permute-start | bytes 1572872 | tf_op jit(solution)/shard_map/ppermute | solution.py:343
  169.2 33.9 %collective-permute-start.42 = (f32[1024,128]{1,0:T(8,128)S(1)}, f32[1024,128]{1,0:T(8,128)S(1)}, u32[]{:S(2)}, u32[]{:S(2)}) collective-permute-start(f32[1024,128]{1,0:T(8,128)S(1)} %add.51), channel_id=1, source_target_pairs={{0,16},{8,24},{16,0},{24,8},{1,17},{9,25},{17,1},{25,9},{2,18},{10... | collective-permute-start | bytes 1572872 | tf_op jit(solution)/shard_map/ppermute | solution.py:346
  203.5 24.1 %collective-permute-start.26 = (f32[1024,128]{1,0:T(8,128)S(1)}, f32[1024,128]{1,0:T(8,128)S(1)}, u32[]{:S(2)}, u32[]{:S(2)}) collective-permute-start(f32[1024,128]{1,0:T(8,128)S(1)} %add_multiply_fusion.1.adj_mine), channel_id=1, source_target_pairs={{0,8},{8,0},{16,24},{24,16},{1,9},{9,1},{17,25},{25,17},{2,10},{10... | collective-permute-start | bytes 1572872 | tf_op jit(solution)/shard_map/ppermute | solution.py:349
  227.5 18.6 %collective-permute-start.47 = (f32[16,2048]{1,0:T(8,128)}, f32[16,2048]{1,0:T(8,128)S(1)}, u32[]{:S(2)}, u32[]{:S(2)}) collective-permute-start(f32[16,2048]{1,0:T(8,128)} %get-tuple-element.111), channel_id=1, source_target_pairs={{0,4},{1,5},{2,6},{3,7},{4,0},{5,1},{6,2},{7,3},{8,12},{9,13},{10,... | collective-permute-start | bytes 393224 | tf_op jit(solution)/shard_map/ppermute | solution.py:362
  229.1 20.7 %collective-permute-start.48 = (f32[16,2048]{1,0:T(8,128)}, f32[16,2048]{1,0:T(8,128)S(1)}, u32[]{:S(2)}, u32[]{:S(2)}) collective-permute-start(f32[16,2048]{1,0:T(8,128)} %get-tuple-element.112), channel_id=1, source_target_pairs={{0,5},{1,4},{2,7},{3,6},{4,1},{5,0},{6,3},{7,2},{8,13},{9,12},{10,... | collective-permute-start | bytes 393224 | tf_op jit(solution)/shard_map/ppermute | solution.py:362
  231.1 18.7 %collective-permute-start.49 = (f32[16,2048]{1,0:T(8,128)}, f32[16,2048]{1,0:T(8,128)S(1)}, u32[]{:S(2)}, u32[]{:S(2)}) collective-permute-start(f32[16,2048]{1,0:T(8,128)} %get-tuple-element.113), channel_id=1, source_target_pairs={{0,6},{1,7},{2,4},{3,5},{4,2},{5,3},{6,0},{7,1},{8,14},{9,15},{10,... | collective-permute-start | bytes 393224 | tf_op jit(solution)/shard_map/ppermute | solution.py:362
  236.4 20.4 %collective-permute-start.50 = (f32[16,2048]{1,0:T(8,128)S(1)}, f32[16,2048]{1,0:T(8,128)S(1)}, u32[]{:S(2)}, u32[]{:S(2)}) collective-permute-start(f32[16,2048]{1,0:T(8,128)S(1)} %copy-done.65), channel_id=1, source_target_pairs={{0,7},{1,6},{2,5},{3,4},{4,3},{5,2},{6,1},{7,0},{8,15},{9,14},{10,... | collective-permute-start | bytes 393224 | tf_op jit(solution)/shard_map/ppermute | solution.py:362
  239.0 18.9 %collective-permute-start.27 = (f32[16,2048]{1,0:T(8,128)}, f32[16,2048]{1,0:T(8,128)S(1)}, u32[]{:S(2)}, u32[]{:S(2)}) collective-permute-start(f32[16,2048]{1,0:T(8,128)} %get-tuple-element.90), channel_id=1, source_target_pairs={{0,1},{1,0},{2,3},{3,2},{4,5},{5,4},{6,7},{7,6},{8,9},{9,8},{10,11... | collective-permute-start | bytes 393224 | tf_op jit(solution)/shard_map/ppermute | solution.py:362
  249.8 19.2 %collective-permute-start.30 = (f32[16,2048]{1,0:T(8,128)}, f32[16,2048]{1,0:T(8,128)S(1)}, u32[]{:S(2)}, u32[]{:S(2)}) collective-permute-start(f32[16,2048]{1,0:T(8,128)} %get-tuple-element.93), channel_id=1, source_target_pairs={{0,4},{1,5},{2,6},{3,7},{4,0},{5,1},{6,2},{7,3},{8,12},{9,13},{10,... | collective-permute-start | bytes 393224 | tf_op jit(solution)/shard_map/ppermute | solution.py:362
  262.1 18.3 %collective-permute-start.10 = (f32[16,2048]{1,0:T(8,128)}, f32[16,2048]{1,0:T(8,128)S(1)}, u32[]{:S(2)}, u32[]{:S(2)}) collective-permute-start(f32[16,2048]{1,0:T(8,128)} %get-tuple-element.72), channel_id=1, source_target_pairs={{0,1},{1,0},{2,3},{3,2},{4,5},{5,4},{6,7},{7,6},{8,9},{9,8},{10,11... | collective-permute-start | bytes 393224 | tf_op jit(solution)/shard_map/ppermute | solution.py:362
  272.3 19.1 %collective-permute-start.13 = (f32[16,2048]{1,0:T(8,128)}, f32[16,2048]{1,0:T(8,128)S(1)}, u32[]{:S(2)}, u32[]{:S(2)}) collective-permute-start(f32[16,2048]{1,0:T(8,128)} %get-tuple-element.75), channel_id=1, source_target_pairs={{0,4},{1,5},{2,6},{3,7},{4,0},{5,1},{6,2},{7,3},{8,12},{9,13},{10,... | collective-permute-start | bytes 393224 | tf_op jit(solution)/shard_map/ppermute | solution.py:362
  274.8 20.0 %collective-permute-start.14 = (f32[16,2048]{1,0:T(8,128)}, f32[16,2048]{1,0:T(8,128)S(1)}, u32[]{:S(2)}, u32[]{:S(2)}) collective-permute-start(f32[16,2048]{1,0:T(8,128)} %get-tuple-element.76), channel_id=1, source_target_pairs={{0,5},{1,4},{2,7},{3,6},{4,1},{5,0},{6,3},{7,2},{8,13},{9,12},{10,... | collective-permute-start | bytes 393224 | tf_op jit(solution)/shard_map/ppermute | solution.py:362
  (96 other events, 1543.4 us)

commit v2 on v1

--- a/solution.py
+++ b/solution.py
@@ -28,53 +28,79 @@
     lax.fori_loop(0, size_x // 8, step, 0, unroll=2)
 
 
-def faces(diff, kx, ky, size_x, size_y):
-    lane = lax.broadcasted_iota(jnp.int32, (GROUP, size_y), 1)
-
-    def step(x, here):
-        following = diff[jnp.minimum(x + 1, size_x - 1)]
-        kx[x] = jnp.where(x < size_x - 1, 0.5 * (here + following), 0.0)
-        ahead = pltpu.roll(here, size_y - 1, 1)
-        ky[x] = jnp.where(lane < size_y - 1, 0.5 * (here + ahead), 0.0)
-        return following
-
-    lax.fori_loop(0, size_x, step, diff[0], unroll=4)
-
-
-def sweep(read, write, kx, ky, size_x, size_y):
-    def step(x, carry):
-        here, flux_before = carry
-        following = read(jnp.minimum(x + 1, size_x - 1))
-        flux_x = kx[x] * (following - here)
-        flux_y = ky[x] * (pltpu.roll(here, size_y - 1, 1) - here)
-        write(x, here + (flux_x - flux_before) + (flux_y - pltpu.roll(flux_y, 1, 1)))
-        return following, flux_x
-
-    first = read(0)
-    lax.fori_loop(0, size_x, step, (first, jnp.zeros_like(first)), unroll=8)
+def faces(diff, face_x, face_up, face_down, size_x, size_y):
+    lane = lax.broadcasted_iota(jnp.int32, (1, GROUP, size_y), 2)
+    rows = 16
+
+    def step(b, _):
+        first = pl.multiple_of(b * rows, rows)
+        here = diff[pl.ds(first, rows)]
+        beyond = diff[pl.ds(jnp.minimum(first + rows, size_x - 1), 1)]
+        ahead = jnp.concatenate([here[1:], beyond], axis=0)
+        row = first + lax.broadcasted_iota(jnp.int32, (rows, GROUP, size_y), 0)
+        face_x[pl.ds(first, rows)] = jnp.where(row < size_x - 1, 0.5 * (here + ahead), 0.0)
+        up = 0.5 * (here + pltpu.roll(here, size_y - 1, 2))
+        face_up[pl.ds(first, rows)] = jnp.where(lane < size_y - 1, up, 0.0)
+        down = 0.5 * (here + pltpu.roll(here, 1, 2))
+        face_down[pl.ds(first, rows)] = jnp.where(lane > 0, down, 0.0)
+        return 0
+
+    lax.fori_loop(0, size_x // rows, step, 0)
+
+
+def sweep(read, write, face_x, face_up, face_down, size_x, size_y):
+    rows = 8
+
+    def step(b, flux_before):
+        first = pl.multiple_of(b * rows, rows)
+        here = read(first, rows)
+        beyond = read(jnp.minimum(first + rows, size_x - 1), 1)
+        ahead = jnp.concatenate([here[1:], beyond], axis=0)
+        flux_x = face_x[pl.ds(first, rows)] * (ahead - here)
+        flux_up = face_up[pl.ds(first, rows)] * (pltpu.roll(here, size_y - 1, 2) - here)
+        flux_down = face_down[pl.ds(first, rows)] * (here - pltpu.roll(here, 1, 2))
+        behind = jnp.concatenate([flux_before, flux_x[:-1]], axis=0)
+        write(first, rows, here + (flux_x - behind) + (flux_up - flux_down))
+        return flux_x[-1:]
+
+    lax.fori_loop(0, size_x // rows, step, jnp.zeros((1, GROUP, size_y), F32), unroll=4)
+
+
+def on_grid(grid):
+    def read(first, rows):
+        return grid[pl.ds(first, rows)]
+
+    def write(first, rows, value):
+        grid[pl.ds(first, rows)] = value
+
+    return read, write
+
+
+def on_flat(flat, size_y):
+    def at(x):
+        return pl.ds(pl.multiple_of(x * size_y, size_y), size_y)
+
+    def read(first, rows):
+        return jnp.stack([flat[:, at(first + i)] for i in range(rows)], axis=0)
+
+    def write(first, rows, value):
+        for i in range(rows):
+            flat[:, at(first + i)] = value[i]
+
+    return read, write
 
 
 def forward_kernel(size_x, size_y, groups, capacity, starts, info, control, diffusivity, diff_out, *rest):
     outs = rest[: groups * PARTS]
-    grid, flat, kx, ky = rest[groups * PARTS :]
+    flat, one, two, *face_refs = rest[groups * PARTS :]
     columns = size_x * size_y
     part = capacity // PARTS
     transpose_in(diffusivity, diff_out, size_x)
-    faces(diff_out, kx, ky, size_x, size_y)
-    transpose_in(control.at[0], grid, size_x)
-
-    def read(x):
-        return grid[x]
-
-    def write(x, value):
-        grid[x] = value
-
-    def write_flat(x, value):
-        flat[:, pl.ds(pl.multiple_of(x * size_y, size_y), size_y)] = value
-
-    for repeat in range(STEPS - 1):
-        sweep(read, write, kx, ky, size_x, size_y)
-    sweep(read, write_flat, kx, ky, size_x, size_y)
+    faces(diff_out, *face_refs, size_x, size_y)
+    transpose_in(control.at[0], one, size_x)
+    stages = [on_grid((one, two)[i % 2]) for i in range(STEPS)] + [on_flat(flat, size_y)]
+    for i in range(STEPS):
+        sweep(stages[i][0], stages[i + 1][1], *face_refs, size_x, size_y)
     flat[:, columns:] = jnp.zeros((GROUP, flat.shape[1] - columns), F32)
 
     lane = lax.broadcasted_iota(jnp.int32, (GROUP, LANES), 1)
@@ -177,7 +203,7 @@
 
 def backward_kernel(size_x, size_y, groups, capacity, starts, info, diff, *rest):
     ins = rest[: groups * PARTS]
-    out, staging, flat, grid, kx, ky, sem = rest[groups * PARTS :]
+    out, staging, flat, one, two, *face_refs, sem = rest[groups * PARTS :]
     part = capacity // PARTS
     me = info[0]
     step_id = pl.program_id(0)
@@ -194,7 +220,7 @@
             )
     for copy in copies:
         copy.start()
-    faces(diff, kx, ky, size_x, size_y)
+    faces(diff, *face_refs, size_x, size_y)
     for copy in copies:
         copy.wait()
 
@@ -224,18 +250,10 @@
 
     lax.fori_loop(0, groups, place, 0)
 
-    def read_flat(x):
-        return flat[:, pl.ds(pl.multiple_of(x * size_y, size_y), size_y)]
-
-    def read(x):
-        return grid[x]
-
-    def write(x, value):
-        grid[x] = value
-
-    sweep(read_flat, write, kx, ky, size_x, size_y)
-    for repeat in range(STEPS - 1):
-        sweep(read, write, kx, ky, size_x, size_y)
+    stages = [on_flat(flat, size_y)] + [on_grid((one, two)[i % 2]) for i in range(STEPS)]
+    for i in range(STEPS):
+        sweep(stages[i][0], stages[i + 1][1], *face_refs, size_x, size_y)
+    grid = (one, two)[(STEPS - 1) % 2]
 
     def back(b, _):
         first = pl.multiple_of(b * 8, 8)
@@ -279,11 +297,9 @@
         + [pl.BlockSpec((GROUP, part), lambda g: (g, 0))] * (groups * PARTS),
         out_shape=[jax.ShapeDtypeStruct((size_x, levels_here, size_y), F32)] + [piece_shape] * (groups * PARTS),
         scratch_shapes=[
-            pltpu.VMEM((size_x, GROUP, size_y), F32),
             pltpu.VMEM((GROUP, flat_width), F32),
-            pltpu.VMEM((size_x, GROUP, size_y), F32),
-            pltpu.VMEM((size_x, GROUP, size_y), F32),
-        ],
+        ]
+        + [pltpu.VMEM((size_x, GROUP, size_y), F32)] * 5,
         compiler_params=params,
         name="smooth_and_cut",
     )(starts, info, control, diffusivity)
@@ -375,11 +391,9 @@
         scratch_shapes=[
             pltpu.VMEM((groups, GROUP, capacity), F32),
             pltpu.VMEM((GROUP, flat_width), F32),
-            pltpu.VMEM((size_x, GROUP, size_y), F32),
-            pltpu.VMEM((size_x, GROUP, size_y), F32),
-            pltpu.VMEM((size_x, GROUP, size_y), F32),
-            pltpu.SemaphoreType.DMA((groups * PARTS,)),
-        ],
+        ]
+        + [pltpu.VMEM((size_x, GROUP, size_y), F32)] * 5
+        + [pltpu.SemaphoreType.DMA((groups * PARTS,))],
         compiler_params=params,
         name="place_and_smooth",
     )(starts, info, diff, *adjoint_pieces)

time: 374 us -> 263 us (0.70)
  Pallas kernels: 214 us -> 103 us
    pallas_call x1, Pallas kernels: 70.6 us -> 14.6 us  [body(): pl.pallas_call(functools.partial(forward_kernel, size_x, size_y, groups,...]
    pallas_call x1, Pallas kernels: 76 us -> 20.7 us  [body(): pl.pallas_call(functools.partial(backward_kernel, size_x, size_y, groups,...]
  transfers between devices with their start and end apart: 51 -> 51, of which waited for: 9 -> 9; matrix products, arithmetic and copies ran while one was open for 2% -> 3% of each run, Pallas kernels for 18% -> 26%
where the time goes in v2:
time: 263 us; the launch traced here: 260 us
  Pallas kernels  103 us (39%)
  starting transfers between devices  88.8 us (34%)
  waiting for transfers between devices  53.1 us (20%)
  other arithmetic  8.16 us (3%)
  local copies, waits for them, and re-layouts  5.14 us (2%)
    ppermute x21, starting transfers between devices, body(): lax.ppermute(outgoing[c * groups + d], 'lev', flip_pairs(groups, d))  46.4 us
    pallas_call x3, Pallas kernels, body(): pl.pallas_call(functools.partial(observation_kernel, rows_here, obs_cap),...  45.2 us
    ppermute x21, starting transfers between devices, body(): adjoint_pieces.append(lax.ppermute(back[d], 'lev', flip_pairs(groups, d)))  38 us
    ppermute x21, waiting for transfers between devices, body(): adjoint_pieces.append(lax.ppermute(back[d], 'lev', flip_pairs(groups, d)))  28.9 us
    pallas_call x1, Pallas kernels, body(): pl.pallas_call(functools.partial(backward_kernel, size_x, size_y, groups,...  20.7 us
    pallas_call x1, Pallas kernels, body(): pl.pallas_call(functools.partial(forward_kernel, size_x, size_y, groups,...  14.6 us
    ppermute x21, waiting for transfers between devices, body(): lax.ppermute(outgoing[c * groups + d], 'lev', flip_pairs(groups, d))  12.8 us
    ppermute x3, waiting for transfers between devices, body(): total = total + lax.ppermute(total, 'mem', flip_pairs(n_mem, bit))  11.5 us
  transfers between devices with their start and end apart: 51, of which 9 were waited for; matrix products, arithmetic and copies ran while one was open for 3% of the time, Pallas kernels for 26%

profile of v2, /device:TPU:0, one launch (start us, length us, event | category | flops | bytes accessed | tf_op | source)
XLA Modules:
  0.0 260.4 jit_solution(11577634037466057457)
XLA Ops:
  2.7 14.6 %smooth_and_cut.1 = (f32[128,16,256]{2,1,0:T(8,128)}, f32[16,2048]{1,0:T(8,128)}, f32[16,2048]{1,0:T(8,128)}, f32[16,2048]{1,0:T(8,128)}, f32[16,2048]{1,0:T(8,1...) custom-call(s32[8]{0:T(128)} %bitcast_subtract_fusion.starts, ...), custom_call_target="tpu_custom_call" | custom-call | tf_op jit(solution)/shard_map/smooth_and_cut/pallas_call | solution.py:287
  32.1 3.6 %collective-permute-start.39 = (f32[16,2048]{1,0:T(8,128)}, f32[16,2048]{1,0:T(8,128)S(1)}, u32[]{:S(2)}, u32[]{:S(2)}) collective-permute-start(f32[16,2048]{1,0:T(8,128)} %get-tuple-element.103), channel_id=1, source_target_pairs={{0,6},{1,7},{2,4},{3,5},{4,2},{5,3},{6,0},{7,1},{8,14},{9,15},{10,... | collective-permute-start | bytes 393224 | tf_op jit(solution)/shard_map/ppermute | solution.py:340
  38.8 5.7 %collective-permute-done.38.rest_5_ = f32[16,2048]{1,0:T(8,128)S(1)} collective-permute-done((f32[16,2048]{1,0:T(8,128)}, f32[16,2048]{1,0:T(8,128)S(1)}, u32[]{:S(2)}, u32[]{:S(2)}) %collective-permute-start.38) | collective-permute-done | bytes 131104 | tf_op jit(solution)/shard_map/ppermute | solution.py:340
  45.1 5.3 %collective-permute-start.20 = (f32[16,2048]{1,0:T(8,128)}, f32[16,2048]{1,0:T(8,128)S(1)}, u32[]{:S(2)}, u32[]{:S(2)}) collective-permute-start(f32[16,2048]{1,0:T(8,128)} %get-tuple-element.83), channel_id=1, source_target_pairs={{0,4},{1,5},{2,6},{3,7},{4,0},{5,1},{6,2},{7,3},{8,12},{9,13},{10,... | collective-permute-start | bytes 393224 | tf_op jit(solution)/shard_map/ppermute | solution.py:340
  50.4 8.1 %collective-permute-start.21 = (f32[16,2048]{1,0:T(8,128)}, f32[16,2048]{1,0:T(8,128)S(1)}, u32[]{:S(2)}, u32[]{:S(2)}) collective-permute-start(f32[16,2048]{1,0:T(8,128)} %get-tuple-element.84), channel_id=1, source_target_pairs={{0,5},{1,4},{2,7},{3,6},{4,1},{5,0},{6,3},{7,2},{8,13},{9,12},{10,... | collective-permute-start | bytes 393224 | tf_op jit(solution)/shard_map/ppermute | solution.py:340
  59.3 3.8 %filter_forward.5 = (f32[1024,128]{1,0:T(8,128)}, f32[1024,128]{1,0:T(8,128)}) custom-call(s32[2]{0:T(128)} %pad_add_fusion.info, f32[128,128]{1,0:T(8,128)} %copy.11.vfilter, f32[1,6144,128]{2,1,0:T(8,128)} %perturb.11, f32[16,2048]{1,0:T(8,128)} %get-tuple-element.97.rest_0_, f32[16,2048]{1,0:T(8,128)} %copy-done.33, f32[16,2048]{1,0:T(8,128)} %copy-done.34, ...), custom_call_target="tpu_custom_call" | custom-call | flops 201326592 | bytes 3145728 | tf_op jit(solution)/shard_map/filter_forward/pallas_call | solution.py:349
  63.1 5.2 %collective-permute-start = (f32[16,2048]{1,0:T(8,128)S(1)}, f32[16,2048]{1,0:T(8,128)S(1)}, u32[]{:S(2)}, u32[]{:S(2)}) collective-permute-start(f32[16,2048]{1,0:T(8,128)S(1)} %copy-done.62), channel_id=1, source_target_pairs={{0,1},{1,0},{2,3},{3,2},{4,5},{5,4},{6,7},{7,6},{8,9},{9,8},{10,11... | collective-permute-start | bytes 393224 | tf_op jit(solution)/shard_map/ppermute | solution.py:340
  73.1 15.1 %observation_weights.5 = f32[1024,128]{1,0:T(8,128)} custom-call(s32[3]{0:T(128)} %pad_add_fusion.4.info, s32[1,6144]{1,0:T(1,128)} %compare_select_fusion.slots, f32[1,6144,128]{2,1,0:T(8,128)} %rinv.5), custom_call_target="tpu_custom_call" | custom-call | flops 3221225472 | bytes 3145728 | tf_op jit(solution)/shard_map/observation_weights/pallas_call | solution.py:320
  88.2 3.8 %filter_forward.4 = (f32[1024,128]{1,0:T(8,128)}, f32[1024,128]{1,0:T(8,128)}) custom-call(s32[2]{0:T(128)} %pad_add_fusion.info, f32[128,128]{1,0:T(8,128)} %copy.11.vfilter, f32[1,6144,128]{2,1,0:T(8,128)} %perturb.11, f32[16,2048]{1,0:T(8,128)} %get-tuple-element.79.rest_0_, f32[16,2048]{1,0:T(8,128)} %copy-done.35, f32[16,2048]{1,0:T(8,128)} %copy-done.39, ...), custom_call_target="tpu_custom_call" | custom-call | flops 201326592 | bytes 3145728 | tf_op jit(solution)/shard_map/filter_forward/pallas_call | solution.py:349
  101.6 7.0 %collective-permute-done.4.rest_5_ = f32[16,2048]{1,0:T(8,128)S(1)} collective-permute-done((f32[16,2048]{1,0:T(8,128)S(1)}, f32[16,2048]{1,0:T(8,128)S(1)}, u32[]{:S(2)}, u32[]{:S(2)}) %collective-permute-start.4) | collective-permute-done | bytes 131104 | tf_op jit(solution)/shard_map/ppermute | solution.py:340
  109.4 3.8 %filter_forward.3 = (f32[1024,128]{1,0:T(8,128)}, f32[1024,128]{1,0:T(8,128)}) custom-call(s32[2]{0:T(128)} %pad_add_fusion.info, f32[128,128]{1,0:T(8,128)} %copy.11.vfilter, f32[1,6144,128]{2,1,0:T(8,128)} %perturb.11, f32[16,2048]{1,0:T(8,128)} %get-tuple-element.61.rest_0_, f32[16,2048]{1,0:T(8,128)} %copy-done.40, f32[16,2048]{1,0:T(8,128)} %copy-done.42, ...), custom_call_target="tpu_custom_call" | custom-call | flops 201326592 | bytes 3145728 | tf_op jit(solution)/shard_map/filter_forward/pallas_call | solution.py:349
  114.7 15.1 %observation_weights.4 = f32[1024,128]{1,0:T(8,128)} custom-call(s32[3]{0:T(128)} %pad_add_fusion.3.info, s32[1,6144]{1,0:T(1,128)} %compare_select_fusion.slots, f32[1,6144,128]{2,1,0:T(8,128)} %rinv.5), custom_call_target="tpu_custom_call" | custom-call | flops 3221225472 | bytes 3145728 | tf_op jit(solution)/shard_map/observation_weights/pallas_call | solution.py:320
  130.5 15.0 %observation_weights.3 = f32[1024,128]{1,0:T(8,128)} custom-call(s32[3]{0:T(128)} %pad_add_fusion.1.info, s32[1,6144]{1,0:T(1,128)} %compare_select_fusion.slots, f32[1,6144,128]{2,1,0:T(8,128)} %rinv.5), custom_call_target="tpu_custom_call" | custom-call | flops 3221225472 | bytes 3145728 | tf_op jit(solution)/shard_map/observation_weights/pallas_call | solution.py:320
  148.0 11.5 %collective-permute-done.8 = f32[1024,128]{1,0:T(8,128)S(1)} collective-permute-done((f32[1024,128]{1,0:T(8,128)S(1)}, f32[1024,128]{1,0:T(8,128)S(1)}, u32[]{:S(2)}, u32[]{:S(2)}) %collective-permute-start.8) | collective-permute-done | bytes 524320 | tf_op jit(solution)/shard_map/ppermute | solution.py:362
  160.6 3.7 %filter_backward.5 = (f32[16,2048]{1,0:T(8,128)}, f32[16,2048]{1,0:T(8,128)}, f32[16,2048]{1,0:T(8,128)}, f32[16,2048]{1,0:T(8,128)}, f32[16,2048]{1,0:T(8,128)}...) custom-call(s32[2]{0:T(128)} %pad_add_fusion.info, f32[128,128]{1,0:T(8,128)} %copy.11.vfilter, ...), custom_call_target="tpu_custom_call" | custom-call | flops 201326592 | bytes 3145728 | tf_op jit(solution)/shard_map/filter_backward/pallas_call | solution.py:366
  165.4 5.9 %collective-permute-start.45 = (f32[16,2048]{1,0:T(8,128)}, f32[16,2048]{1,0:T(8,128)S(1)}, u32[]{:S(2)}, u32[]{:S(2)}) collective-permute-start(f32[16,2048]{1,0:T(8,128)} %get-tuple-element.109), channel_id=1, source_target_pairs={{0,2},{1,3},{2,0},{3,1},{4,6},{5,7},{6,4},{7,5},{8,10},{9,11},{10,... | collective-permute-start | bytes 393224 | tf_op jit(solution)/shard_map/ppermute | solution.py:378
  176.6 3.7 %filter_backward.4 = (f32[16,2048]{1,0:T(8,128)}, f32[16,2048]{1,0:T(8,128)}, f32[16,2048]{1,0:T(8,128)}, f32[16,2048]{1,0:T(8,128)}, f32[16,2048]{1,0:T(8,128)}...) custom-call(s32[2]{0:T(128)} %pad_add_fusion.info, f32[128,128]{1,0:T(8,128)} %copy.11.vfilter, ...), custom_call_target="tpu_custom_call" | custom-call | flops 201326592 | bytes 3145728 | tf_op jit(solution)/shard_map/filter_backward/pallas_call | solution.py:366
  184.2 5.9 %collective-permute-done.47.rest_20_ = f32[16,2048]{1,0:T(8,128)S(1)} collective-permute-done((f32[16,2048]{1,0:T(8,128)}, f32[16,2048]{1,0:T(8,128)S(1)}, u32[]{:S(2)}, u32[]{:S(2)}) %collective-permute-start.47) | collective-permute-done | bytes 131104 | tf_op jit(solution)/shard_map/ppermute | solution.py:378
  190.1 3.7 %collective-permute-done.48.rest_21_ = f32[16,2048]{1,0:T(8,128)S(1)} collective-permute-done((f32[16,2048]{1,0:T(8,128)}, f32[16,2048]{1,0:T(8,128)S(1)}, u32[]{:S(2)}, u32[]{:S(2)}) %collective-permute-start.48) | collective-permute-done | bytes 131104 | tf_op jit(solution)/shard_map/ppermute | solution.py:378
  197.0 3.7 %filter_backward.3 = (f32[16,2048]{1,0:T(8,128)}, f32[16,2048]{1,0:T(8,128)}, f32[16,2048]{1,0:T(8,128)}, f32[16,2048]{1,0:T(8,128)}, f32[16,2048]{1,0:T(8,128)}...) custom-call(s32[2]{0:T(128)} %pad_add_fusion.info, f32[128,128]{1,0:T(8,128)} %copy.11.vfilter, ...), custom_call_target="tpu_custom_call" | custom-call | flops 201326592 | bytes 3145728 | tf_op jit(solution)/shard_map/filter_backward/pallas_call | solution.py:366
  207.3 5.7 %collective-permute-done.30.rest_12_ = f32[16,2048]{1,0:T(8,128)S(1)} collective-permute-done((f32[16,2048]{1,0:T(8,128)}, f32[16,2048]{1,0:T(8,128)S(1)}, u32[]{:S(2)}, u32[]{:S(2)}) %collective-permute-start.30) | collective-permute-done | bytes 131104 | tf_op jit(solution)/shard_map/ppermute | solution.py:378
  218.8 5.6 %collective-permute-start.14 = (f32[16,2048]{1,0:T(8,128)}, f32[16,2048]{1,0:T(8,128)S(1)}, u32[]{:S(2)}, u32[]{:S(2)}) collective-permute-start(f32[16,2048]{1,0:T(8,128)} %get-tuple-element.76), channel_id=1, source_target_pairs={{0,5},{1,4},{2,7},{3,6},{4,1},{5,0},{6,3},{7,2},{8,13},{9,12},{10,... | collective-permute-start | bytes 393224 | tf_op jit(solution)/shard_map/ppermute | solution.py:378
  228.5 6.9 %collective-permute-done.13.rest_4_ = f32[16,2048]{1,0:T(8,128)S(1)} collective-permute-done((f32[16,2048]{1,0:T(8,128)}, f32[16,2048]{1,0:T(8,128)S(1)}, u32[]{:S(2)}, u32[]{:S(2)}) %collective-permute-start.13) | collective-permute-done | bytes 131104 | tf_op jit(solution)/shard_map/ppermute | solution.py:378
  239.5 20.7 %place_and_smooth.1 = f32[1,16,128,256]{3,2,1,0:T(8,128)} custom-call(s32[8]{0:T(128)} %bitcast_subtract_fusion.starts, s32[2]{0:T(128)} %pad_add_fusion.info, f32[128,16,256]{2,1,0:T(8,128)} %get-tuple-element.60.diff, f32[16,2048]{1,0:T(8,128)} %get-tuple-element.71.rest_0_, f32[16,2048]{1,0:T(8,128)} %copy-done.26, f32[16,2048]{1,0:T(8,128)} %copy-done.27, ...), custom_call_target="tpu_custom_call" | custom-call | tf_op jit(solution)/shard_map/place_and_smooth/pallas_call | solution.py:380
  (247 shorter events, 75.2 us)
Async XLA Ops:
  24.8 19.7 %collective-permute-start.38 = (f32[16,2048]{1,0:T(8,128)}, f32[16,2048]{1,0:T(8,128)S(1)}, u32[]{:S(2)}, u32[]{:S(2)}) collective-permute-start(f32[16,2048]{1,0:T(8,128)} %get-tuple-element.102), channel_id=1, source_target_pairs={{0,5},{1,4},{2,7},{3,6},{4,1},{5,0},{6,3},{7,2},{8,13},{9,12},{10,... | collective-permute-start | bytes 393224 | tf_op jit(solution)/shard_map/ppermute | solution.py:340
  35.7 22.8 %collective-permute-start.17 = (f32[16,2048]{1,0:T(8,128)}, f32[16,2048]{1,0:T(8,128)S(1)}, u32[]{:S(2)}, u32[]{:S(2)}) collective-permute-start(f32[16,2048]{1,0:T(8,128)} %get-tuple-element.80), channel_id=1, source_target_pairs={{0,1},{1,0},{2,3},{3,2},{4,5},{5,4},{6,7},{7,6},{8,9},{9,8},{10,11... | collective-permute-start | bytes 393224 | tf_op jit(solution)/shard_map/ppermute | solution.py:340
  37.4 21.1 %collective-permute-start.18 = (f32[16,2048]{1,0:T(8,128)}, f32[16,2048]{1,0:T(8,128)S(1)}, u32[]{:S(2)}, u32[]{:S(2)}) collective-permute-start(f32[16,2048]{1,0:T(8,128)} %get-tuple-element.81), channel_id=1, source_target_pairs={{0,2},{1,3},{2,0},{3,1},{4,6},{5,7},{6,4},{7,5},{8,10},{9,11},{10,... | collective-permute-start | bytes 393224 | tf_op jit(solution)/shard_map/ppermute | solution.py:340
  44.5 18.6 %collective-permute-start.19 = (f32[16,2048]{1,0:T(8,128)}, f32[16,2048]{1,0:T(8,128)S(1)}, u32[]{:S(2)}, u32[]{:S(2)}) collective-permute-start(f32[16,2048]{1,0:T(8,128)} %get-tuple-element.82), channel_id=1, source_target_pairs={{0,3},{1,2},{2,1},{3,0},{4,7},{5,6},{6,5},{7,4},{8,11},{9,10},{10,... | collective-permute-start | bytes 393224 | tf_op jit(solution)/shard_map/ppermute | solution.py:340
  45.1 23.3 %collective-permute-start.20 = (f32[16,2048]{1,0:T(8,128)}, f32[16,2048]{1,0:T(8,128)S(1)}, u32[]{:S(2)}, u32[]{:S(2)}) collective-permute-start(f32[16,2048]{1,0:T(8,128)} %get-tuple-element.83), channel_id=1, source_target_pairs={{0,4},{1,5},{2,6},{3,7},{4,0},{5,1},{6,2},{7,3},{8,12},{9,13},{10,... | collective-permute-start | bytes 393224 | tf_op jit(solution)/shard_map/ppermute | solution.py:340
  50.4 18.0 %collective-permute-start.21 = (f32[16,2048]{1,0:T(8,128)}, f32[16,2048]{1,0:T(8,128)S(1)}, u32[]{:S(2)}, u32[]{:S(2)}) collective-permute-start(f32[16,2048]{1,0:T(8,128)} %get-tuple-element.84), channel_id=1, source_target_pairs={{0,5},{1,4},{2,7},{3,6},{4,1},{5,0},{6,3},{7,2},{8,13},{9,12},{10,... | collective-permute-start | bytes 393224 | tf_op jit(solution)/shard_map/ppermute | solution.py:340
  63.1 28.9 %collective-permute-start = (f32[16,2048]{1,0:T(8,128)S(1)}, f32[16,2048]{1,0:T(8,128)S(1)}, u32[]{:S(2)}, u32[]{:S(2)}) collective-permute-start(f32[16,2048]{1,0:T(8,128)S(1)} %copy-done.62), channel_id=1, source_target_pairs={{0,1},{1,0},{2,3},{3,2},{4,5},{5,4},{6,7},{7,6},{8,9},{9,8},{10,11... | collective-permute-start | bytes 393224 | tf_op jit(solution)/shard_map/ppermute | solution.py:340
  68.3 27.0 %collective-permute-start.1 = (f32[16,2048]{1,0:T(8,128)S(1)}, f32[16,2048]{1,0:T(8,128)S(1)}, u32[]{:S(2)}, u32[]{:S(2)}) collective-permute-start(f32[16,2048]{1,0:T(8,128)S(1)} %copy-done.61), channel_id=1, source_target_pairs={{0,2},{1,3},{2,0},{3,1},{4,6},{5,7},{6,4},{7,5},{8,10},{9,11},{10,... | collective-permute-start | bytes 393224 | tf_op jit(solution)/shard_map/ppermute | solution.py:340
  68.5 28.4 %collective-permute-start.2 = (f32[16,2048]{1,0:T(8,128)S(1)}, f32[16,2048]{1,0:T(8,128)S(1)}, u32[]{:S(2)}, u32[]{:S(2)}) collective-permute-start(f32[16,2048]{1,0:T(8,128)S(1)} %copy-done.60), channel_id=1, source_target_pairs={{0,3},{1,2},{2,1},{3,0},{4,7},{5,6},{6,5},{7,4},{8,11},{9,10},{10,... | collective-permute-start | bytes 393224 | tf_op jit(solution)/shard_map/ppermute | solution.py:340
  70.0 30.3 %collective-permute-start.3 = (f32[16,2048]{1,0:T(8,128)S(1)}, f32[16,2048]{1,0:T(8,128)S(1)}, u32[]{:S(2)}, u32[]{:S(2)}) collective-permute-start(f32[16,2048]{1,0:T(8,128)S(1)} %copy-done.59), channel_id=1, source_target_pairs={{0,4},{1,5},{2,6},{3,7},{4,0},{5,1},{6,2},{7,3},{8,12},{9,13},{10,... | collective-permute-start | bytes 393224 | tf_op jit(solution)/shard_map/ppermute | solution.py:340
  73.1 40.1 %collective-permute-start.41 = (f32[1024,128]{1,0:T(8,128)}, f32[1024,128]{1,0:T(8,128)S(1)}, u32[]{:S(2)}, u32[]{:S(2)}) collective-permute-start(f32[1024,128]{1,0:T(8,128)} %get-tuple-element.106), channel_id=1, source_target_pairs={{0,8},{8,0},{16,24},{24,16},{1,9},{9,1},{17,25},{25,17},{2,10},{10... | collective-permute-start | bytes 1572872 | tf_op jit(solution)/shard_map/ppermute | solution.py:359
  100.3 29.5 %collective-permute-start.24 = (f32[1024,128]{1,0:T(8,128)}, f32[1024,128]{1,0:T(8,128)S(1)}, u32[]{:S(2)}, u32[]{:S(2)}) collective-permute-start(f32[1024,128]{1,0:T(8,128)} %get-tuple-element.88), channel_id=1, source_target_pairs={{0,8},{8,0},{16,24},{24,16},{1,9},{9,1},{17,25},{25,17},{2,10},{10... | collective-permute-start | bytes 1572872 | tf_op jit(solution)/shard_map/ppermute | solution.py:359
  113.1 32.5 %collective-permute-start.7 = (f32[1024,128]{1,0:T(8,128)}, f32[1024,128]{1,0:T(8,128)S(1)}, u32[]{:S(2)}, u32[]{:S(2)}) collective-permute-start(f32[1024,128]{1,0:T(8,128)} %get-tuple-element.70), channel_id=1, source_target_pairs={{0,8},{8,0},{16,24},{24,16},{1,9},{9,1},{17,25},{25,17},{2,10},{10... | collective-permute-start | bytes 1572872 | tf_op jit(solution)/shard_map/ppermute | solution.py:359
  113.2 33.9 %collective-permute-start.42 = (f32[1024,128]{1,0:T(8,128)S(1)}, f32[1024,128]{1,0:T(8,128)S(1)}, u32[]{:S(2)}, u32[]{:S(2)}) collective-permute-start(f32[1024,128]{1,0:T(8,128)S(1)} %add.51), channel_id=1, source_target_pairs={{0,16},{8,24},{16,0},{24,8},{1,17},{9,25},{17,1},{25,9},{2,18},{10... | collective-permute-start | bytes 1572872 | tf_op jit(solution)/shard_map/ppermute | solution.py:362
  147.5 24.1 %collective-permute-start.26 = (f32[1024,128]{1,0:T(8,128)S(1)}, f32[1024,128]{1,0:T(8,128)S(1)}, u32[]{:S(2)}, u32[]{:S(2)}) collective-permute-start(f32[1024,128]{1,0:T(8,128)S(1)} %add_multiply_fusion.1.adj_mine), channel_id=1, source_target_pairs={{0,8},{8,0},{16,24},{24,16},{1,9},{9,1},{17,25},{25,17},{2,10},{10... | collective-permute-start | bytes 1572872 | tf_op jit(solution)/shard_map/ppermute | solution.py:365
  171.5 18.6 %collective-permute-start.47 = (f32[16,2048]{1,0:T(8,128)}, f32[16,2048]{1,0:T(8,128)S(1)}, u32[]{:S(2)}, u32[]{:S(2)}) collective-permute-start(f32[16,2048]{1,0:T(8,128)} %get-tuple-element.111), channel_id=1, source_target_pairs={{0,4},{1,5},{2,6},{3,7},{4,0},{5,1},{6,2},{7,3},{8,12},{9,13},{10,... | collective-permute-start | bytes 393224 | tf_op jit(solution)/shard_map/ppermute | solution.py:378
  173.1 20.7 %collective-permute-start.48 = (f32[16,2048]{1,0:T(8,128)}, f32[16,2048]{1,0:T(8,128)S(1)}, u32[]{:S(2)}, u32[]{:S(2)}) collective-permute-start(f32[16,2048]{1,0:T(8,128)} %get-tuple-element.112), channel_id=1, source_target_pairs={{0,5},{1,4},{2,7},{3,6},{4,1},{5,0},{6,3},{7,2},{8,13},{9,12},{10,... | collective-permute-start | bytes 393224 | tf_op jit(solution)/shard_map/ppermute | solution.py:378
  175.1 18.7 %collective-permute-start.49 = (f32[16,2048]{1,0:T(8,128)}, f32[16,2048]{1,0:T(8,128)S(1)}, u32[]{:S(2)}, u32[]{:S(2)}) collective-permute-start(f32[16,2048]{1,0:T(8,128)} %get-tuple-element.113), channel_id=1, source_target_pairs={{0,6},{1,7},{2,4},{3,5},{4,2},{5,3},{6,0},{7,1},{8,14},{9,15},{10,... | collective-permute-start | bytes 393224 | tf_op jit(solution)/shard_map/ppermute | solution.py:378
  180.4 20.4 %collective-permute-start.50 = (f32[16,2048]{1,0:T(8,128)S(1)}, f32[16,2048]{1,0:T(8,128)S(1)}, u32[]{:S(2)}, u32[]{:S(2)}) collective-permute-start(f32[16,2048]{1,0:T(8,128)S(1)} %copy-done.65), channel_id=1, source_target_pairs={{0,7},{1,6},{2,5},{3,4},{4,3},{5,2},{6,1},{7,0},{8,15},{9,14},{10,... | collective-permute-start | bytes 393224 | tf_op jit(solution)/shard_map/ppermute | solution.py:378
  183.0 18.9 %collective-permute-start.27 = (f32[16,2048]{1,0:T(8,128)}, f32[16,2048]{1,0:T(8,128)S(1)}, u32[]{:S(2)}, u32[]{:S(2)}) collective-permute-start(f32[16,2048]{1,0:T(8,128)} %get-tuple-element.90), channel_id=1, source_target_pairs={{0,1},{1,0},{2,3},{3,2},{4,5},{5,4},{6,7},{7,6},{8,9},{9,8},{10,11... | collective-permute-start | bytes 393224 | tf_op jit(solution)/shard_map/ppermute | solution.py:378
  193.8 19.2 %collective-permute-start.30 = (f32[16,2048]{1,0:T(8,128)}, f32[16,2048]{1,0:T(8,128)S(1)}, u32[]{:S(2)}, u32[]{:S(2)}) collective-permute-start(f32[16,2048]{1,0:T(8,128)} %get-tuple-element.93), channel_id=1, source_target_pairs={{0,4},{1,5},{2,6},{3,7},{4,0},{5,1},{6,2},{7,3},{8,12},{9,13},{10,... | collective-permute-start | bytes 393224 | tf_op jit(solution)/shard_map/ppermute | solution.py:378
  206.1 18.2 %collective-permute-start.10 = (f32[16,2048]{1,0:T(8,128)}, f32[16,2048]{1,0:T(8,128)S(1)}, u32[]{:S(2)}, u32[]{:S(2)}) collective-permute-start(f32[16,2048]{1,0:T(8,128)} %get-tuple-element.72), channel_id=1, source_target_pairs={{0,1},{1,0},{2,3},{3,2},{4,5},{5,4},{6,7},{7,6},{8,9},{9,8},{10,11... | collective-permute-start | bytes 393224 | tf_op jit(solution)/shard_map/ppermute | solution.py:378
  216.3 19.1 %collective-permute-start.13 = (f32[16,2048]{1,0:T(8,128)}, f32[16,2048]{1,0:T(8,128)S(1)}, u32[]{:S(2)}, u32[]{:S(2)}) collective-permute-start(f32[16,2048]{1,0:T(8,128)} %get-tuple-element.75), channel_id=1, source_target_pairs={{0,4},{1,5},{2,6},{3,7},{4,0},{5,1},{6,2},{7,3},{8,12},{9,13},{10,... | collective-permute-start | bytes 393224 | tf_op jit(solution)/shard_map/ppermute | solution.py:378
  218.8 20.0 %collective-permute-start.14 = (f32[16,2048]{1,0:T(8,128)}, f32[16,2048]{1,0:T(8,128)S(1)}, u32[]{:S(2)}, u32[]{:S(2)}) collective-permute-start(f32[16,2048]{1,0:T(8,128)} %get-tuple-element.76), channel_id=1, source_target_pairs={{0,5},{1,4},{2,7},{3,6},{4,1},{5,0},{6,3},{7,2},{8,13},{9,12},{10,... | collective-permute-start | bytes 393224 | tf_op jit(solution)/shard_map/ppermute | solution.py:378
  (96 other events, 1319.3 us)

commit v3 on v2

--- a/solution.py
+++ b/solution.py
@@ -8,7 +8,7 @@
 from jax.sharding import PartitionSpec as P
 
 STEPS = 4
-PARTS = 3
+PARTS = 2
 LANES = 128
 GROUP = 8
 F32 = jnp.float32
@@ -90,7 +90,11 @@
     return read, write
 
 
-def forward_kernel(size_x, size_y, groups, capacity, starts, info, control, diffusivity, diff_out, *rest):
+def start_of(widths, j):
+    return lax.fori_loop(0, j, lambda k, total: total + widths[k], jnp.int32(0))
+
+
+def forward_kernel(size_x, size_y, groups, capacity, widths, control, diffusivity, diff_out, *rest):
     outs = rest[: groups * PARTS]
     flat, one, two, *face_refs = rest[groups * PARTS :]
     columns = size_x * size_y
@@ -104,10 +108,10 @@
     flat[:, columns:] = jnp.zeros((GROUP, flat.shape[1] - columns), F32)
 
     lane = lax.broadcasted_iota(jnp.int32, (GROUP, LANES), 1)
-    me = info[0]
+    me = lax.axis_index("lev")
     tiles = part // LANES
-    for d in range(groups):
-        start = starts[jnp.bitwise_xor(me, d)]
+    for d, turn in enumerate(turns_of(groups)):
+        start = start_of(widths, jnp.bitwise_xor(me, turn))
         base = start // LANES
         shift = start - base * LANES
         back = lax.rem(LANES - shift, LANES)
@@ -127,48 +131,46 @@
                 now = later
 
 
-def split3(value):
+def turns_of(groups):
+    return [0] + list(range(groups // 2, groups)) + list(range(groups // 2 - 1, 0, -1))
+
+
+def split2(value):
     high = value.astype(BF16)
     return high, (value - high.astype(F32)).astype(BF16)
 
 
 def dot3(a, b, dims):
-    ah, al = split3(a)
-    bh, bl = split3(b)
+    ah, al = split2(a)
+    bh, bl = split2(b)
     dot = functools.partial(lax.dot_general, dimension_numbers=(dims, ((), ())), preferred_element_type=F32)
     return dot(ah, bh) + (dot(ah, bl) + dot(al, bh))
 
 
-def observation_kernel(rows_here, obs_cap, info, slots, rinv, out, split):
+def observation_kernel(part_rows, index, obs_cap, slots, rinv, out, split):
     step = pl.program_id(0)
+    rows_here, levels = out.shape
 
     @pl.when(step == 0)
     def _():
-        values = rinv[0]
-        high = values.astype(BF16)
-        split[:, :LANES] = high
-        split[:, LANES:] = (values - high.astype(F32)).astype(BF16)
-
-    first = info[2] + step * rows_here
-    block = 512
-    row = first + lax.broadcasted_iota(jnp.int32, (rows_here, block), 0)
-
-    def add(b, total):
-        at = pl.multiple_of(b * block, block)
-        hit = row == slots[:, pl.ds(at, block)]
-        onehot = jnp.where(hit, 1.0, 0.0).astype(BF16)
-        return total + jnp.dot(onehot, split[pl.ds(at, block), :], preferred_element_type=F32)
-
-    total = lax.fori_loop(0, obs_cap // block, add, jnp.zeros((rows_here, 2 * LANES), F32))
-    out[...] = total[:, :LANES] + total[:, LANES:]
-
-
-def filter_kernel(groups, info, vfilter, perturb, *rest):
+        high, low = split2(rinv[0])
+        split[:, :levels] = high
+        split[:, levels:] = low
+
+    core = lax.axis_index("mem") % 2
+    first = index * part_rows + core * (part_rows // 2) + step * rows_here
+    row = first + lax.broadcasted_iota(jnp.int32, (rows_here, obs_cap), 0)
+    onehot = jnp.where(row == slots[...], 1.0, 0.0).astype(BF16)
+    total = jnp.dot(onehot, split[...], preferred_element_type=F32)
+    out[...] = total[:, :levels] + total[:, levels:]
+
+
+def filter_kernel(groups, vfilter, perturb, *rest):
     pieces = rest[:groups]
     keep, send = rest[groups:]
     half = keep.shape[0]
     width = 256
-    mine = info[1]
+    mine = lax.axis_index("mem") % 2
     for which, out in ((mine, keep), (1 - mine, send)):
 
         def step(b, _):
@@ -183,11 +185,11 @@
         lax.fori_loop(0, half // width, step, 0, unroll=2)
 
 
-def back_kernel(groups, info, vfilter, perturb, adj_mine, adj_other, *pieces):
+def back_kernel(groups, vfilter, perturb, adj_mine, adj_other, *pieces):
     half = adj_mine.shape[0]
     width = 256
     levels = pieces[0].shape[0]
-    mine = info[1]
+    mine = lax.axis_index("mem") % 2
     for which, adj in ((mine, adj_mine), (1 - mine, adj_other)):
 
         def step(b, _):
@@ -201,20 +203,20 @@
         lax.fori_loop(0, half // width, step, 0, unroll=2)
 
 
-def backward_kernel(size_x, size_y, groups, capacity, starts, info, diff, *rest):
+def backward_kernel(size_x, size_y, groups, capacity, widths, diff, *rest):
     ins = rest[: groups * PARTS]
     out, staging, flat, one, two, *face_refs, sem = rest[groups * PARTS :]
     part = capacity // PARTS
-    me = info[0]
+    me = lax.axis_index("lev")
     step_id = pl.program_id(0)
     level = pl.multiple_of(step_id * GROUP, GROUP)
     copies = []
     for c in range(PARTS):
-        for d in range(groups):
+        for d, turn in enumerate(turns_of(groups)):
             copies.append(
                 pltpu.make_async_copy(
                     ins[c * groups + d].at[pl.ds(level, GROUP), :],
-                    staging.at[jnp.bitwise_xor(me, d), :, pl.ds(c * part, part)],
+                    staging.at[jnp.bitwise_xor(me, turn), :, pl.ds(c * part, part)],
                     sem.at[c * groups + d],
                 )
             )
@@ -229,7 +231,7 @@
     some = 8
 
     def place(j, _):
-        start = starts[j]
+        start = start_of(widths, j)
         base = start // LANES
         shift = start - base * LANES
         high = lane >= shift
@@ -261,6 +263,10 @@
         return 0
 
     lax.fori_loop(0, size_x // 8, back, 0, unroll=2)
+
+
+def after(value, *others):
+    return lax.optimization_barrier((value,) + others)[0]
 
 
 def body(control, diffusivity, perturb, vertical_filter, sub_widths, obs_raw, obs_counts, obs_rinv):
@@ -274,10 +280,6 @@
     half = part // 2
     n_mem = lax.axis_size("mem")
     me = lax.axis_index("lev")
-    mem = lax.axis_index("mem")
-    core = mem % 2
-    starts = (jnp.cumsum(sub_widths) - sub_widths).astype(jnp.int32)
-    info = jnp.stack([me, core]).astype(jnp.int32)
     smem = pl.BlockSpec(memory_space=pltpu.SMEM)
     params = pltpu.CompilerParams(vmem_limit_bytes=56 << 20)
     flat_width = columns + capacity + LANES
@@ -288,7 +290,6 @@
         functools.partial(forward_kernel, size_x, size_y, groups, capacity),
         grid=(steps,),
         in_specs=[
-            smem,
             smem,
             pl.BlockSpec((1, GROUP, size_x, size_y), lambda g: (0, g, 0, 0)),
             pl.BlockSpec((GROUP, size_x, size_y), lambda g: (g, 0, 0)),
@@ -302,26 +303,29 @@
         + [pltpu.VMEM((size_x, GROUP, size_y), F32)] * 5,
         compiler_params=params,
         name="smooth_and_cut",
-    )(starts, info, control, diffusivity)
+    )(sub_widths, control, diffusivity)
     diff = results[0]
-    outgoing = results[1:]
+    outgoing = [results[1 + c * groups : 1 + (c + 1) * groups] for c in range(PARTS)]
 
     width = sub_widths[me]
     live = jnp.arange(obs_cap, dtype=jnp.int32) < obs_counts[me]
     slots = jnp.where(live, obs_raw[0] % width, -1)[None, :]
-    order = jnp.bitwise_xor(me, jnp.arange(groups))
+    turns = turns_of(groups)
+    order = jnp.bitwise_xor(me, jnp.array(turns, jnp.int32))
     vfilter = vertical_filter.reshape(levels, groups, levels_here)[:, order, :].reshape(levels, levels)
 
+    whole = pl.BlockSpec((levels_here, part), lambda g: (0, 0))
+    square = pl.BlockSpec((levels, levels), lambda g: (0, 0))
+    half_block = pl.BlockSpec((half, levels), lambda g: (0, 0))
+    half_shape = jax.ShapeDtypeStruct((half, levels), F32)
+    cost = pl.CostEstimate(flops=0, bytes_accessed=0, transcendentals=0)
     rows_here = 256
-    adjoint_pieces = []
-    for c in range(PARTS):
-        row0 = c * part + core * half
-        w_info = jnp.stack([me, core, row0]).astype(jnp.int32)
-        obs_weight = pl.pallas_call(
-            functools.partial(observation_kernel, rows_here, obs_cap),
+
+    def weights(c, slots):
+        return pl.pallas_call(
+            functools.partial(observation_kernel, part, c, obs_cap),
             grid=(half // rows_here,),
             in_specs=[
-                smem,
                 pl.BlockSpec((1, obs_cap), lambda g: (0, 0)),
                 pl.BlockSpec((1, obs_cap, levels), lambda g: (0, 0, 0)),
             ],
@@ -329,59 +333,71 @@
             out_shape=jax.ShapeDtypeStruct((half, levels), F32),
             scratch_shapes=[pltpu.VMEM((obs_cap, 2 * levels), BF16)],
             compiler_params=params,
-            cost_estimate=pl.CostEstimate(
-                flops=4 * half * obs_cap * levels, bytes_accessed=4 * obs_cap * levels, transcendentals=0
-            ),
+            cost_estimate=cost,
             name="observation_weights",
-        )(w_info, slots, obs_rinv)
-
-        pieces = [outgoing[c * groups]]
-        for d in range(1, groups):
-            pieces.append(lax.ppermute(outgoing[c * groups + d], "lev", flip_pairs(groups, d)))
-        whole = pl.BlockSpec((levels_here, part), lambda g: (0, 0))
-        chunk = pl.BlockSpec((1, part, levels), lambda g, c=c: (0, c, 0))
-        square = pl.BlockSpec((levels, levels), lambda g: (0, 0))
-        half_block = pl.BlockSpec((half, levels), lambda g: (0, 0))
-        half_shape = jax.ShapeDtypeStruct((half, levels), F32)
-        cost = pl.CostEstimate(
-            flops=6 * part * levels * levels, bytes_accessed=12 * part * levels, transcendentals=0
-        )
-        keep, send = pl.pallas_call(
+        )(slots, obs_rinv)
+
+    def filter_forward(c, vfilter, pieces):
+        chunk = pl.BlockSpec((1, part, levels), lambda g: (0, c, 0))
+        return pl.pallas_call(
             functools.partial(filter_kernel, groups),
             grid=(1,),
-            in_specs=[smem, square, chunk] + [whole] * groups,
+            in_specs=[square, chunk] + [whole] * groups,
             out_specs=[half_block, half_block],
             out_shape=[half_shape, half_shape],
             compiler_params=params,
             cost_estimate=cost,
             name="filter_forward",
-        )(info, vfilter, perturb, *pieces)
-        total = keep + lax.ppermute(send, "mem", flip_pairs(n_mem, 1))
-        bit = 2
-        while bit < n_mem:
-            total = total + lax.ppermute(total, "mem", flip_pairs(n_mem, bit))
-            bit *= 2
-        adj_mine = total * obs_weight
-        adj_other = lax.ppermute(adj_mine, "mem", flip_pairs(n_mem, 1))
-        back = pl.pallas_call(
+        )(vfilter, perturb, *pieces)
+
+    def filter_backward(c, adj_mine, adj_other):
+        chunk = pl.BlockSpec((1, part, levels), lambda g: (0, c, 0))
+        return pl.pallas_call(
             functools.partial(back_kernel, groups),
             grid=(1,),
-            in_specs=[smem, square, chunk, half_block, half_block],
+            in_specs=[square, chunk, half_block, half_block],
             out_specs=[whole] * groups,
             out_shape=[piece_shape] * groups,
             compiler_params=params,
             cost_estimate=cost,
             name="filter_backward",
-        )(info, vfilter, perturb, adj_mine, adj_other)
-        adjoint_pieces.append(back[0])
-        for d in range(1, groups):
-            adjoint_pieces.append(lax.ppermute(back[d], "lev", flip_pairs(groups, d)))
+        )(vfilter, perturb, adj_mine, adj_other)
+
+    def exchange(pieces):
+        return [pieces[0]] + [lax.ppermute(pieces[d], "lev", flip_pairs(groups, turns[d])) for d in range(1, groups)]
+
+    def sum_members(keep, send, gate):
+        total = keep + lax.ppermute(send, "mem", flip_pairs(n_mem, 1))
+        bit = 2
+        while bit < n_mem:
+            other = lax.ppermute(total, "mem", flip_pairs(n_mem, bit))
+            total = total + (after(other, *gate) if gate else other)
+            bit *= 2
+        return total
+
+    def adjoint(total, obs_weight):
+        mine = total * obs_weight
+        return mine, lax.ppermute(mine, "mem", flip_pairs(n_mem, 1))
+
+    got = [exchange(outgoing[c]) for c in range(PARTS)]
+    slots = after(slots, got[0][1])
+    weight = [weights(c, slots) for c in range(PARTS)]
+    back = []
+    gate_filter = []
+    gate_sum = []
+    for c in range(PARTS):
+        gated = after(vfilter, *gate_filter) if gate_filter else vfilter
+        keep, send = filter_forward(c, gated, got[c])
+        mine, other = adjoint(sum_members(keep, send, gate_sum), weight[c])
+        gate_filter = [mine] + weight
+        pieces = exchange(filter_backward(c, mine, other))
+        gate_sum = [pieces[3]]
+        back += pieces
 
     return pl.pallas_call(
         functools.partial(backward_kernel, size_x, size_y, groups, capacity),
         grid=(steps,),
         in_specs=[
-            smem,
             smem,
             pl.BlockSpec((size_x, GROUP, size_y), lambda g: (0, g, 0)),
         ]
@@ -396,7 +412,7 @@
         + [pltpu.SemaphoreType.DMA((groups * PARTS,))],
         compiler_params=params,
         name="place_and_smooth",
-    )(starts, info, diff, *adjoint_pieces)
+    )(sub_widths, diff, *back)
 
 
 def solution(mesh):

time: 263 us -> 222 us (0.84)
  starting transfers between devices: 88.8 us -> 54.6 us
  Pallas kernels: 103 us -> 74.3 us
  waiting for transfers between devices: 53.1 us -> 78.4 us
    ppermute x51 -> x34, starting transfers between devices: 88.8 us -> 54.6 us  [the longest x28 51.9 us: exchange(): lax.ppermute(pieces[d], 'lev', flip_pairs(groups, turns[d]))]
    pallas_call x9 -> x6, Pallas kernels: 67.5 us -> 37.6 us  [the longest x2 18.4 us: weights(): pl.pallas_call(functools.partial(observation_kernel, part, c, obs_cap), g...]
    ppermute x51 -> x34, waiting for transfers between devices: 53.1 us -> 78.4 us  [the longest x28 71.5 us: exchange(): lax.ppermute(pieces[d], 'lev', flip_pairs(groups, turns[d]))]
    another operation x5 -> x0, other arithmetic: 3.3 us -> none  [the longest x3 1.89 us: body(): w_info = jnp.stack([me, core, row0]).astype(jnp.int32)]
  transfers between devices with their start and end apart: 51 -> 34, of which waited for: 9 -> 17; matrix products, arithmetic and copies ran while one was open for 3% -> 4% of each run, Pallas kernels for 26% -> 13%
where the time goes in v3:
time: 222 us; the launch traced here: 221 us
  waiting for transfers between devices  78.4 us (35%)
  Pallas kernels  74.3 us (33%)
  starting transfers between devices  54.6 us (25%)
  local copies, waits for them, and re-layouts  6.47 us (3%)
  other arithmetic  5.84 us (3%)
    ppermute x28, waiting for transfers between devices, exchange(): lax.ppermute(pieces[d], 'lev', flip_pairs(groups, turns[d]))  71.5 us
    ppermute x28, starting transfers between devices, exchange(): lax.ppermute(pieces[d], 'lev', flip_pairs(groups, turns[d]))  51.9 us
    pallas_call x1, Pallas kernels, body(): pl.pallas_call(functools.partial(backward_kernel, size_x, size_y, groups,...  21 us
    pallas_call x2, Pallas kernels, weights(): pl.pallas_call(functools.partial(observation_kernel, part, c, obs_cap), g...  18.4 us
    pallas_call x1, Pallas kernels, body(): pl.pallas_call(functools.partial(forward_kernel, size_x, size_y, groups,...  15.7 us
    pallas_call x2, Pallas kernels, filter_forward(): pl.pallas_call(functools.partial(filter_kernel, groups), grid=(1,), in_sp...  9.62 us
    pallas_call x2, Pallas kernels, filter_backward(): pl.pallas_call(functools.partial(back_kernel, groups), grid=(1,), in_spec...  9.6 us
    ppermute x2, waiting for transfers between devices, sum_members(): other = lax.ppermute(total, 'mem', flip_pairs(n_mem, bit))  4.48 us
  transfers between devices with their start and end apart: 34, of which 17 were waited for; matrix products, arithmetic and copies ran while one was open for 4% of the time, Pallas kernels for 13%

profile of v3, /device:TPU:0, one launch (start us, length us, event | category | flops | bytes accessed | tf_op | source)
XLA Modules:
  0.0 221.3 jit_solution(11547955900045366588)
XLA Ops:
  0.0 15.7 %smooth_and_cut.1 = (f32[128,16,256]{2,1,0:T(8,128)}, f32[16,3072]{1,0:T(8,128)}, f32[16,3072]{1,0:T(8,128)}, f32[16,3072]{1,0:T(8,128)}, f32[16,3072]{1,0:T(8,1...) custom-call(s32[8]{0:T(128)} %widths.3, ...), custom_call_target="tpu_custom_call" | custom-call | tf_op jit(solution)/shard_map/smooth_and_cut/pallas_call | solution.py:289
  15.7 4.1 %collective-permute-start = (f32[16,3072]{1,0:T(8,128)}, f32[16,3072]{1,0:T(8,128)S(1)}, u32[]{:S(2)}, u32[]{:S(2)}) collective-permute-start(f32[16,3072]{1,0:T(8,128)} %get-tuple-element.47), channel_id=1, source_target_pairs={{0,4},{1,5},{2,6},{3,7},{4,0},{5,1},{6,2},{7,3},{8,12},{9,13},{10,... | collective-permute-start | bytes 589832 | tf_op jit(solution)/shard_map/ppermute | solution.py:367
  21.1 3.6 %collective-permute-start.2 = (f32[16,3072]{1,0:T(8,128)}, f32[16,3072]{1,0:T(8,128)S(1)}, u32[]{:S(2)}, u32[]{:S(2)}) collective-permute-start(f32[16,3072]{1,0:T(8,128)} %get-tuple-element.49), channel_id=1, source_target_pairs={{0,6},{1,7},{2,4},{3,5},{4,2},{5,3},{6,0},{7,1},{8,14},{9,15},{10,... | collective-permute-start | bytes 589832 | tf_op jit(solution)/shard_map/ppermute | solution.py:367
  25.6 17.1 %collective-permute-done.rest_1_ = f32[16,3072]{1,0:T(8,128)S(1)} collective-permute-done((f32[16,3072]{1,0:T(8,128)}, f32[16,3072]{1,0:T(8,128)S(1)}, u32[]{:S(2)}, u32[]{:S(2)}) %collective-permute-start) | collective-permute-done | bytes 196640 | tf_op jit(solution)/shard_map/ppermute | solution.py:367
  42.8 5.4 %collective-permute-done.1.rest_2_ = f32[16,3072]{1,0:T(8,128)S(1)} collective-permute-done((f32[16,3072]{1,0:T(8,128)}, f32[16,3072]{1,0:T(8,128)S(1)}, u32[]{:S(2)}, u32[]{:S(2)}) %collective-permute-start.1) | collective-permute-done | bytes 196640 | tf_op jit(solution)/shard_map/ppermute | solution.py:367
  54.8 4.8 %filter_forward.2 = (f32[1536,128]{1,0:T(8,128)}, f32[1536,128]{1,0:T(8,128)}) custom-call(f32[128,128]{1,0:T(8,128)} %copy.12.vfilter, f32[1,6144,128]{2,1,0:T(8,128)} %perturb.7, f32[16,3072]{1,0:T(8,128)} %get-tuple-element.46.rest_0_, f32[16,3072]{1,0:T(8,128)} %copy-done.10, f32[16,3072]{1,0:T(8,128)} %copy-done.11, f32[16,3072]{1,0:T(8,128)} %copy-done.12, ...), custom_call_target="tpu_custom_call" | custom-call | tf_op jit(solution)/shard_map/filter_forward/pallas_call | solution.py:342
  59.7 4.3 %collective-permute-start.17 = (f32[16,3072]{1,0:T(8,128)S(1)}, f32[16,3072]{1,0:T(8,128)S(1)}, u32[]{:S(2)}, u32[]{:S(2)}) collective-permute-start(f32[16,3072]{1,0:T(8,128)S(1)} %copy-done.43), channel_id=1, source_target_pairs={{0,4},{1,5},{2,6},{3,7},{4,0},{5,1},{6,2},{7,3},{8,12},{9,13},{10,... | collective-permute-start | bytes 589832 | tf_op jit(solution)/shard_map/ppermute | solution.py:367
  64.0 3.2 %collective-permute-start.19 = (f32[16,3072]{1,0:T(8,128)S(1)}, f32[16,3072]{1,0:T(8,128)S(1)}, u32[]{:S(2)}, u32[]{:S(2)}) collective-permute-start(f32[16,3072]{1,0:T(8,128)S(1)} %copy-done.41), channel_id=1, source_target_pairs={{0,6},{1,7},{2,4},{3,5},{4,2},{5,3},{6,0},{7,1},{8,14},{9,15},{10,... | collective-permute-start | bytes 589832 | tf_op jit(solution)/shard_map/ppermute | solution.py:367
  74.1 3.2 %compare_select_fusion.slots = s32[1,6144]{1,0:T(1,128)} fusion(pred[]{:T(512)S(6)} %lt.34, s32[1,6144]{1,0:T(1,128)S(1)} %copy-done.35, s32[]{:T(128)S(6)} %select_n.24, s32[]{:T(128)} %bitcast.3), kind=kLoop, calls=%fused_computation.4 | loop fusion | flops 55296 | bytes 49161 | tf_op jit(solution)/shard_map/jit(_where)/select_n | solution.py:312
  77.3 9.1 %observation_weights.2 = f32[1536,128]{1,0:T(8,128)} custom-call(s32[1,6144]{1,0:T(1,128)} %compare_select_fusion.slots, f32[1,6144,128]{2,1,0:T(8,128)} %rinv.3), custom_call_target="tpu_custom_call" | custom-call | tf_op jit(solution)/shard_map/observation_weights/pallas_call | solution.py:325
  86.4 9.2 %observation_weights.3 = f32[1536,128]{1,0:T(8,128)} custom-call(s32[1,6144]{1,0:T(1,128)} %compare_select_fusion.slots, f32[1,6144,128]{2,1,0:T(8,128)} %rinv.3), custom_call_target="tpu_custom_call" | custom-call | tf_op jit(solution)/shard_map/observation_weights/pallas_call | solution.py:325
  100.3 4.2 %collective-permute-done.21.rest_5_ = f32[16,3072]{1,0:T(8,128)S(1)} collective-permute-done((f32[16,3072]{1,0:T(8,128)S(1)}, f32[16,3072]{1,0:T(8,128)S(1)}, u32[]{:S(2)}, u32[]{:S(2)}) %collective-permute-start.21) | collective-permute-done | bytes 196640 | tf_op jit(solution)/shard_map/ppermute | solution.py:367
  107.6 4.8 %filter_forward.3 = (f32[1536,128]{1,0:T(8,128)}, f32[1536,128]{1,0:T(8,128)}) custom-call(f32[128,128]{1,0:T(8,128)} %copy.13.vfilter, f32[1,6144,128]{2,1,0:T(8,128)} %perturb.7, f32[16,3072]{1,0:T(8,128)} %get-tuple-element.66.rest_0_, f32[16,3072]{1,0:T(8,128)} %copy-done.6, f32[16,3072]{1,0:T(8,128)} %copy-done.7, f32[16,3072]{1,0:T(8,128)} %copy-done.8, ...), custom_call_target="tpu_custom_call" | custom-call | tf_op jit(solution)/shard_map/filter_forward/pallas_call | solution.py:342
  118.0 4.8 %filter_backward.2 = (f32[16,3072]{1,0:T(8,128)}, f32[16,3072]{1,0:T(8,128)}, f32[16,3072]{1,0:T(8,128)}, f32[16,3072]{1,0:T(8,128)}, f32[16,3072]{1,0:T(8,128)}...) custom-call(f32[128,128]{1,0:T(8,128)} %copy.12.vfilter, f32[1,6144,128]{2,1,0:T(8,128)} %perturb.7, ...), custom_call_target="tpu_custom_call" | custom-call | tf_op jit(solution)/shard_map/filter_backward/pallas_call | solution.py:355
  125.3 6.4 %collective-permute-done.12.rest_3_ = f32[16,3072]{1,0:T(8,128)S(1)} collective-permute-done((f32[16,3072]{1,0:T(8,128)}, f32[16,3072]{1,0:T(8,128)S(1)}, u32[]{:S(2)}, u32[]{:S(2)}) %collective-permute-start.12) | collective-permute-done | bytes 196640 | tf_op jit(solution)/shard_map/ppermute | solution.py:367
  131.7 4.5 %collective-permute-done.25 = f32[1536,128]{1,0:T(8,128)S(1)} collective-permute-done((f32[1536,128]{1,0:T(8,128)S(1)}, f32[1536,128]{1,0:T(8,128)S(1)}, u32[]{:S(2)}, u32[]{:S(2)}) %collective-permute-start.25) | collective-permute-done | bytes 786464 | tf_op jit(solution)/shard_map/ppermute | solution.py:373
  145.6 4.8 %filter_backward.3 = (f32[16,3072]{1,0:T(8,128)}, f32[16,3072]{1,0:T(8,128)}, f32[16,3072]{1,0:T(8,128)}, f32[16,3072]{1,0:T(8,128)}, f32[16,3072]{1,0:T(8,128)}...) custom-call(f32[128,128]{1,0:T(8,128)} %copy.12.vfilter, f32[1,6144,128]{2,1,0:T(8,128)} %perturb.7, ...), custom_call_target="tpu_custom_call" | custom-call | tf_op jit(solution)/shard_map/filter_backward/pallas_call | solution.py:355
  150.4 7.4 %collective-permute-done.10.rest_1_ = f32[16,3072]{1,0:T(8,128)S(1)} collective-permute-done((f32[16,3072]{1,0:T(8,128)S(1)}, f32[16,3072]{1,0:T(8,128)S(1)}, u32[]{:S(2)}, u32[]{:S(2)}) %collective-permute-start.10) | collective-permute-done | bytes 196640 | tf_op jit(solution)/shard_map/ppermute | solution.py:367
  158.5 3.6 %collective-permute-done.11.rest_2_ = f32[16,3072]{1,0:T(8,128)S(1)} collective-permute-done((f32[16,3072]{1,0:T(8,128)S(1)}, f32[16,3072]{1,0:T(8,128)S(1)}, u32[]{:S(2)}, u32[]{:S(2)}) %collective-permute-start.11) | collective-permute-done | bytes 196640 | tf_op jit(solution)/shard_map/ppermute | solution.py:367
  162.1 10.7 %collective-permute-start.28 = (f32[16,3072]{1,0:T(8,128)}, f32[16,3072]{1,0:T(8,128)S(1)}, u32[]{:S(2)}, u32[]{:S(2)}) collective-permute-start(f32[16,3072]{1,0:T(8,128)} %get-tuple-element.79), channel_id=1, source_target_pairs={{0,5},{1,4},{2,7},{3,6},{4,1},{5,0},{6,3},{7,2},{8,13},{9,12},{10,... | collective-permute-start | bytes 589832 | tf_op jit(solution)/shard_map/ppermute | solution.py:367
  177.4 8.8 %collective-permute-done.27.rest_9_ = f32[16,3072]{1,0:T(8,128)S(1)} collective-permute-done((f32[16,3072]{1,0:T(8,128)}, f32[16,3072]{1,0:T(8,128)S(1)}, u32[]{:S(2)}, u32[]{:S(2)}) %collective-permute-start.27) | collective-permute-done | bytes 196640 | tf_op jit(solution)/shard_map/ppermute | solution.py:367
  186.3 5.2 %collective-permute-done.28.rest_10_ = f32[16,3072]{1,0:T(8,128)S(1)} collective-permute-done((f32[16,3072]{1,0:T(8,128)}, f32[16,3072]{1,0:T(8,128)S(1)}, u32[]{:S(2)}, u32[]{:S(2)}) %collective-permute-start.28) | collective-permute-done | bytes 196640 | tf_op jit(solution)/shard_map/ppermute | solution.py:367
  195.5 3.3 %collective-permute-done.32.rest_14_ = f32[16,3072]{1,0:T(8,128)S(1)} collective-permute-done((f32[16,3072]{1,0:T(8,128)}, f32[16,3072]{1,0:T(8,128)S(1)}, u32[]{:S(2)}, u32[]{:S(2)}) %collective-permute-start.32) | collective-permute-done | bytes 196640 | tf_op jit(solution)/shard_map/ppermute | solution.py:367
  200.3 21.0 %place_and_smooth.1 = f32[1,16,128,256]{3,2,1,0:T(8,128)} custom-call(s32[8]{0:T(128)} %widths.3, f32[128,16,256]{2,1,0:T(8,128)} %get-tuple-element.45.diff, f32[16,3072]{1,0:T(8,128)} %get-tuple-element.57.rest_0_, f32[16,3072]{1,0:T(8,128)} %copy-done.21, f32[16,3072]{1,0:T(8,128)} %copy-done.22, f32[16,3072]{1,0:T(8,128)} %copy-done.20, ...), custom_call_target="tpu_custom_call" | custom-call | tf_op jit(solution)/shard_map/place_and_smooth/pallas_call | solution.py:397
  (169 shorter events, 50.3 us)
Async XLA Ops:
  15.7 27.0 %collective-permute-start = (f32[16,3072]{1,0:T(8,128)}, f32[16,3072]{1,0:T(8,128)S(1)}, u32[]{:S(2)}, u32[]{:S(2)}) collective-permute-start(f32[16,3072]{1,0:T(8,128)} %get-tuple-element.47), channel_id=1, source_target_pairs={{0,4},{1,5},{2,6},{3,7},{4,0},{5,1},{6,2},{7,3},{8,12},{9,13},{10,... | collective-permute-start | bytes 589832 | tf_op jit(solution)/shard_map/ppermute | solution.py:367
  19.8 28.4 %collective-permute-start.1 = (f32[16,3072]{1,0:T(8,128)}, f32[16,3072]{1,0:T(8,128)S(1)}, u32[]{:S(2)}, u32[]{:S(2)}) collective-permute-start(f32[16,3072]{1,0:T(8,128)} %get-tuple-element.48), channel_id=1, source_target_pairs={{0,5},{1,4},{2,7},{3,6},{4,1},{5,0},{6,3},{7,2},{8,13},{9,12},{10,... | collective-permute-start | bytes 589832 | tf_op jit(solution)/shard_map/ppermute | solution.py:367
  21.1 28.6 %collective-permute-start.2 = (f32[16,3072]{1,0:T(8,128)}, f32[16,3072]{1,0:T(8,128)S(1)}, u32[]{:S(2)}, u32[]{:S(2)}) collective-permute-start(f32[16,3072]{1,0:T(8,128)} %get-tuple-element.49), channel_id=1, source_target_pairs={{0,6},{1,7},{2,4},{3,5},{4,2},{5,3},{6,0},{7,1},{8,14},{9,15},{10,... | collective-permute-start | bytes 589832 | tf_op jit(solution)/shard_map/ppermute | solution.py:367
  24.7 25.0 %collective-permute-start.3 = (f32[16,3072]{1,0:T(8,128)}, f32[16,3072]{1,0:T(8,128)S(1)}, u32[]{:S(2)}, u32[]{:S(2)}) collective-permute-start(f32[16,3072]{1,0:T(8,128)} %get-tuple-element.50), channel_id=1, source_target_pairs={{0,7},{1,6},{2,5},{3,4},{4,3},{5,2},{6,1},{7,0},{8,15},{9,14},{10,... | collective-permute-start | bytes 589832 | tf_op jit(solution)/shard_map/ppermute | solution.py:367
  24.7 25.1 %collective-permute-start.4 = (f32[16,3072]{1,0:T(8,128)}, f32[16,3072]{1,0:T(8,128)S(1)}, u32[]{:S(2)}, u32[]{:S(2)}) collective-permute-start(f32[16,3072]{1,0:T(8,128)} %get-tuple-element.51), channel_id=1, source_target_pairs={{0,3},{1,2},{2,1},{3,0},{4,7},{5,6},{6,5},{7,4},{8,11},{9,10},{10,... | collective-permute-start | bytes 589832 | tf_op jit(solution)/shard_map/ppermute | solution.py:367
  59.6 11.7 %collective-permute-start.7 = (f32[1536,128]{1,0:T(8,128)}, f32[1536,128]{1,0:T(8,128)S(1)}, u32[]{:S(2)}, u32[]{:S(2)}) collective-permute-start(f32[1536,128]{1,0:T(8,128)} %get-tuple-element.55), channel_id=1, source_target_pairs={{0,8},{8,0},{16,24},{24,16},{1,9},{9,1},{17,25},{25,17},{2,10},{10... | collective-permute-start | bytes 2359304 | tf_op jit(solution)/shard_map/ppermute | solution.py:370
  59.7 36.0 %collective-permute-start.17 = (f32[16,3072]{1,0:T(8,128)S(1)}, f32[16,3072]{1,0:T(8,128)S(1)}, u32[]{:S(2)}, u32[]{:S(2)}) collective-permute-start(f32[16,3072]{1,0:T(8,128)S(1)} %copy-done.43), channel_id=1, source_target_pairs={{0,4},{1,5},{2,6},{3,7},{4,0},{5,1},{6,2},{7,3},{8,12},{9,13},{10,... | collective-permute-start | bytes 589832 | tf_op jit(solution)/shard_map/ppermute | solution.py:367
  63.9 33.6 %collective-permute-start.18 = (f32[16,3072]{1,0:T(8,128)S(1)}, f32[16,3072]{1,0:T(8,128)S(1)}, u32[]{:S(2)}, u32[]{:S(2)}) collective-permute-start(f32[16,3072]{1,0:T(8,128)S(1)} %copy-done.42), channel_id=1, source_target_pairs={{0,5},{1,4},{2,7},{3,6},{4,1},{5,0},{6,3},{7,2},{8,13},{9,12},{10,... | collective-permute-start | bytes 589832 | tf_op jit(solution)/shard_map/ppermute | solution.py:367
  64.0 36.3 %collective-permute-start.19 = (f32[16,3072]{1,0:T(8,128)S(1)}, f32[16,3072]{1,0:T(8,128)S(1)}, u32[]{:S(2)}, u32[]{:S(2)}) collective-permute-start(f32[16,3072]{1,0:T(8,128)S(1)} %copy-done.41), channel_id=1, source_target_pairs={{0,6},{1,7},{2,4},{3,5},{4,2},{5,3},{6,0},{7,1},{8,14},{9,15},{10,... | collective-permute-start | bytes 589832 | tf_op jit(solution)/shard_map/ppermute | solution.py:367
  67.2 33.1 %collective-permute-start.20 = (f32[16,3072]{1,0:T(8,128)S(1)}, f32[16,3072]{1,0:T(8,128)S(1)}, u32[]{:S(2)}, u32[]{:S(2)}) collective-permute-start(f32[16,3072]{1,0:T(8,128)S(1)} %copy-done.40), channel_id=1, source_target_pairs={{0,7},{1,6},{2,5},{3,4},{4,3},{5,2},{6,1},{7,0},{8,15},{9,14},{10,... | collective-permute-start | bytes 589832 | tf_op jit(solution)/shard_map/ppermute | solution.py:367
  72.6 25.3 %collective-permute-start.8 = (f32[1536,128]{1,0:T(8,128)S(1)}, f32[1536,128]{1,0:T(8,128)S(1)}, u32[]{:S(2)}, u32[]{:S(2)}) collective-permute-start(f32[1536,128]{1,0:T(8,128)S(1)} %add.27), channel_id=1, source_target_pairs={{0,16},{8,24},{16,0},{24,8},{1,17},{9,25},{17,1},{25,9},{2,18},{10... | collective-permute-start | bytes 2359304 | tf_op jit(solution)/shard_map/ppermute | solution.py:373
  116.5 19.6 %collective-permute-start.25 = (f32[1536,128]{1,0:T(8,128)S(1)}, f32[1536,128]{1,0:T(8,128)S(1)}, u32[]{:S(2)}, u32[]{:S(2)}) collective-permute-start(f32[1536,128]{1,0:T(8,128)S(1)} %add.31), channel_id=1, source_target_pairs={{0,16},{8,24},{16,0},{24,8},{1,17},{9,25},{17,1},{25,9},{2,18},{10... | collective-permute-start | bytes 2359304 | tf_op jit(solution)/shard_map/ppermute | solution.py:373
  136.4 21.4 %collective-permute-start.10 = (f32[16,3072]{1,0:T(8,128)S(1)}, f32[16,3072]{1,0:T(8,128)S(1)}, u32[]{:S(2)}, u32[]{:S(2)}) collective-permute-start(f32[16,3072]{1,0:T(8,128)S(1)} %copy-done.49), channel_id=1, source_target_pairs={{0,4},{1,5},{2,6},{3,7},{4,0},{5,1},{6,2},{7,3},{8,12},{9,13},{10,... | collective-permute-start | bytes 589832 | tf_op jit(solution)/shard_map/ppermute | solution.py:367
  139.1 22.9 %collective-permute-start.11 = (f32[16,3072]{1,0:T(8,128)S(1)}, f32[16,3072]{1,0:T(8,128)S(1)}, u32[]{:S(2)}, u32[]{:S(2)}) collective-permute-start(f32[16,3072]{1,0:T(8,128)S(1)} %copy-done.48), channel_id=1, source_target_pairs={{0,5},{1,4},{2,7},{3,6},{4,1},{5,0},{6,3},{7,2},{8,13},{9,12},{10,... | collective-permute-start | bytes 589832 | tf_op jit(solution)/shard_map/ppermute | solution.py:367
  139.5 22.6 %collective-permute-start.13 = (f32[16,3072]{1,0:T(8,128)S(1)}, f32[16,3072]{1,0:T(8,128)S(1)}, u32[]{:S(2)}, u32[]{:S(2)}) collective-permute-start(f32[16,3072]{1,0:T(8,128)S(1)} %copy-done.47), channel_id=1, source_target_pairs={{0,7},{1,6},{2,5},{3,4},{4,3},{5,2},{6,1},{7,0},{8,15},{9,14},{10,... | collective-permute-start | bytes 589832 | tf_op jit(solution)/shard_map/ppermute | solution.py:367
  142.7 30.1 %collective-permute-start.14 = (f32[16,3072]{1,0:T(8,128)S(1)}, f32[16,3072]{1,0:T(8,128)S(1)}, u32[]{:S(2)}, u32[]{:S(2)}) collective-permute-start(f32[16,3072]{1,0:T(8,128)S(1)} %copy-done.46), channel_id=1, source_target_pairs={{0,3},{1,2},{2,1},{3,0},{4,7},{5,6},{6,5},{7,4},{8,11},{9,10},{10,... | collective-permute-start | bytes 589832 | tf_op jit(solution)/shard_map/ppermute | solution.py:367
  143.7 30.6 %collective-permute-start.15 = (f32[16,3072]{1,0:T(8,128)S(1)}, f32[16,3072]{1,0:T(8,128)S(1)}, u32[]{:S(2)}, u32[]{:S(2)}) collective-permute-start(f32[16,3072]{1,0:T(8,128)S(1)} %copy-done.45), channel_id=1, source_target_pairs={{0,2},{1,3},{2,0},{3,1},{4,6},{5,7},{6,4},{7,5},{8,10},{9,11},{10,... | collective-permute-start | bytes 589832 | tf_op jit(solution)/shard_map/ppermute | solution.py:367
  157.8 19.6 %collective-permute-start.16 = (f32[16,3072]{1,0:T(8,128)S(1)}, f32[16,3072]{1,0:T(8,128)S(1)}, u32[]{:S(2)}, u32[]{:S(2)}) collective-permute-start(f32[16,3072]{1,0:T(8,128)S(1)} %copy-done.44), channel_id=1, source_target_pairs={{0,1},{1,0},{2,3},{3,2},{4,5},{5,4},{6,7},{7,6},{8,9},{9,8},{10,11... | collective-permute-start | bytes 589832 | tf_op jit(solution)/shard_map/ppermute | solution.py:367
  162.1 24.2 %collective-permute-start.27 = (f32[16,3072]{1,0:T(8,128)}, f32[16,3072]{1,0:T(8,128)S(1)}, u32[]{:S(2)}, u32[]{:S(2)}) collective-permute-start(f32[16,3072]{1,0:T(8,128)} %get-tuple-element.78), channel_id=1, source_target_pairs={{0,4},{1,5},{2,6},{3,7},{4,0},{5,1},{6,2},{7,3},{8,12},{9,13},{10,... | collective-permute-start | bytes 589832 | tf_op jit(solution)/shard_map/ppermute | solution.py:367
  162.1 29.4 %collective-permute-start.28 = (f32[16,3072]{1,0:T(8,128)}, f32[16,3072]{1,0:T(8,128)S(1)}, u32[]{:S(2)}, u32[]{:S(2)}) collective-permute-start(f32[16,3072]{1,0:T(8,128)} %get-tuple-element.79), channel_id=1, source_target_pairs={{0,5},{1,4},{2,7},{3,6},{4,1},{5,0},{6,3},{7,2},{8,13},{9,12},{10,... | collective-permute-start | bytes 589832 | tf_op jit(solution)/shard_map/ppermute | solution.py:367
  172.8 20.2 %collective-permute-start.29 = (f32[16,3072]{1,0:T(8,128)}, f32[16,3072]{1,0:T(8,128)S(1)}, u32[]{:S(2)}, u32[]{:S(2)}) collective-permute-start(f32[16,3072]{1,0:T(8,128)} %get-tuple-element.80), channel_id=1, source_target_pairs={{0,6},{1,7},{2,4},{3,5},{4,2},{5,3},{6,0},{7,1},{8,14},{9,15},{10,... | collective-permute-start | bytes 589832 | tf_op jit(solution)/shard_map/ppermute | solution.py:367
  174.3 18.7 %collective-permute-start.30 = (f32[16,3072]{1,0:T(8,128)}, f32[16,3072]{1,0:T(8,128)S(1)}, u32[]{:S(2)}, u32[]{:S(2)}) collective-permute-start(f32[16,3072]{1,0:T(8,128)} %get-tuple-element.81), channel_id=1, source_target_pairs={{0,7},{1,6},{2,5},{3,4},{4,3},{5,2},{6,1},{7,0},{8,15},{9,14},{10,... | collective-permute-start | bytes 589832 | tf_op jit(solution)/shard_map/ppermute | solution.py:367
  177.4 18.1 %collective-permute-start.31 = (f32[16,3072]{1,0:T(8,128)}, f32[16,3072]{1,0:T(8,128)S(1)}, u32[]{:S(2)}, u32[]{:S(2)}) collective-permute-start(f32[16,3072]{1,0:T(8,128)} %get-tuple-element.82), channel_id=1, source_target_pairs={{0,3},{1,2},{2,1},{3,0},{4,7},{5,6},{6,5},{7,4},{8,11},{9,10},{10,... | collective-permute-start | bytes 589832 | tf_op jit(solution)/shard_map/ppermute | solution.py:367
  186.3 12.5 %collective-permute-start.32 = (f32[16,3072]{1,0:T(8,128)}, f32[16,3072]{1,0:T(8,128)S(1)}, u32[]{:S(2)}, u32[]{:S(2)}) collective-permute-start(f32[16,3072]{1,0:T(8,128)} %get-tuple-element.83), channel_id=1, source_target_pairs={{0,2},{1,3},{2,0},{3,1},{4,6},{5,7},{6,4},{7,5},{8,10},{9,11},{10,... | collective-permute-start | bytes 589832 | tf_op jit(solution)/shard_map/ppermute | solution.py:367
  (62 other events, 762.9 us)

commit v4 on v3

--- a/solution.py
+++ b/solution.py
@@ -95,8 +95,8 @@
 
 
 def forward_kernel(size_x, size_y, groups, capacity, widths, control, diffusivity, diff_out, *rest):
-    outs = rest[: groups * PARTS]
-    flat, one, two, *face_refs = rest[groups * PARTS :]
+    outs = rest[:PARTS]
+    flat, one, two, *face_refs = rest[PARTS:]
     columns = size_x * size_y
     part = capacity // PARTS
     transpose_in(diffusivity, diff_out, size_x)
@@ -108,16 +108,15 @@
     flat[:, columns:] = jnp.zeros((GROUP, flat.shape[1] - columns), F32)
 
     lane = lax.broadcasted_iota(jnp.int32, (GROUP, LANES), 1)
-    me = lax.axis_index("lev")
     tiles = part // LANES
-    for d, turn in enumerate(turns_of(groups)):
-        start = start_of(widths, jnp.bitwise_xor(me, turn))
+    for j in range(groups):
+        start = start_of(widths, j)
         base = start // LANES
         shift = start - base * LANES
         back = lax.rem(LANES - shift, LANES)
         low = lane < LANES - shift
         for c in range(PARTS):
-            out = outs[c * groups + d]
+            out = outs[c]
             begin = base + c * tiles
 
             def load(t):
@@ -127,24 +126,13 @@
             now = load(0)
             for t in range(tiles):
                 later = load(t + 1)
-                out[:, t * LANES : (t + 1) * LANES] = jnp.where(low, now, later)
+                out[j, :, t * LANES : (t + 1) * LANES] = jnp.where(low, now, later)
                 now = later
-
-
-def turns_of(groups):
-    return [0] + list(range(groups // 2, groups)) + list(range(groups // 2 - 1, 0, -1))
 
 
 def split2(value):
     high = value.astype(BF16)
     return high, (value - high.astype(F32)).astype(BF16)
-
-
-def dot3(a, b, dims):
-    ah, al = split2(a)
-    bh, bl = split2(b)
-    dot = functools.partial(lax.dot_general, dimension_numbers=(dims, ((), ())), preferred_element_type=F32)
-    return dot(ah, bh) + (dot(ah, bl) + dot(al, bh))
 
 
 def observation_kernel(part_rows, index, obs_cap, slots, rinv, out, split):
@@ -165,61 +153,65 @@
     out[...] = total[:, :levels] + total[:, levels:]
 
 
-def filter_kernel(groups, vfilter, perturb, *rest):
-    pieces = rest[:groups]
-    keep, send = rest[groups:]
-    half = keep.shape[0]
-    width = 256
-    mine = lax.axis_index("mem") % 2
-    for which, out in ((mine, keep), (1 - mine, send)):
-
-        def step(b, _):
-            at = pl.multiple_of(which * half + b * width, width)
-            slab = jnp.concatenate([piece[:, pl.ds(at, width)] for piece in pieces], axis=0)
-            filtered = dot3(slab.T, vfilter[...], ((1,), (1,)))
-            out[pl.ds(pl.multiple_of(b * width, width), width), :] = (
-                perturb[0, pl.ds(at, width), :] * filtered
-            )
-            return 0
-
-        lax.fori_loop(0, half // width, step, 0, unroll=2)
-
-
-def back_kernel(groups, vfilter, perturb, adj_mine, adj_other, *pieces):
-    half = adj_mine.shape[0]
-    width = 256
-    levels = pieces[0].shape[0]
-    mine = lax.axis_index("mem") % 2
-    for which, adj in ((mine, adj_mine), (1 - mine, adj_other)):
-
-        def step(b, _):
-            at = pl.multiple_of(which * half + b * width, width)
-            weighted = perturb[0, pl.ds(at, width), :] * adj[pl.ds(pl.multiple_of(b * width, width), width), :]
-            result = dot3(vfilter[...], weighted, ((0,), (1,)))
-            for d in range(groups):
-                pieces[d][:, pl.ds(at, width)] = result[d * levels : (d + 1) * levels]
-            return 0
-
-        lax.fori_loop(0, half // width, step, 0, unroll=2)
+def filter_kernel(core, vfilter, perturb, pieces, keep, send, table):
+    levels = vfilter.shape[0]
+    rows = keep.shape[0]
+    step = pl.program_id(0)
+    blocks = pl.num_programs(0) // 2
+
+    @pl.when(step == 0)
+    def _():
+        high, low = split2(vfilter[...].T)
+        table[:levels, :levels] = high
+        table[levels:, :levels] = high
+        table[:levels, levels:] = low
+        table[levels:, levels:] = jnp.zeros_like(low)
+
+    slab = pieces[...].reshape(levels, rows)
+    both = jnp.concatenate(split2(slab.T), axis=1)
+    products = jnp.dot(both, table[...], preferred_element_type=F32)
+    result = perturb[0] * (products[:, :levels] + products[:, levels:])
+
+    @pl.when(step < blocks)
+    def _():
+        keep[...] = result
+
+    @pl.when(step >= blocks)
+    def _():
+        send[...] = result
+
+
+def back_kernel(core, vfilter, perturb, adj_mine, adj_other, pieces, table):
+    levels = vfilter.shape[0]
+    step = pl.program_id(0)
+    blocks = pl.num_programs(0) // 2
+
+    @pl.when(step == 0)
+    def _():
+        high, low = split2(vfilter[...])
+        table[:levels, :levels] = high
+        table[levels:, :levels] = high
+        table[:levels, levels:] = low
+        table[levels:, levels:] = jnp.zeros_like(low)
+
+    adj = jnp.where(step < blocks, adj_mine[...], adj_other[...])
+    both = jnp.concatenate(split2(perturb[0] * adj), axis=1)
+    products = jnp.dot(both, table[...], preferred_element_type=F32)
+    result = (products[:, :levels] + products[:, levels:]).T
+    pieces[...] = result.reshape(pieces.shape)
 
 
 def backward_kernel(size_x, size_y, groups, capacity, widths, diff, *rest):
-    ins = rest[: groups * PARTS]
-    out, staging, flat, one, two, *face_refs, sem = rest[groups * PARTS :]
+    ins = rest[:PARTS]
+    out, staging, flat, one, two, *face_refs, sem = rest[PARTS:]
     part = capacity // PARTS
-    me = lax.axis_index("lev")
-    step_id = pl.program_id(0)
-    level = pl.multiple_of(step_id * GROUP, GROUP)
-    copies = []
-    for c in range(PARTS):
-        for d, turn in enumerate(turns_of(groups)):
-            copies.append(
-                pltpu.make_async_copy(
-                    ins[c * groups + d].at[pl.ds(level, GROUP), :],
-                    staging.at[jnp.bitwise_xor(me, turn), :, pl.ds(c * part, part)],
-                    sem.at[c * groups + d],
-                )
-            )
+    level = pl.multiple_of(pl.program_id(0) * GROUP, GROUP)
+    copies = [
+        pltpu.make_async_copy(
+            ins[c].at[:, pl.ds(level, GROUP), :], staging.at[:, :, pl.ds(c * part, part)], sem.at[c]
+        )
+        for c in range(PARTS)
+    ]
     for copy in copies:
         copy.start()
     faces(diff, *face_refs, size_x, size_y)
@@ -228,7 +220,6 @@
 
     lane = lax.broadcasted_iota(jnp.int32, (GROUP, LANES), 1)
     tiles = capacity // LANES
-    some = 8
 
     def place(j, _):
         start = start_of(widths, j)
@@ -236,18 +227,13 @@
         shift = start - base * LANES
         high = lane >= shift
 
-        def several(b, before):
-            for t in range(some):
-                at = pl.multiple_of((b * some + t) * LANES, LANES)
-                to = pl.multiple_of((base + b * some + t) * LANES, LANES)
-                here = pltpu.roll(staging[j, :, pl.ds(at, LANES)], shift, 1)
-                flat[:, pl.ds(to, LANES)] = jnp.where(high, here, before)
-                before = here
-            return before
-
-        existing = flat[:, pl.ds(pl.multiple_of(base * LANES, LANES), LANES)]
-        last = lax.fori_loop(0, tiles // some, several, existing)
-        flat[:, pl.ds(pl.multiple_of((base + tiles) * LANES, LANES), LANES)] = last
+        before = flat[:, pl.ds(pl.multiple_of(base * LANES, LANES), LANES)]
+        for t in range(tiles):
+            to = pl.multiple_of((base + t) * LANES, LANES)
+            here = pltpu.roll(staging[j, :, t * LANES : (t + 1) * LANES], shift, 1)
+            flat[:, pl.ds(to, LANES)] = jnp.where(high, here, before)
+            before = here
+        flat[:, pl.ds(pl.multiple_of((base + tiles) * LANES, LANES), LANES)] = before
         return 0
 
     lax.fori_loop(0, groups, place, 0)
@@ -283,7 +269,7 @@
     smem = pl.BlockSpec(memory_space=pltpu.SMEM)
     params = pltpu.CompilerParams(vmem_limit_bytes=56 << 20)
     flat_width = columns + capacity + LANES
-    piece_shape = jax.ShapeDtypeStruct((levels_here, part), F32)
+    pieces_shape = jax.ShapeDtypeStruct((groups, levels_here, part), F32)
     steps = levels_here // GROUP
 
     results = pl.pallas_call(
@@ -295,8 +281,8 @@
             pl.BlockSpec((GROUP, size_x, size_y), lambda g: (g, 0, 0)),
         ],
         out_specs=[pl.BlockSpec((size_x, GROUP, size_y), lambda g: (0, g, 0))]
-        + [pl.BlockSpec((GROUP, part), lambda g: (g, 0))] * (groups * PARTS),
-        out_shape=[jax.ShapeDtypeStruct((size_x, levels_here, size_y), F32)] + [piece_shape] * (groups * PARTS),
+        + [pl.BlockSpec((groups, GROUP, part), lambda g: (0, g, 0))] * PARTS,
+        out_shape=[jax.ShapeDtypeStruct((size_x, levels_here, size_y), F32)] + [pieces_shape] * PARTS,
         scratch_shapes=[
             pltpu.VMEM((GROUP, flat_width), F32),
         ]
@@ -305,19 +291,27 @@
         name="smooth_and_cut",
     )(sub_widths, control, diffusivity)
     diff = results[0]
-    outgoing = [results[1 + c * groups : 1 + (c + 1) * groups] for c in range(PARTS)]
+    outgoing = results[1:]
 
     width = sub_widths[me]
     live = jnp.arange(obs_cap, dtype=jnp.int32) < obs_counts[me]
     slots = jnp.where(live, obs_raw[0] % width, -1)[None, :]
-    turns = turns_of(groups)
-    order = jnp.bitwise_xor(me, jnp.array(turns, jnp.int32))
-    vfilter = vertical_filter.reshape(levels, groups, levels_here)[:, order, :].reshape(levels, levels)
-
-    whole = pl.BlockSpec((levels_here, part), lambda g: (0, 0))
-    square = pl.BlockSpec((levels, levels), lambda g: (0, 0))
-    half_block = pl.BlockSpec((half, levels), lambda g: (0, 0))
+
+    vfilter = vertical_filter
+    width = half
+    blocks = part // width
+    some = blocks // 2
+
+    def block_of(g, core):
+        return (g // some + core[0]) % 2 * some + g % some
+
+    square = pl.BlockSpec((levels, levels), lambda g, core: (0, 0))
+    slab = pl.BlockSpec((groups, levels_here, width), lambda g, core: (0, 0, block_of(g, core)))
+    first_half = pl.BlockSpec((width, levels), lambda g, core: (jnp.minimum(g, some - 1), 0))
+    second_half = pl.BlockSpec((width, levels), lambda g, core: (jnp.maximum(g - some, 0), 0))
     half_shape = jax.ShapeDtypeStruct((half, levels), F32)
+    core = (lax.axis_index("mem") % 2).astype(jnp.int32)[None]
+    table = pltpu.VMEM((2 * levels, 2 * levels), BF16)
     cost = pl.CostEstimate(flops=0, bytes_accessed=0, transcendentals=0)
     rows_here = 256
 
@@ -337,41 +331,49 @@
             name="observation_weights",
         )(slots, obs_rinv)
 
+    def perturb_part(c):
+        return pl.BlockSpec((1, width, levels), lambda g, core: (0, c * blocks + block_of(g, core), 0))
+
     def filter_forward(c, vfilter, pieces):
-        chunk = pl.BlockSpec((1, part, levels), lambda g: (0, c, 0))
         return pl.pallas_call(
-            functools.partial(filter_kernel, groups),
-            grid=(1,),
-            in_specs=[square, chunk] + [whole] * groups,
-            out_specs=[half_block, half_block],
+            filter_kernel,
+            grid_spec=pltpu.PrefetchScalarGridSpec(
+                num_scalar_prefetch=1,
+                grid=(blocks,),
+                in_specs=[square, perturb_part(c), slab],
+                out_specs=[first_half, second_half],
+                scratch_shapes=[table],
+            ),
             out_shape=[half_shape, half_shape],
             compiler_params=params,
             cost_estimate=cost,
             name="filter_forward",
-        )(vfilter, perturb, *pieces)
+        )(core, vfilter, perturb, pieces)
 
     def filter_backward(c, adj_mine, adj_other):
-        chunk = pl.BlockSpec((1, part, levels), lambda g: (0, c, 0))
         return pl.pallas_call(
-            functools.partial(back_kernel, groups),
-            grid=(1,),
-            in_specs=[square, chunk, half_block, half_block],
-            out_specs=[whole] * groups,
-            out_shape=[piece_shape] * groups,
+            back_kernel,
+            grid_spec=pltpu.PrefetchScalarGridSpec(
+                num_scalar_prefetch=1,
+                grid=(blocks,),
+                in_specs=[square, perturb_part(c), first_half, second_half],
+                out_specs=slab,
+                scratch_shapes=[table],
+            ),
+            out_shape=pieces_shape,
             compiler_params=params,
             cost_estimate=cost,
             name="filter_backward",
-        )(vfilter, perturb, adj_mine, adj_other)
+        )(core, vfilter, perturb, adj_mine, adj_other)
 
     def exchange(pieces):
-        return [pieces[0]] + [lax.ppermute(pieces[d], "lev", flip_pairs(groups, turns[d])) for d in range(1, groups)]
-
-    def sum_members(keep, send, gate):
+        return lax.all_to_all(pieces, "lev", 0, 0, tiled=True)
+
+    def sum_members(keep, send):
         total = keep + lax.ppermute(send, "mem", flip_pairs(n_mem, 1))
         bit = 2
         while bit < n_mem:
-            other = lax.ppermute(total, "mem", flip_pairs(n_mem, bit))
-            total = total + (after(other, *gate) if gate else other)
+            total = total + lax.ppermute(total, "mem", flip_pairs(n_mem, bit))
             bit *= 2
         return total
 
@@ -380,19 +382,17 @@
         return mine, lax.ppermute(mine, "mem", flip_pairs(n_mem, 1))
 
     got = [exchange(outgoing[c]) for c in range(PARTS)]
-    slots = after(slots, got[0][1])
     weight = [weights(c, slots) for c in range(PARTS)]
     back = []
     gate_filter = []
-    gate_sum = []
     for c in range(PARTS):
         gated = after(vfilter, *gate_filter) if gate_filter else vfilter
         keep, send = filter_forward(c, gated, got[c])
-        mine, other = adjoint(sum_members(keep, send, gate_sum), weight[c])
-        gate_filter = [mine] + weight
-        pieces = exchange(filter_backward(c, mine, other))
-        gate_sum = [pieces[3]]
-        back += pieces
+        mine, other = adjoint(sum_members(keep, send), weight[c])
+        adjoint_pieces = filter_backward(c, mine, other)
+        pieces = exchange(adjoint_pieces)
+        gate_filter = [adjoint_pieces]
+        back.append(pieces)
 
     return pl.pallas_call(
         functools.partial(backward_kernel, size_x, size_y, groups, capacity),
@@ -401,7 +401,7 @@
             smem,
             pl.BlockSpec((size_x, GROUP, size_y), lambda g: (0, g, 0)),
         ]
-        + [pl.BlockSpec(memory_space=pl.ANY)] * (groups * PARTS),
+        + [pl.BlockSpec(memory_space=pl.ANY)] * PARTS,
         out_specs=pl.BlockSpec((1, GROUP, size_x, size_y), lambda g: (0, g, 0, 0)),
         out_shape=jax.ShapeDtypeStruct((members, levels_here, size_x, size_y), F32),
         scratch_shapes=[
@@ -409,7 +409,7 @@
             pltpu.VMEM((GROUP, flat_width), F32),
         ]
         + [pltpu.VMEM((size_x, GROUP, size_y), F32)] * 5
-        + [pltpu.SemaphoreType.DMA((groups * PARTS,))],
+        + [pltpu.SemaphoreType.DMA((PARTS,))],
         compiler_params=params,
         name="place_and_smooth",
     )(sub_widths, diff, *back)

time: 222 us -> 210 us (0.946)
  blocking collectives: 0 us -> 41.2 us
  starting transfers between devices: 54.6 us -> 18.1 us
  Pallas kernels: 74.3 us -> 63.5 us
  waiting for transfers between devices: 78.4 us -> 73.6 us
    ppermute x30 -> x2, waiting for transfers between devices: 76 us -> 15.3 us  [sum_members(): total = total + lax.ppermute(total, 'mem', flip_pairs(n_mem, bit))]
    all_to_all x0 -> x3, waiting for transfers between devices: none -> 53.8 us  [exchange(): return lax.all_to_all(pieces, 'lev', 0, 0, tiled=True)]
    ppermute x30 -> x2, starting transfers between devices: 54 us -> 3.11 us  [sum_members(): total = total + lax.ppermute(total, 'mem', flip_pairs(n_mem, bit))]
    all_to_all x0 -> x1, blocking collectives: none -> 41.2 us  [exchange(): return lax.all_to_all(pieces, 'lev', 0, 0, tiled=True)]
    all_to_all x0 -> x3, starting transfers between devices: none -> 14.8 us  [exchange(): return lax.all_to_all(pieces, 'lev', 0, 0, tiled=True)]
    pallas_call x1, Pallas kernels: 21 us -> 15.4 us  [body(): pl.pallas_call(functools.partial(backward_kernel, size_x, size_y, groups,...]
    pallas_call x4, Pallas kernels: 19.2 us -> 14.4 us  [the longest x2 7.34 us: filter_forward(): pl.pallas_call(filter_kernel, grid_spec=pltpu.PrefetchScalarGridSpec(num_...]
    ppermute x2, waiting for transfers between devices: 0.01 us -> 4.54 us  [adjoint(): return (mine, lax.ppermute(mine, 'mem', flip_pairs(n_mem, 1)))]
  transfers between devices with their start and end apart: 34 -> 9, of which waited for: 17 -> 7; matrix products, arithmetic and copies ran while one was open for 4% -> 3% of each run, Pallas kernels for 13% -> 12%
where the time goes in v4:
time: 210 us; the launch traced here: 209 us
  waiting for transfers between devices  73.6 us (35%)
  Pallas kernels  63.5 us (30%)
  blocking collectives  41.2 us (20%)
  starting transfers between devices  18.1 us (9%)
  other arithmetic  5.85 us (3%)
  local copies, waits for them, and re-layouts  5.31 us (3%)
    all_to_all x3, waiting for transfers between devices, exchange(): return lax.all_to_all(pieces, 'lev', 0, 0, tiled=True)  53.8 us
    all_to_all x1, blocking collectives, exchange(): return lax.all_to_all(pieces, 'lev', 0, 0, tiled=True)  41.2 us
    pallas_call x2, Pallas kernels, weights(): pl.pallas_call(functools.partial(observation_kernel, part, c, obs_cap), g...  18.2 us
    pallas_call x1, Pallas kernels, body(): pl.pallas_call(functools.partial(forward_kernel, size_x, size_y, groups,...  15.5 us
    pallas_call x1, Pallas kernels, body(): pl.pallas_call(functools.partial(backward_kernel, size_x, size_y, groups,...  15.4 us
    ppermute x2, waiting for transfers between devices, sum_members(): total = total + lax.ppermute(total, 'mem', flip_pairs(n_mem, bit))  15.3 us
    all_to_all x3, starting transfers between devices, exchange(): return lax.all_to_all(pieces, 'lev', 0, 0, tiled=True)  14.8 us
    pallas_call x2, Pallas kernels, filter_forward(): pl.pallas_call(filter_kernel, grid_spec=pltpu.PrefetchScalarGridSpec(num_...  7.34 us
  transfers between devices with their start and end apart: 9, of which 7 were waited for; matrix products, arithmetic and copies ran while one was open for 3% of the time, Pallas kernels for 12%

profile of v4, /device:TPU:0, one launch (start us, length us, event | category | flops | bytes accessed | tf_op | source)
XLA Modules:
  0.0 209.0 jit_solution(812639470015294428)
XLA Ops:
  0.0 15.5 %smooth_and_cut.1 = (f32[128,16,256]{2,1,0:T(8,128)}, f32[8,16,3072]{2,1,0:T(8,128)}, f32[8,16,3072]{2,1,0:T(8,128)}) custom-call(s32[8]{0:T(128)} %widths.3, f32[1,16,128,256]{3,2,1,0:T(8,128)} %control.1, f32[16,128,256]{2,1,0:T(8,128)} %diffusivity.1), custom_call_target="tpu_custom_call" | custom-call | tf_op jit(solution)/shard_map/smooth_and_cut/pallas_call | solution.py:275
  15.5 7.3 %all-to-all-start = ((f32[8,16,3072]{2,1,0:T(8,128)}), f32[8,16,3072]{2,1,0:T(8,128)S(1)}, u32[]{:S(2)}, u32[]{:S(2)}) async-start(f32[8,16,3072]{2,1,0:T(8,128)} %get-tuple-element.14), calls=%async_computation | async-start | bytes 3145728 | tf_op jit(solution)/shard_map/all_to_all | solution.py:370
  22.7 37.0 %all-to-all-done.pieces = f32[8,16,3072]{2,1,0:T(8,128)S(1)} async-done(((f32[8,16,3072]{2,1,0:T(8,128)}), f32[8,16,3072]{2,1,0:T(8,128)S(1)}, u32[]{:S(2)}, u32[]{:S(2)}) %all-to-all-start) | async-done | bytes 1572896 | tf_op jit(solution)/shard_map/all_to_all | solution.py:370
  60.9 3.7 %filter_forward.2 = (f32[1536,128]{1,0:T(8,128)}, f32[1536,128]{1,0:T(8,128)}) custom-call(s32[1]{0:T(128)} %bitcast.core, f32[128,128]{1,0:T(8,128)} %vfilter.6, f32[1,6144,128]{2,1,0:T(8,128)} %perturb.7, f32[8,16,3072]{2,1,0:T(8,128)} %copy-done.1), custom_call_target="tpu_custom_call" | custom-call | tf_op jit(solution)/shard_map/filter_forward/pallas_call | solution.py:338
  64.6 3.8 %all-to-all-start.2 = ((f32[8,16,3072]{2,1,0:T(8,128)}), f32[8,16,3072]{2,1,0:T(8,128)S(1)}, u32[]{:S(2)}, u32[]{:S(2)}) async-start(f32[8,16,3072]{2,1,0:T(8,128)} %get-tuple-element.18), calls=%async_computation.2 | async-start | bytes 3145728 | tf_op jit(solution)/shard_map/all_to_all | solution.py:370
  71.0 1.6 collective-permute-start.1
  72.5 3.2 %compare_select_fusion.slots = s32[1,6144]{1,0:T(1,128)} fusion(pred[]{:T(512)S(6)} %lt.37, s32[1,6144]{1,0:T(1,128)S(1)} %copy-done.9, s32[]{:T(128)S(6)} %select_n.27, s32[]{:T(128)} %bitcast.1), kind=kLoop, calls=%fused_computation.3 | loop fusion | flops 55296 | bytes 49161 | tf_op jit(solution)/shard_map/jit(_where)/select_n | solution.py:298
  75.7 9.1 %observation_weights.2 = f32[1536,128]{1,0:T(8,128)} custom-call(s32[1,6144]{1,0:T(1,128)} %compare_select_fusion.slots, f32[1,6144,128]{2,1,0:T(8,128)} %rinv.3), custom_call_target="tpu_custom_call" | custom-call | tf_op jit(solution)/shard_map/observation_weights/pallas_call | solution.py:319
  84.8 6.1 %collective-permute-done.1 = f32[1536,128]{1,0:T(8,128)S(1)} collective-permute-done((f32[1536,128]{1,0:T(8,128)S(1)}, f32[1536,128]{1,0:T(8,128)S(1)}, u32[]{:S(2)}, u32[]{:S(2)}) %collective-permute-start.1) | collective-permute-done | bytes 786464 | tf_op jit(solution)/shard_map/ppermute | solution.py:376
  90.9 1.2 add_multiply_fusion.1.adj_mine
  92.3 2.3 %collective-permute-done.2.adj_other = f32[1536,128]{1,0:T(8,128)S(1)} collective-permute-done((f32[1536,128]{1,0:T(8,128)S(1)}, f32[1536,128]{1,0:T(8,128)S(1)}, u32[]{:S(2)}, u32[]{:S(2)}) %collective-permute-start.2) | collective-permute-done | bytes 786464 | tf_op jit(solution)/shard_map/ppermute | solution.py:382
  95.5 3.5 %filter_backward.2 = f32[8,16,3072]{2,1,0:T(8,128)} custom-call(s32[1]{0:T(128)} %bitcast.core, f32[128,128]{1,0:T(8,128)} %vfilter.6, f32[1,6144,128]{2,1,0:T(8,128)} %perturb.7, f32[1536,128]{1,0:T(8,128)} %copy-done.4, f32[1536,128]{1,0:T(8,128)} %copy-done.6), custom_call_target="tpu_custom_call" | custom-call | tf_op jit(solution)/shard_map/filter_backward/pallas_call | solution.py:354
  99.0 7.2 %all-to-all-done.2.pieces = f32[8,16,3072]{2,1,0:T(8,128)S(1)} async-done(((f32[8,16,3072]{2,1,0:T(8,128)}), f32[8,16,3072]{2,1,0:T(8,128)S(1)}, u32[]{:S(2)}, u32[]{:S(2)}) %all-to-all-start.2) | async-done | bytes 1572896 | tf_op jit(solution)/shard_map/all_to_all | solution.py:370
  107.3 3.7 %filter_forward.3 = (f32[1536,128]{1,0:T(8,128)}, f32[1536,128]{1,0:T(8,128)}) custom-call(s32[1]{0:T(128)} %bitcast.core, f32[128,128]{1,0:T(8,128)} %vfilter.6, f32[1,6144,128]{2,1,0:T(8,128)} %perturb.7, f32[8,16,3072]{2,1,0:T(8,128)} %copy-done), custom_call_target="tpu_custom_call" | custom-call | tf_op jit(solution)/shard_map/filter_forward/pallas_call | solution.py:338
  111.0 3.8 %all-to-all-start.1 = ((f32[8,16,3072]{2,1,0:T(8,128)}), f32[8,16,3072]{2,1,0:T(8,128)S(1)}, u32[]{:S(2)}, u32[]{:S(2)}) async-start(f32[8,16,3072]{2,1,0:T(8,128)} %filter_backward.2), calls=%async_computation.1 | async-start | bytes 3145728 | tf_op jit(solution)/shard_map/all_to_all | solution.py:370
  114.9 1.6 collective-permute-start.4
  116.4 9.1 %observation_weights.3 = f32[1536,128]{1,0:T(8,128)} custom-call(s32[1,6144]{1,0:T(1,128)} %compare_select_fusion.slots, f32[1,6144,128]{2,1,0:T(8,128)} %rinv.3), custom_call_target="tpu_custom_call" | custom-call | tf_op jit(solution)/shard_map/observation_weights/pallas_call | solution.py:319
  125.5 9.2 %collective-permute-done.4 = f32[1536,128]{1,0:T(8,128)S(1)} collective-permute-done((f32[1536,128]{1,0:T(8,128)S(1)}, f32[1536,128]{1,0:T(8,128)S(1)}, u32[]{:S(2)}, u32[]{:S(2)}) %collective-permute-start.4) | collective-permute-done | bytes 786464 | tf_op jit(solution)/shard_map/ppermute | solution.py:376
  134.7 1.2 add_multiply_fusion.adj_mine
  136.0 2.3 %collective-permute-done.5.adj_other = f32[1536,128]{1,0:T(8,128)S(1)} collective-permute-done((f32[1536,128]{1,0:T(8,128)S(1)}, f32[1536,128]{1,0:T(8,128)S(1)}, u32[]{:S(2)}, u32[]{:S(2)}) %collective-permute-start.5) | collective-permute-done | bytes 786464 | tf_op jit(solution)/shard_map/ppermute | solution.py:382
  139.2 3.5 %filter_backward.3 = f32[8,16,3072]{2,1,0:T(8,128)} custom-call(s32[1]{0:T(128)} %bitcast.core, f32[128,128]{1,0:T(8,128)} %vfilter.6, f32[1,6144,128]{2,1,0:T(8,128)} %perturb.7, f32[1536,128]{1,0:T(8,128)} %copy-done.3, f32[1536,128]{1,0:T(8,128)} %copy-done.5), custom_call_target="tpu_custom_call" | custom-call | tf_op jit(solution)/shard_map/filter_backward/pallas_call | solution.py:354
  142.8 9.7 %all-to-all-done.1.rest_0_ = f32[8,16,3072]{2,1,0:T(8,128)S(1)} async-done(((f32[8,16,3072]{2,1,0:T(8,128)}), f32[8,16,3072]{2,1,0:T(8,128)S(1)}, u32[]{:S(2)}, u32[]{:S(2)}) %all-to-all-start.1) | async-done | bytes 1572896 | tf_op jit(solution)/shard_map/all_to_all | solution.py:370
  152.4 41.2 %all_to_all.20.rest_1_ = f32[8,16,3072]{2,1,0:T(8,128)} all-to-all(f32[8,16,3072]{2,1,0:T(8,128)} %filter_backward.3), channel_id=1, replica_groups=mesh['mem'=4,'lev'=8] {'lev'}, dimensions={0} | all-to-all | bytes 3145728 | tf_op jit(solution)/shard_map/all_to_all | solution.py:370
  193.6 15.4 %place_and_smooth.1 = f32[1,16,128,256]{3,2,1,0:T(8,128)} custom-call(s32[8]{0:T(128)} %widths.3, f32[128,16,256]{2,1,0:T(8,128)} %get-tuple-element.13.diff, f32[8,16,3072]{2,1,0:T(8,128)} %copy-done.2, f32[8,16,3072]{2,1,0:T(8,128)} %all_to_all.20.rest_1_), custom_call_target="tpu_custom_call" | custom-call | tf_op jit(solution)/shard_map/place_and_smooth/pallas_call | solution.py:397
  (34 shorter events, 5.6 us)
Async XLA Ops:
  15.5 44.3 %all-to-all-start = ((f32[8,16,3072]{2,1,0:T(8,128)}), f32[8,16,3072]{2,1,0:T(8,128)S(1)}, u32[]{:S(2)}, u32[]{:S(2)}) async-start(f32[8,16,3072]{2,1,0:T(8,128)} %get-tuple-element.14), calls=%async_computation | async-start | bytes 3145728 | tf_op jit(solution)/shard_map/all_to_all | solution.py:370
  59.8 1.1 copy-start.1
  64.6 6.3 %collective-permute-start = (f32[1536,128]{1,0:T(8,128)}, f32[1536,128]{1,0:T(8,128)S(1)}, u32[]{:S(2)}, u32[]{:S(2)}) collective-permute-start(f32[1536,128]{1,0:T(8,128)} %get-tuple-element.16), channel_id=1, source_target_pairs={{0,8},{8,0},{16,24},{24,16},{1,9},{9,1},{17,25},{25,17},{2,10},{10... | collective-permute-start | bytes 2359304 | tf_op jit(solution)/shard_map/ppermute | solution.py:373
  64.6 3.8 %copy-start.10 = (s32[8]{0:T(128)S(1)}, s32[8]{0:T(128)}, u32[]{:S(2)}) copy-start(s32[8]{0:T(128)} %widths.3) | copy-start | bytes 100
  64.6 5.7 %copy-start.11 = (s32[8]{0:T(128)S(1)}, s32[8]{0:T(128)}, u32[]{:S(2)}) copy-start(s32[8]{0:T(128)} %param.14) | copy-start | bytes 100
  64.6 6.3 %copy-start.7 = (f32[1536,128]{1,0:T(8,128)S(1)}, f32[1536,128]{1,0:T(8,128)}, u32[]{:S(2)}) copy-start(f32[1536,128]{1,0:T(8,128)} %get-tuple-element.15) | copy-start | bytes 2359300
  64.6 41.6 %all-to-all-start.2 = ((f32[8,16,3072]{2,1,0:T(8,128)}), f32[8,16,3072]{2,1,0:T(8,128)S(1)}, u32[]{:S(2)}, u32[]{:S(2)}) async-start(f32[8,16,3072]{2,1,0:T(8,128)} %get-tuple-element.18), calls=%async_computation.2 | async-start | bytes 3145728 | tf_op jit(solution)/shard_map/all_to_all | solution.py:370
  68.4 4.2 %copy-start.9 = (s32[1,6144]{1,0:T(1,128)S(1)}, s32[1,6144]{1,0:T(1,128)}, u32[]{:S(2)}) copy-start(s32[1,6144]{1,0:T(1,128)} %param.13) | copy-start | bytes 73732
  71.0 20.0 %collective-permute-start.1 = (f32[1536,128]{1,0:T(8,128)S(1)}, f32[1536,128]{1,0:T(8,128)S(1)}, u32[]{:S(2)}, u32[]{:S(2)}) collective-permute-start(f32[1536,128]{1,0:T(8,128)S(1)} %add.28), channel_id=1, source_target_pairs={{0,16},{8,24},{16,0},{24,8},{1,17},{9,25},{17,1},{25,9},{2,18},{10... | collective-permute-start | bytes 2359304 | tf_op jit(solution)/shard_map/ppermute | solution.py:376
  92.2 2.4 %copy-start.4 = (f32[1536,128]{1,0:T(8,128)}, f32[1536,128]{1,0:T(8,128)S(1)}, u32[]{:S(2)}) copy-start(f32[1536,128]{1,0:T(8,128)S(1)} %add_multiply_fusion.1.adj_mine) | copy-start | bytes 2359300
  92.2 2.4 %collective-permute-start.2 = (f32[1536,128]{1,0:T(8,128)S(1)}, f32[1536,128]{1,0:T(8,128)S(1)}, u32[]{:S(2)}, u32[]{:S(2)}) collective-permute-start(f32[1536,128]{1,0:T(8,128)S(1)} %add_multiply_fusion.1.adj_mine), channel_id=1, source_target_pairs={{0,8},{8,0},{16,24},{24,16},{1,9},{9,1},{17,25},{25,17},{2,10},{10... | collective-permute-start | bytes 2359304 | tf_op jit(solution)/shard_map/ppermute | solution.py:382
  94.5 0.9 copy-start.6
  106.2 1.1 copy-start
  111.0 3.8 %copy-start.8 = (f32[1536,128]{1,0:T(8,128)S(1)}, f32[1536,128]{1,0:T(8,128)}, u32[]{:S(2)}) copy-start(f32[1536,128]{1,0:T(8,128)} %get-tuple-element.19) | copy-start | bytes 2359300
  111.0 3.8 %collective-permute-start.3 = (f32[1536,128]{1,0:T(8,128)}, f32[1536,128]{1,0:T(8,128)S(1)}, u32[]{:S(2)}, u32[]{:S(2)}) collective-permute-start(f32[1536,128]{1,0:T(8,128)} %get-tuple-element.20), channel_id=1, source_target_pairs={{0,8},{8,0},{16,24},{24,16},{1,9},{9,1},{17,25},{25,17},{2,10},{10... | collective-permute-start | bytes 2359304 | tf_op jit(solution)/shard_map/ppermute | solution.py:373
  111.0 41.5 %all-to-all-start.1 = ((f32[8,16,3072]{2,1,0:T(8,128)}), f32[8,16,3072]{2,1,0:T(8,128)S(1)}, u32[]{:S(2)}, u32[]{:S(2)}) async-start(f32[8,16,3072]{2,1,0:T(8,128)} %filter_backward.2), calls=%async_computation.1 | async-start | bytes 3145728 | tf_op jit(solution)/shard_map/all_to_all | solution.py:370
  114.9 19.8 %collective-permute-start.4 = (f32[1536,128]{1,0:T(8,128)S(1)}, f32[1536,128]{1,0:T(8,128)S(1)}, u32[]{:S(2)}, u32[]{:S(2)}) collective-permute-start(f32[1536,128]{1,0:T(8,128)S(1)} %add.32), channel_id=1, source_target_pairs={{0,16},{8,24},{16,0},{24,8},{1,17},{9,25},{17,1},{25,9},{2,18},{10... | collective-permute-start | bytes 2359304 | tf_op jit(solution)/shard_map/ppermute | solution.py:376
  135.9 2.4 %copy-start.3 = (f32[1536,128]{1,0:T(8,128)}, f32[1536,128]{1,0:T(8,128)S(1)}, u32[]{:S(2)}) copy-start(f32[1536,128]{1,0:T(8,128)S(1)} %add_multiply_fusion.adj_mine) | copy-start | bytes 2359300
  136.0 2.4 %collective-permute-start.5 = (f32[1536,128]{1,0:T(8,128)S(1)}, f32[1536,128]{1,0:T(8,128)S(1)}, u32[]{:S(2)}, u32[]{:S(2)}) collective-permute-start(f32[1536,128]{1,0:T(8,128)S(1)} %add_multiply_fusion.adj_mine), channel_id=1, source_target_pairs={{0,8},{8,0},{16,24},{24,16},{1,9},{9,1},{17,25},{25,17},{2,10},{10... | collective-permute-start | bytes 2359304 | tf_op jit(solution)/shard_map/ppermute | solution.py:382
  138.3 0.9 copy-start.5
  152.4 41.2 %copy-start.2 = (f32[8,16,3072]{2,1,0:T(8,128)}, f32[8,16,3072]{2,1,0:T(8,128)S(1)}, u32[]{:S(2)}) copy-start(f32[8,16,3072]{2,1,0:T(8,128)S(1)} %all-to-all-done.1.rest_0_) | copy-start | bytes 4718596

commit v5 on v4

--- a/solution.py
+++ b/solution.py
@@ -94,11 +94,16 @@
     return lax.fori_loop(0, j, lambda k, total: total + widths[k], jnp.int32(0))
 
 
-def forward_kernel(size_x, size_y, groups, capacity, widths, control, diffusivity, diff_out, *rest):
-    outs = rest[:PARTS]
-    flat, one, two, *face_refs = rest[PARTS:]
+def turns_of(groups):
+    return [0] + list(range(groups // 2, groups)) + list(range(groups // 2 - 1, 0, -1))
+
+
+def forward_kernel(size_x, size_y, groups, widths, control, diffusivity, *rest):
+    *rest, flat, one, two, face_x, face_up, face_down = rest
+    diff_out, later, *sooner = rest[-groups - 2 :]
+    face_refs = (face_x, face_up, face_down)
     columns = size_x * size_y
-    part = capacity // PARTS
+    part = later.shape[2]
     transpose_in(diffusivity, diff_out, size_x)
     faces(diff_out, *face_refs, size_x, size_y)
     transpose_in(control.at[0], one, size_x)
@@ -108,26 +113,37 @@
     flat[:, columns:] = jnp.zeros((GROUP, flat.shape[1] - columns), F32)
 
     lane = lax.broadcasted_iota(jnp.int32, (GROUP, LANES), 1)
+    me = lax.axis_index("lev")
     tiles = part // LANES
-    for j in range(groups):
+
+    def cut(j, c, store):
         start = start_of(widths, j)
         base = start // LANES
         shift = start - base * LANES
         back = lax.rem(LANES - shift, LANES)
         low = lane < LANES - shift
-        for c in range(PARTS):
-            out = outs[c]
-            begin = base + c * tiles
-
-            def load(t):
-                at = pl.multiple_of((begin + t) * LANES, LANES)
-                return pltpu.roll(flat[:, pl.ds(at, LANES)], back, 1)
-
-            now = load(0)
-            for t in range(tiles):
-                later = load(t + 1)
-                out[j, :, t * LANES : (t + 1) * LANES] = jnp.where(low, now, later)
-                now = later
+        begin = base + c * tiles
+
+        def load(t):
+            at = pl.multiple_of((begin + t) * LANES, LANES)
+            return pltpu.roll(flat[:, pl.ds(at, LANES)], back, 1)
+
+        now = load(0)
+        for t in range(tiles):
+            following = load(t + 1)
+            store(t, jnp.where(low, now, following))
+            now = following
+
+    for d, turn in enumerate(turns_of(groups)):
+
+        def store_sooner(t, value):
+            sooner[d][:, t * LANES : (t + 1) * LANES] = value
+
+        def store_later(t, value):
+            later[d, :, t * LANES : (t + 1) * LANES] = value
+
+        cut(jnp.bitwise_xor(me, turn), 0, store_sooner)
+        cut(d, 1, store_later)
 
 
 def split2(value):
@@ -153,7 +169,8 @@
     out[...] = total[:, :levels] + total[:, levels:]
 
 
-def filter_kernel(core, vfilter, perturb, pieces, keep, send, table):
+def filter_kernel(core, vfilter, perturb, *rest):
+    *pieces, keep, send, table = rest
     levels = vfilter.shape[0]
     rows = keep.shape[0]
     step = pl.program_id(0)
@@ -167,7 +184,7 @@
         table[:levels, levels:] = low
         table[levels:, levels:] = jnp.zeros_like(low)
 
-    slab = pieces[...].reshape(levels, rows)
+    slab = jnp.concatenate([piece[...].reshape(-1, rows) for piece in pieces], axis=0)
     both = jnp.concatenate(split2(slab.T), axis=1)
     products = jnp.dot(both, table[...], preferred_element_type=F32)
     result = perturb[0] * (products[:, :levels] + products[:, levels:])
@@ -181,7 +198,8 @@
         send[...] = result
 
 
-def back_kernel(core, vfilter, perturb, adj_mine, adj_other, pieces, table):
+def back_kernel(core, vfilter, perturb, adj_mine, adj_other, *rest):
+    *pieces, table = rest
     levels = vfilter.shape[0]
     step = pl.program_id(0)
     blocks = pl.num_programs(0) // 2
@@ -198,20 +216,31 @@
     both = jnp.concatenate(split2(perturb[0] * adj), axis=1)
     products = jnp.dot(both, table[...], preferred_element_type=F32)
     result = (products[:, :levels] + products[:, levels:]).T
-    pieces[...] = result.reshape(pieces.shape)
-
-
-def backward_kernel(size_x, size_y, groups, capacity, widths, diff, *rest):
-    ins = rest[:PARTS]
-    out, staging, flat, one, two, *face_refs, sem = rest[PARTS:]
+    first = 0
+    for piece in pieces:
+        count = piece.size // piece.shape[-1]
+        piece[...] = result[first : first + count].reshape(piece.shape)
+        first += count
+
+
+def backward_kernel(size_x, size_y, groups, capacity, group, widths, diff, *rest):
+    *rest, staging, flat, one, two, face_x, face_up, face_down, sem = rest
+    face_refs = (face_x, face_up, face_down)
+    sooner, *later = rest[: groups + 1]
+    out = rest[-1]
     part = capacity // PARTS
-    level = pl.multiple_of(pl.program_id(0) * GROUP, GROUP)
+    me = lax.axis_index("lev")
     copies = [
         pltpu.make_async_copy(
-            ins[c].at[:, pl.ds(level, GROUP), :], staging.at[:, :, pl.ds(c * part, part)], sem.at[c]
+            sooner.at[:, pl.ds(group * GROUP, GROUP), :], staging.at[:, :, pl.ds(0, part)], sem.at[0]
         )
-        for c in range(PARTS)
     ]
+    for d, turn in enumerate(turns_of(groups)):
+        copies.append(
+            pltpu.make_async_copy(
+                later[d], staging.at[jnp.bitwise_xor(me, turn), :, pl.ds(part, part)], sem.at[1 + d]
+            )
+        )
     for copy in copies:
         copy.start()
     faces(diff, *face_refs, size_x, size_y)
@@ -269,35 +298,54 @@
     smem = pl.BlockSpec(memory_space=pltpu.SMEM)
     params = pltpu.CompilerParams(vmem_limit_bytes=56 << 20)
     flat_width = columns + capacity + LANES
+    piece_shape = jax.ShapeDtypeStruct((GROUP, part), F32)
     pieces_shape = jax.ShapeDtypeStruct((groups, levels_here, part), F32)
-    steps = levels_here // GROUP
-
-    results = pl.pallas_call(
-        functools.partial(forward_kernel, size_x, size_y, groups, capacity),
-        grid=(steps,),
-        in_specs=[
-            smem,
-            pl.BlockSpec((1, GROUP, size_x, size_y), lambda g: (0, g, 0, 0)),
-            pl.BlockSpec((GROUP, size_x, size_y), lambda g: (g, 0, 0)),
-        ],
-        out_specs=[pl.BlockSpec((size_x, GROUP, size_y), lambda g: (0, g, 0))]
-        + [pl.BlockSpec((groups, GROUP, part), lambda g: (0, g, 0))] * PARTS,
-        out_shape=[jax.ShapeDtypeStruct((size_x, levels_here, size_y), F32)] + [pieces_shape] * PARTS,
-        scratch_shapes=[
-            pltpu.VMEM((GROUP, flat_width), F32),
-        ]
-        + [pltpu.VMEM((size_x, GROUP, size_y), F32)] * 5,
-        compiler_params=params,
-        name="smooth_and_cut",
-    )(sub_widths, control, diffusivity)
-    diff = results[0]
-    outgoing = results[1:]
+    n_groups = levels_here // GROUP
+    any_spec = pl.BlockSpec(memory_space=pl.ANY)
+    turns = turns_of(groups)
+
+    def permute(piece, d):
+        return lax.ppermute(piece, "lev", flip_pairs(groups, turns[d])) if d else piece
+
+    diffs, later, got = [], None, {}
+    widths = sub_widths
+    for group in range(n_groups):
+        before = [] if later is None else [later]
+        results = pl.pallas_call(
+            functools.partial(forward_kernel, size_x, size_y, groups),
+            grid=(1,),
+            in_specs=[
+                smem,
+                pl.BlockSpec((1, GROUP, size_x, size_y), lambda g, group=group: (0, group, 0, 0)),
+                pl.BlockSpec((GROUP, size_x, size_y), lambda g, group=group: (group, 0, 0)),
+            ]
+            + [any_spec] * len(before),
+            out_specs=[
+                pl.BlockSpec((size_x, GROUP, size_y), lambda g: (0, 0, 0)),
+                pl.BlockSpec((groups, GROUP, part), lambda g, group=group: (0, group, 0)),
+            ]
+            + [pl.BlockSpec((GROUP, part), lambda g: (0, 0))] * groups,
+            out_shape=[jax.ShapeDtypeStruct((size_x, GROUP, size_y), F32), pieces_shape] + [piece_shape] * groups,
+            input_output_aliases={3: 1} if before else {},
+            scratch_shapes=[pltpu.VMEM((GROUP, flat_width), F32)]
+            + [pltpu.VMEM((size_x, GROUP, size_y), F32)] * 5,
+            compiler_params=params,
+            cost_estimate=pl.CostEstimate(flops=0, bytes_accessed=0, transcendentals=0),
+            name="smooth_and_cut",
+        )(widths, control, diffusivity, *before)
+        diffs.append(results[0])
+        later = results[1]
+        for d in range(groups):
+            got[d, group] = permute(results[2 + d], d)
+        widths = after(sub_widths, got[7, group])
 
     width = sub_widths[me]
     live = jnp.arange(obs_cap, dtype=jnp.int32) < obs_counts[me]
     slots = jnp.where(live, obs_raw[0] % width, -1)[None, :]
 
-    vfilter = vertical_filter
+    order = jnp.bitwise_xor(me, jnp.array(turns, jnp.int32))
+    turned = vertical_filter.reshape(levels, groups, levels_here)[:, order, :].reshape(levels, levels)
+
     width = half
     blocks = part // width
     some = blocks // 2
@@ -307,6 +355,8 @@
 
     square = pl.BlockSpec((levels, levels), lambda g, core: (0, 0))
     slab = pl.BlockSpec((groups, levels_here, width), lambda g, core: (0, 0, block_of(g, core)))
+    strip = pl.BlockSpec((GROUP, width), lambda g, core: (0, block_of(g, core)))
+    n_strips = groups * n_groups
     first_half = pl.BlockSpec((width, levels), lambda g, core: (jnp.minimum(g, some - 1), 0))
     second_half = pl.BlockSpec((width, levels), lambda g, core: (jnp.maximum(g - some, 0), 0))
     half_shape = jax.ShapeDtypeStruct((half, levels), F32)
@@ -334,13 +384,13 @@
     def perturb_part(c):
         return pl.BlockSpec((1, width, levels), lambda g, core: (0, c * blocks + block_of(g, core), 0))
 
-    def filter_forward(c, vfilter, pieces):
+    def filter_forward(c, vfilter, *pieces):
         return pl.pallas_call(
             filter_kernel,
             grid_spec=pltpu.PrefetchScalarGridSpec(
                 num_scalar_prefetch=1,
                 grid=(blocks,),
-                in_specs=[square, perturb_part(c), slab],
+                in_specs=[square, perturb_part(c)] + ([slab] if len(pieces) == 1 else [strip] * n_strips),
                 out_specs=[first_half, second_half],
                 scratch_shapes=[table],
             ),
@@ -348,19 +398,19 @@
             compiler_params=params,
             cost_estimate=cost,
             name="filter_forward",
-        )(core, vfilter, perturb, pieces)
-
-    def filter_backward(c, adj_mine, adj_other):
+        )(core, vfilter, perturb, *pieces)
+
+    def filter_backward(c, vfilter, adj_mine, adj_other, strips):
         return pl.pallas_call(
             back_kernel,
             grid_spec=pltpu.PrefetchScalarGridSpec(
                 num_scalar_prefetch=1,
                 grid=(blocks,),
                 in_specs=[square, perturb_part(c), first_half, second_half],
-                out_specs=slab,
+                out_specs=[strip] * n_strips if strips else [slab],
                 scratch_shapes=[table],
             ),
-            out_shape=pieces_shape,
+            out_shape=[piece_shape] * n_strips if strips else [pieces_shape],
             compiler_params=params,
             cost_estimate=cost,
             name="filter_backward",
@@ -381,38 +431,45 @@
         mine = total * obs_weight
         return mine, lax.ppermute(mine, "mem", flip_pairs(n_mem, 1))
 
-    got = [exchange(outgoing[c]) for c in range(PARTS)]
+    in_order = [(d, group) for d in range(groups) for group in range(n_groups)]
+    slots = after(slots, got[1, 0])
     weight = [weights(c, slots) for c in range(PARTS)]
-    back = []
-    gate_filter = []
-    for c in range(PARTS):
-        gated = after(vfilter, *gate_filter) if gate_filter else vfilter
-        keep, send = filter_forward(c, gated, got[c])
-        mine, other = adjoint(sum_members(keep, send), weight[c])
-        adjoint_pieces = filter_backward(c, mine, other)
-        pieces = exchange(adjoint_pieces)
-        gate_filter = [adjoint_pieces]
-        back.append(pieces)
-
-    return pl.pallas_call(
-        functools.partial(backward_kernel, size_x, size_y, groups, capacity),
-        grid=(steps,),
-        in_specs=[
-            smem,
-            pl.BlockSpec((size_x, GROUP, size_y), lambda g: (0, g, 0)),
-        ]
-        + [pl.BlockSpec(memory_space=pl.ANY)] * PARTS,
-        out_specs=pl.BlockSpec((1, GROUP, size_x, size_y), lambda g: (0, g, 0, 0)),
-        out_shape=jax.ShapeDtypeStruct((members, levels_here, size_x, size_y), F32),
-        scratch_shapes=[
-            pltpu.VMEM((groups, GROUP, capacity), F32),
-            pltpu.VMEM((GROUP, flat_width), F32),
-        ]
-        + [pltpu.VMEM((size_x, GROUP, size_y), F32)] * 5
-        + [pltpu.SemaphoreType.DMA((PARTS,))],
-        compiler_params=params,
-        name="place_and_smooth",
-    )(sub_widths, diff, *back)
+    got_later = exchange(later)
+
+    keep, send = filter_forward(0, turned, *[got[key] for key in in_order])
+    mine, other = adjoint(sum_members(keep, send), weight[0])
+    pieces = filter_backward(0, vertical_filter, mine, other, False)[0]
+    back_sooner = exchange(pieces)
+
+    keep, send = filter_forward(1, after(vertical_filter, pieces), got_later)
+    mine, other = adjoint(sum_members(keep, send), weight[1])
+    pieces = filter_backward(1, turned, mine, other, True)
+    out = None
+    for group in range(n_groups):
+        before = [] if out is None else [out]
+        back = []
+        for d in range(groups):
+            piece = pieces[in_order.index((d, group))]
+            back.append(permute(after(piece, out) if before and d in (6,) else piece, d))
+        out = pl.pallas_call(
+            functools.partial(backward_kernel, size_x, size_y, groups, capacity, group),
+            grid=(1,),
+            in_specs=[smem, pl.BlockSpec((size_x, GROUP, size_y), lambda g: (0, 0, 0))]
+            + [any_spec] * (1 + groups + len(before)),
+            out_specs=pl.BlockSpec((1, GROUP, size_x, size_y), lambda g, group=group: (0, group, 0, 0)),
+            out_shape=jax.ShapeDtypeStruct((members, levels_here, size_x, size_y), F32),
+            input_output_aliases={3 + groups: 0} if before else {},
+            scratch_shapes=[
+                pltpu.VMEM((groups, GROUP, capacity), F32),
+                pltpu.VMEM((GROUP, flat_width), F32),
+            ]
+            + [pltpu.VMEM((size_x, GROUP, size_y), F32)] * 5
+            + [pltpu.SemaphoreType.DMA((1 + groups,))],
+            compiler_params=params,
+            cost_estimate=pl.CostEstimate(flops=0, bytes_accessed=0, transcendentals=0),
+            name="place_and_smooth",
+        )(sub_widths, diffs[group], back_sooner, *back, *before)
+    return out
 
 
 def solution(mesh):

time: 210 us -> 196 us (0.933)
  blocking collectives: 41.2 us -> 0 us
  starting transfers between devices: 18.1 us -> 57.4 us
  waiting for transfers between devices: 73.6 us -> 52.1 us
  Pallas kernels: 63.5 us -> 70.5 us
  local copies, waits for them, and re-layouts: 5.31 us -> 7.96 us
    all_to_all x3 -> x2, waiting for transfers between devices: 53.8 us -> 7.22 us  [exchange(): return lax.all_to_all(pieces, 'lev', 0, 0, tiled=True)]
    ppermute x0 -> x28, starting transfers between devices: none -> 44.9 us  [permute(): lax.ppermute(piece, 'lev', flip_pairs(groups, turns[d]))]
    all_to_all x1 -> x0, blocking collectives: 41.2 us -> none  [exchange(): return lax.all_to_all(pieces, 'lev', 0, 0, tiled=True)]
    ppermute x0 -> x28, waiting for transfers between devices: none -> 25.4 us  [permute(): lax.ppermute(piece, 'lev', flip_pairs(groups, turns[d]))]
    all_to_all x3 -> x2, starting transfers between devices: 14.8 us -> 9.17 us  [exchange(): return lax.all_to_all(pieces, 'lev', 0, 0, tiled=True)]
    pallas_call x1 -> x2, Pallas kernels: 15.5 us -> 19.7 us  [body(): pl.pallas_call(functools.partial(forward_kernel, size_x, size_y, groups),...]
    pallas_call x1 -> x2, Pallas kernels: 15.4 us -> 17.2 us  [body(): pl.pallas_call(functools.partial(backward_kernel, size_x, size_y, groups,...]
    unnamed x24 -> x89, local copies, waits for them, and re-layouts: 4.13 us -> 5.45 us
  transfers between devices with their start and end apart: 9 -> 36, of which waited for: 7 -> 13; matrix products, arithmetic and copies ran while one was open for 3% -> 4% of each run, Pallas kernels for 12% -> 23%
where the time goes in v5:
time: 196 us
  Pallas kernels  70.5 us (36%)
  starting transfers between devices  57.4 us (29%)
  waiting for transfers between devices  52.1 us (27%)
  local copies, waits for them, and re-layouts  7.96 us (4%)
  other arithmetic  5.85 us (3%)
  between operations  2 us (1%)
    ppermute x28, starting transfers between devices, permute(): lax.ppermute(piece, 'lev', flip_pairs(groups, turns[d]))  44.9 us
    ppermute x28, waiting for transfers between devices, permute(): lax.ppermute(piece, 'lev', flip_pairs(groups, turns[d]))  25.4 us
    pallas_call x2, Pallas kernels, body(): pl.pallas_call(functools.partial(forward_kernel, size_x, size_y, groups),...  19.7 us
    pallas_call x2, Pallas kernels, weights(): pl.pallas_call(functools.partial(observation_kernel, part, c, obs_cap), g...  18.3 us
    pallas_call x2, Pallas kernels, body(): pl.pallas_call(functools.partial(backward_kernel, size_x, size_y, groups,...  17.2 us
    ppermute x2, waiting for transfers between devices, sum_members(): total = total + lax.ppermute(total, 'mem', flip_pairs(n_mem, bit))  15 us
    all_to_all x2, starting transfers between devices, exchange(): return lax.all_to_all(pieces, 'lev', 0, 0, tiled=True)  9.17 us
    pallas_call x2, Pallas kernels, filter_forward(): pl.pallas_call(filter_kernel, grid_spec=pltpu.PrefetchScalarGridSpec(num_...  7.81 us
  transfers between devices with their start and end apart: 36, of which 13 were waited for; matrix products, arithmetic and copies ran while one was open for 4% of the time, Pallas kernels for 23%

profile of v5, /device:TPU:0, one launch (start us, length us, event | category | flops | bytes accessed | tf_op | source)
XLA Modules:
  0.0 195.9 jit_solution(16549175238966304164)
XLA Ops:
  0.0 9.8 %smooth_and_cut.2 = (f32[128,8,256]{2,1,0:T(8,128)}, f32[8,16,3072]{2,1,0:T(8,128)}, f32[8,3072]{1,0:T(8,128)}, f32[8,3072]{1,0:T(8,128)}, f32[8,3072]{1,0:T(8,1...) custom-call(s32[8]{0:T(128)} %widths.6, ...), custom_call_target="tpu_custom_call" | custom-call | tf_op jit(solution)/shard_map/smooth_and_cut/pallas_call | solution.py:314
  9.8 3.0 %collective-permute-start = (f32[8,3072]{1,0:T(8,128)}, f32[8,3072]{1,0:T(8,128)S(1)}, u32[]{:S(2)}, u32[]{:S(2)}) collective-permute-start(f32[8,3072]{1,0:T(8,128)} %get-tuple-element.49), channel_id=1, source_target_pairs={{0,1},{1,0},{2,3},{3,2},{4,5},{5,4},{6,7},{7,6},{8,9},{9,8},{10,11... | collective-permute-start | bytes 294920 | tf_op jit(solution)/shard_map/ppermute | solution.py:308
  22.1 9.9 %smooth_and_cut.3 = (f32[128,8,256]{2,1,0:T(8,128)}, f32[8,16,3072]{2,1,0:T(8,128)}, f32[8,3072]{1,0:T(8,128)}, f32[8,3072]{1,0:T(8,128)}, f32[8,3072]{1,0:T(8,1...) custom-call(s32[8]{0:T(128)} %widths.6, ...), custom_call_target="tpu_custom_call", output_to_operand_aliasing={{1}: (3, {})} | custom-call | tf_op jit(solution)/shard_map/smooth_and_cut/pallas_call | solution.py:314
  40.2 3.4 %collective-permute-start.6 = (f32[8,3072]{1,0:T(8,128)}, f32[8,3072]{1,0:T(8,128)S(1)}, u32[]{:S(2)}, u32[]{:S(2)}) collective-permute-start(f32[8,3072]{1,0:T(8,128)} %get-tuple-element.60), channel_id=1, source_target_pairs={{0,6},{1,7},{2,4},{3,5},{4,2},{5,3},{6,0},{7,1},{8,14},{9,15},{10,... | collective-permute-start | bytes 294920 | tf_op jit(solution)/shard_map/ppermute | solution.py:308
  46.1 3.3 %collective-permute-done.2.rest_3_ = f32[8,3072]{1,0:T(8,128)S(1)} collective-permute-done((f32[8,3072]{1,0:T(8,128)}, f32[8,3072]{1,0:T(8,128)S(1)}, u32[]{:S(2)}, u32[]{:S(2)}) %collective-permute-start.2) | collective-permute-done | bytes 98336 | tf_op jit(solution)/shard_map/ppermute | solution.py:308
  49.4 3.7 %collective-permute-done.4.rest_5_ = f32[8,3072]{1,0:T(8,128)S(1)} collective-permute-done((f32[8,3072]{1,0:T(8,128)}, f32[8,3072]{1,0:T(8,128)S(1)}, u32[]{:S(2)}, u32[]{:S(2)}) %collective-permute-start.4) | collective-permute-done | bytes 98336 | tf_op jit(solution)/shard_map/ppermute | solution.py:308
  53.8 4.1 %filter_forward.2 = (f32[1536,128]{1,0:T(8,128)}, f32[1536,128]{1,0:T(8,128)}) custom-call(s32[1]{0:T(128)} %bitcast.core, f32[128,128]{1,0:T(8,128)} %copy.13.vfilter, f32[1,6144,128]{2,1,0:T(8,128)} %perturb.7, f32[8,3072]{1,0:T(8,128)} %get-tuple-element.53.rest_0_, f32[8,3072]{1,0:T(8,128)} %get-tuple-element.54.rest_1_, f32[8,3072]{1,0:T(8,128)} %copy-done.17, ...), custom_call_target="tpu_custom_call" | custom-call | tf_op jit(solution)/shard_map/filter_forward/pallas_call | solution.py:388
  58.0 5.3 %all-to-all-start.1 = ((f32[8,16,3072]{2,1,0:T(8,128)}), f32[8,16,3072]{2,1,0:T(8,128)S(1)}, u32[]{:S(2)}, u32[]{:S(2)}) async-start(f32[8,16,3072]{2,1,0:T(8,128)} %get-tuple-element.72), calls=%async_computation.1 | async-start | bytes 3145728 | tf_op jit(solution)/shard_map/all_to_all | solution.py:420
  67.5 3.2 %compare_select_fusion.slots = s32[1,6144]{1,0:T(1,128)} fusion(pred[]{:T(512)S(6)} %lt.41, s32[1,6144]{1,0:T(1,128)S(1)} %copy-done.37, s32[]{:T(128)S(6)} %select_n.31, s32[]{:T(128)} %bitcast.4), kind=kLoop, calls=%fused_computation.4 | loop fusion | flops 55296 | bytes 49161 | tf_op jit(solution)/shard_map/jit(_where)/select_n | solution.py:344
  70.6 9.1 %observation_weights.2 = f32[1536,128]{1,0:T(8,128)} custom-call(s32[1,6144]{1,0:T(1,128)} %compare_select_fusion.slots, f32[1,6144,128]{2,1,0:T(8,128)} %rinv.3), custom_call_target="tpu_custom_call" | custom-call | tf_op jit(solution)/shard_map/observation_weights/pallas_call | solution.py:369
  79.8 5.8 %collective-permute-done.15 = f32[1536,128]{1,0:T(8,128)S(1)} collective-permute-done((f32[1536,128]{1,0:T(8,128)S(1)}, f32[1536,128]{1,0:T(8,128)S(1)}, u32[]{:S(2)}, u32[]{:S(2)}) %collective-permute-start.15) | collective-permute-done | bytes 786464 | tf_op jit(solution)/shard_map/ppermute | solution.py:426
  90.1 3.6 %filter_backward.2 = f32[8,16,3072]{2,1,0:T(8,128)} custom-call(s32[1]{0:T(128)} %bitcast.core, f32[128,128]{1,0:T(8,128)} %vfilter.2, f32[1,6144,128]{2,1,0:T(8,128)} %perturb.7, f32[1536,128]{1,0:T(8,128)} %copy-done.3, f32[1536,128]{1,0:T(8,128)} %copy-done.5), custom_call_target="tpu_custom_call" | custom-call | tf_op jit(solution)/shard_map/filter_backward/pallas_call | solution.py:404
  93.7 7.2 %all-to-all-done.1.rest_0_ = f32[8,16,3072]{2,1,0:T(8,128)S(1)} async-done(((f32[8,16,3072]{2,1,0:T(8,128)}), f32[8,16,3072]{2,1,0:T(8,128)S(1)}, u32[]{:S(2)}, u32[]{:S(2)}) %all-to-all-start.1) | async-done | bytes 1572896 | tf_op jit(solution)/shard_map/all_to_all | solution.py:420
  102.1 3.7 %filter_forward.3 = (f32[1536,128]{1,0:T(8,128)}, f32[1536,128]{1,0:T(8,128)}) custom-call(s32[1]{0:T(128)} %bitcast.core, f32[128,128]{1,0:T(8,128)} %vfilter.2, f32[1,6144,128]{2,1,0:T(8,128)} %perturb.7, f32[8,16,3072]{2,1,0:T(8,128)} %copy-done.1), custom_call_target="tpu_custom_call" | custom-call | tf_op jit(solution)/shard_map/filter_forward/pallas_call | solution.py:388
  105.8 3.9 %all-to-all-start = ((f32[8,16,3072]{2,1,0:T(8,128)}), f32[8,16,3072]{2,1,0:T(8,128)S(1)}, u32[]{:S(2)}, u32[]{:S(2)}) async-start(f32[8,16,3072]{2,1,0:T(8,128)} %filter_backward.2), calls=%async_computation | async-start | bytes 3145728 | tf_op jit(solution)/shard_map/all_to_all | solution.py:420
  111.4 9.1 %observation_weights.3 = f32[1536,128]{1,0:T(8,128)} custom-call(s32[1,6144]{1,0:T(1,128)} %compare_select_fusion.slots, f32[1,6144,128]{2,1,0:T(8,128)} %rinv.3), custom_call_target="tpu_custom_call" | custom-call | tf_op jit(solution)/shard_map/observation_weights/pallas_call | solution.py:369
  120.5 9.2 %collective-permute-done.18 = f32[1536,128]{1,0:T(8,128)S(1)} collective-permute-done((f32[1536,128]{1,0:T(8,128)S(1)}, f32[1536,128]{1,0:T(8,128)S(1)}, u32[]{:S(2)}, u32[]{:S(2)}) %collective-permute-start.18) | collective-permute-done | bytes 786464 | tf_op jit(solution)/shard_map/ppermute | solution.py:426
  134.2 3.9 %filter_backward.3 = (f32[8,3072]{1,0:T(8,128)}, f32[8,3072]{1,0:T(8,128)}, f32[8,3072]{1,0:T(8,128)}, f32[8,3072]{1,0:T(8,128)}, f32[8,3072]{1,0:T(8,128)}, /*i...) custom-call(s32[1]{0:T(128)} %bitcast.core, ...), custom_call_target="tpu_custom_call" | custom-call | tf_op jit(solution)/shard_map/filter_backward/pallas_call | solution.py:404
  141.9 3.3 %collective-permute-start.27 = (f32[8,3072]{1,0:T(8,128)}, f32[8,3072]{1,0:T(8,128)S(1)}, u32[]{:S(2)}, u32[]{:S(2)}) collective-permute-start(f32[8,3072]{1,0:T(8,128)} %get-tuple-element.86), channel_id=1, source_target_pairs={{0,6},{1,7},{2,4},{3,5},{4,2},{5,3},{6,0},{7,1},{8,14},{9,15},{10,... | collective-permute-start | bytes 294920 | tf_op jit(solution)/shard_map/ppermute | solution.py:308
  146.3 12.2 %collective-permute-done.25.rest_2_ = f32[8,3072]{1,0:T(8,128)S(1)} collective-permute-done((f32[8,3072]{1,0:T(8,128)}, f32[8,3072]{1,0:T(8,128)S(1)}, u32[]{:S(2)}, u32[]{:S(2)}) %collective-permute-start.25) | collective-permute-done | bytes 98336 | tf_op jit(solution)/shard_map/ppermute | solution.py:308
  158.6 3.0 %collective-permute-done.26.rest_3_ = f32[8,3072]{1,0:T(8,128)S(1)} collective-permute-done((f32[8,3072]{1,0:T(8,128)}, f32[8,3072]{1,0:T(8,128)S(1)}, u32[]{:S(2)}, u32[]{:S(2)}) %collective-permute-start.26) | collective-permute-done | bytes 98336 | tf_op jit(solution)/shard_map/ppermute | solution.py:308
  163.5 3.0 %collective-permute-start.21 = (f32[8,3072]{1,0:T(8,128)}, f32[8,3072]{1,0:T(8,128)S(1)}, u32[]{:S(2)}, u32[]{:S(2)}) collective-permute-start(f32[8,3072]{1,0:T(8,128)} %get-tuple-element.77), channel_id=1, source_target_pairs={{0,5},{1,4},{2,7},{3,6},{4,1},{5,0},{6,3},{7,2},{8,13},{9,12},{10,... | collective-permute-start | bytes 294920 | tf_op jit(solution)/shard_map/ppermute | solution.py:308
  171.6 8.6 %place_and_smooth.2.rest_9_ = f32[1,16,128,256]{3,2,1,0:T(8,128)} custom-call(s32[8]{0:T(128)} %widths.6, f32[128,8,256]{2,1,0:T(8,128)} %get-tuple-element.82.diff, f32[8,16,3072]{2,1,0:T(8,128)} %copy-done, f32[8,3072]{1,0:T(8,128)} %get-tuple-element.83.rest_1_, f32[8,3072]{1,0:T(8,128)} %copy-done.25, f32[8,3072]{1,0:T(8,128)} %copy-done.27, ...), custom_call_target="tpu_custom_call" | custom-call | tf_op jit(solution)/shard_map/place_and_smooth/pallas_call | solution.py:454
  187.1 8.6 %place_and_smooth.3 = f32[1,16,128,256]{3,2,1,0:T(8,128)} custom-call(s32[8]{0:T(128)} %widths.6, f32[128,8,256]{2,1,0:T(8,128)} %get-tuple-element.52.diff, f32[8,16,3072]{2,1,0:T(8,128)} %copy-done, f32[8,3072]{1,0:T(8,128)} %get-tuple-element.75.rest_1_, f32[8,3072]{1,0:T(8,128)} %copy-done.9, ...), custom_call_target="tpu_custom_call", output_to_operand_aliasing={{}: (11, {})} | custom-call | tf_op jit(solution)/shard_map/place_and_smooth/pallas_call | solution.py:454
  (158 shorter events, 53.9 us)
Async XLA Ops:
  9.8 10.0 %collective-permute-start = (f32[8,3072]{1,0:T(8,128)}, f32[8,3072]{1,0:T(8,128)S(1)}, u32[]{:S(2)}, u32[]{:S(2)}) collective-permute-start(f32[8,3072]{1,0:T(8,128)} %get-tuple-element.49), channel_id=1, source_target_pairs={{0,1},{1,0},{2,3},{3,2},{4,5},{5,4},{6,7},{7,6},{8,9},{9,8},{10,11... | collective-permute-start | bytes 294920 | tf_op jit(solution)/shard_map/ppermute | solution.py:308
  12.9 19.1 %collective-permute-start.1 = (f32[8,3072]{1,0:T(8,128)}, f32[8,3072]{1,0:T(8,128)S(1)}, u32[]{:S(2)}, u32[]{:S(2)}) collective-permute-start(f32[8,3072]{1,0:T(8,128)} %get-tuple-element.55), channel_id=1, source_target_pairs={{0,4},{1,5},{2,6},{3,7},{4,0},{5,1},{6,2},{7,3},{8,12},{9,13},{10,... | collective-permute-start | bytes 294920 | tf_op jit(solution)/shard_map/ppermute | solution.py:308
  15.5 16.6 %collective-permute-start.11 = (f32[8,3072]{1,0:T(8,128)}, f32[8,3072]{1,0:T(8,128)S(1)}, u32[]{:S(2)}, u32[]{:S(2)}) collective-permute-start(f32[8,3072]{1,0:T(8,128)} %get-tuple-element.65), channel_id=1, source_target_pairs={{0,2},{1,3},{2,0},{3,1},{4,6},{5,7},{6,4},{7,5},{8,10},{9,11},{10,... | collective-permute-start | bytes 294920 | tf_op jit(solution)/shard_map/ppermute | solution.py:308
  17.0 18.0 %collective-permute-start.3 = (f32[8,3072]{1,0:T(8,128)}, f32[8,3072]{1,0:T(8,128)S(1)}, u32[]{:S(2)}, u32[]{:S(2)}) collective-permute-start(f32[8,3072]{1,0:T(8,128)} %get-tuple-element.57), channel_id=1, source_target_pairs={{0,5},{1,4},{2,7},{3,6},{4,1},{5,0},{6,3},{7,2},{8,13},{9,12},{10,... | collective-permute-start | bytes 294920 | tf_op jit(solution)/shard_map/ppermute | solution.py:308
  17.3 17.9 %collective-permute-start.5 = (f32[8,3072]{1,0:T(8,128)}, f32[8,3072]{1,0:T(8,128)S(1)}, u32[]{:S(2)}, u32[]{:S(2)}) collective-permute-start(f32[8,3072]{1,0:T(8,128)} %get-tuple-element.59), channel_id=1, source_target_pairs={{0,6},{1,7},{2,4},{3,5},{4,2},{5,3},{6,0},{7,1},{8,14},{9,15},{10,... | collective-permute-start | bytes 294920 | tf_op jit(solution)/shard_map/ppermute | solution.py:308
  19.8 16.1 %collective-permute-start.7 = (f32[8,3072]{1,0:T(8,128)}, f32[8,3072]{1,0:T(8,128)S(1)}, u32[]{:S(2)}, u32[]{:S(2)}) collective-permute-start(f32[8,3072]{1,0:T(8,128)} %get-tuple-element.61), channel_id=1, source_target_pairs={{0,7},{1,6},{2,5},{3,4},{4,3},{5,2},{6,1},{7,0},{8,15},{9,14},{10,... | collective-permute-start | bytes 294920 | tf_op jit(solution)/shard_map/ppermute | solution.py:308
  35.2 10.9 %collective-permute-start.13 = (f32[8,3072]{1,0:T(8,128)}, f32[8,3072]{1,0:T(8,128)S(1)}, u32[]{:S(2)}, u32[]{:S(2)}) collective-permute-start(f32[8,3072]{1,0:T(8,128)} %get-tuple-element.67), channel_id=1, source_target_pairs={{0,1},{1,0},{2,3},{3,2},{4,5},{5,4},{6,7},{7,6},{8,9},{9,8},{10,11... | collective-permute-start | bytes 294920 | tf_op jit(solution)/shard_map/ppermute | solution.py:308
  35.9 13.5 %collective-permute-start.2 = (f32[8,3072]{1,0:T(8,128)}, f32[8,3072]{1,0:T(8,128)S(1)}, u32[]{:S(2)}, u32[]{:S(2)}) collective-permute-start(f32[8,3072]{1,0:T(8,128)} %get-tuple-element.56), channel_id=1, source_target_pairs={{0,4},{1,5},{2,6},{3,7},{4,0},{5,1},{6,2},{7,3},{8,12},{9,13},{10,... | collective-permute-start | bytes 294920 | tf_op jit(solution)/shard_map/ppermute | solution.py:308
  39.0 14.0 %collective-permute-start.4 = (f32[8,3072]{1,0:T(8,128)}, f32[8,3072]{1,0:T(8,128)S(1)}, u32[]{:S(2)}, u32[]{:S(2)}) collective-permute-start(f32[8,3072]{1,0:T(8,128)} %get-tuple-element.58), channel_id=1, source_target_pairs={{0,5},{1,4},{2,7},{3,6},{4,1},{5,0},{6,3},{7,2},{8,13},{9,12},{10,... | collective-permute-start | bytes 294920 | tf_op jit(solution)/shard_map/ppermute | solution.py:308
  40.2 12.9 %collective-permute-start.6 = (f32[8,3072]{1,0:T(8,128)}, f32[8,3072]{1,0:T(8,128)S(1)}, u32[]{:S(2)}, u32[]{:S(2)}) collective-permute-start(f32[8,3072]{1,0:T(8,128)} %get-tuple-element.60), channel_id=1, source_target_pairs={{0,6},{1,7},{2,4},{3,5},{4,2},{5,3},{6,0},{7,1},{8,14},{9,15},{10,... | collective-permute-start | bytes 294920 | tf_op jit(solution)/shard_map/ppermute | solution.py:308
  58.0 42.9 %all-to-all-start.1 = ((f32[8,16,3072]{2,1,0:T(8,128)}), f32[8,16,3072]{2,1,0:T(8,128)S(1)}, u32[]{:S(2)}, u32[]{:S(2)}) async-start(f32[8,16,3072]{2,1,0:T(8,128)} %get-tuple-element.72), calls=%async_computation.1 | async-start | bytes 3145728 | tf_op jit(solution)/shard_map/all_to_all | solution.py:420
  65.9 19.7 %collective-permute-start.15 = (f32[1536,128]{1,0:T(8,128)S(1)}, f32[1536,128]{1,0:T(8,128)S(1)}, u32[]{:S(2)}, u32[]{:S(2)}) collective-permute-start(f32[1536,128]{1,0:T(8,128)S(1)} %add.32), channel_id=1, source_target_pairs={{0,16},{8,24},{16,0},{24,8},{1,17},{9,25},{17,1},{25,9},{2,18},{10... | collective-permute-start | bytes 2359304 | tf_op jit(solution)/shard_map/ppermute | solution.py:426
  105.8 64.7 %all-to-all-start = ((f32[8,16,3072]{2,1,0:T(8,128)}), f32[8,16,3072]{2,1,0:T(8,128)S(1)}, u32[]{:S(2)}, u32[]{:S(2)}) async-start(f32[8,16,3072]{2,1,0:T(8,128)} %filter_backward.2), calls=%async_computation | async-start | bytes 3145728 | tf_op jit(solution)/shard_map/all_to_all | solution.py:420
  109.8 19.9 %collective-permute-start.18 = (f32[1536,128]{1,0:T(8,128)S(1)}, f32[1536,128]{1,0:T(8,128)S(1)}, u32[]{:S(2)}, u32[]{:S(2)}) collective-permute-start(f32[1536,128]{1,0:T(8,128)S(1)} %add.36), channel_id=1, source_target_pairs={{0,16},{8,24},{16,0},{24,8},{1,17},{9,25},{17,1},{25,9},{2,18},{10... | collective-permute-start | bytes 2359304 | tf_op jit(solution)/shard_map/ppermute | solution.py:426
  138.1 20.5 %collective-permute-start.25 = (f32[8,3072]{1,0:T(8,128)}, f32[8,3072]{1,0:T(8,128)S(1)}, u32[]{:S(2)}, u32[]{:S(2)}) collective-permute-start(f32[8,3072]{1,0:T(8,128)} %get-tuple-element.84), channel_id=1, source_target_pairs={{0,4},{1,5},{2,6},{3,7},{4,0},{5,1},{6,2},{7,3},{8,12},{9,13},{10,... | collective-permute-start | bytes 294920 | tf_op jit(solution)/shard_map/ppermute | solution.py:308
  140.5 21.0 %collective-permute-start.26 = (f32[8,3072]{1,0:T(8,128)}, f32[8,3072]{1,0:T(8,128)S(1)}, u32[]{:S(2)}, u32[]{:S(2)}) collective-permute-start(f32[8,3072]{1,0:T(8,128)} %get-tuple-element.85), channel_id=1, source_target_pairs={{0,5},{1,4},{2,7},{3,6},{4,1},{5,0},{6,3},{7,2},{8,13},{9,12},{10,... | collective-permute-start | bytes 294920 | tf_op jit(solution)/shard_map/ppermute | solution.py:308
  141.9 20.2 %collective-permute-start.27 = (f32[8,3072]{1,0:T(8,128)}, f32[8,3072]{1,0:T(8,128)S(1)}, u32[]{:S(2)}, u32[]{:S(2)}) collective-permute-start(f32[8,3072]{1,0:T(8,128)} %get-tuple-element.86), channel_id=1, source_target_pairs={{0,6},{1,7},{2,4},{3,5},{4,2},{5,3},{6,0},{7,1},{8,14},{9,15},{10,... | collective-permute-start | bytes 294920 | tf_op jit(solution)/shard_map/ppermute | solution.py:308
  145.2 18.2 %collective-permute-start.28 = (f32[8,3072]{1,0:T(8,128)}, f32[8,3072]{1,0:T(8,128)S(1)}, u32[]{:S(2)}, u32[]{:S(2)}) collective-permute-start(f32[8,3072]{1,0:T(8,128)} %get-tuple-element.87), channel_id=1, source_target_pairs={{0,7},{1,6},{2,5},{3,4},{4,3},{5,2},{6,1},{7,0},{8,15},{9,14},{10,... | collective-permute-start | bytes 294920 | tf_op jit(solution)/shard_map/ppermute | solution.py:308
  145.8 20.8 %collective-permute-start.29 = (f32[8,3072]{1,0:T(8,128)}, f32[8,3072]{1,0:T(8,128)S(1)}, u32[]{:S(2)}, u32[]{:S(2)}) collective-permute-start(f32[8,3072]{1,0:T(8,128)} %get-tuple-element.88), channel_id=1, source_target_pairs={{0,3},{1,2},{2,1},{3,0},{4,7},{5,6},{6,5},{7,4},{8,11},{9,10},{10,... | collective-permute-start | bytes 294920 | tf_op jit(solution)/shard_map/ppermute | solution.py:308
  162.1 18.1 %collective-permute-start.20 = (f32[8,3072]{1,0:T(8,128)}, f32[8,3072]{1,0:T(8,128)S(1)}, u32[]{:S(2)}, u32[]{:S(2)}) collective-permute-start(f32[8,3072]{1,0:T(8,128)} %get-tuple-element.76), channel_id=1, source_target_pairs={{0,4},{1,5},{2,6},{3,7},{4,0},{5,1},{6,2},{7,3},{8,12},{9,13},{10,... | collective-permute-start | bytes 294920 | tf_op jit(solution)/shard_map/ppermute | solution.py:308
  163.5 18.3 %collective-permute-start.21 = (f32[8,3072]{1,0:T(8,128)}, f32[8,3072]{1,0:T(8,128)S(1)}, u32[]{:S(2)}, u32[]{:S(2)}) collective-permute-start(f32[8,3072]{1,0:T(8,128)} %get-tuple-element.77), channel_id=1, source_target_pairs={{0,5},{1,4},{2,7},{3,6},{4,1},{5,0},{6,3},{7,2},{8,13},{9,12},{10,... | collective-permute-start | bytes 294920 | tf_op jit(solution)/shard_map/ppermute | solution.py:308
  166.5 17.3 %collective-permute-start.22 = (f32[8,3072]{1,0:T(8,128)}, f32[8,3072]{1,0:T(8,128)S(1)}, u32[]{:S(2)}, u32[]{:S(2)}) collective-permute-start(f32[8,3072]{1,0:T(8,128)} %get-tuple-element.78), channel_id=1, source_target_pairs={{0,6},{1,7},{2,4},{3,5},{4,2},{5,3},{6,0},{7,1},{8,14},{9,15},{10,... | collective-permute-start | bytes 294920 | tf_op jit(solution)/shard_map/ppermute | solution.py:308
  168.1 15.8 %collective-permute-start.23 = (f32[8,3072]{1,0:T(8,128)}, f32[8,3072]{1,0:T(8,128)S(1)}, u32[]{:S(2)}, u32[]{:S(2)}) collective-permute-start(f32[8,3072]{1,0:T(8,128)} %get-tuple-element.79), channel_id=1, source_target_pairs={{0,7},{1,6},{2,5},{3,4},{4,3},{5,2},{6,1},{7,0},{8,15},{9,14},{10,... | collective-permute-start | bytes 294920 | tf_op jit(solution)/shard_map/ppermute | solution.py:308
  170.4 13.5 %collective-permute-start.24 = (f32[8,3072]{1,0:T(8,128)}, f32[8,3072]{1,0:T(8,128)S(1)}, u32[]{:S(2)}, u32[]{:S(2)}) collective-permute-start(f32[8,3072]{1,0:T(8,128)} %get-tuple-element.80), channel_id=1, source_target_pairs={{0,3},{1,2},{2,1},{3,0},{4,7},{5,6},{6,5},{7,4},{8,11},{9,10},{10,... | collective-permute-start | bytes 294920 | tf_op jit(solution)/shard_map/ppermute | solution.py:308
  (56 other events, 395.8 us)

commit v6 on v5

--- a/solution.py
+++ b/solution.py
@@ -94,13 +94,18 @@
     return lax.fori_loop(0, j, lambda k, total: total + widths[k], jnp.int32(0))
 
 
-def turns_of(groups):
-    return [0] + list(range(groups // 2, groups)) + list(range(groups // 2 - 1, 0, -1))
-
-
-def forward_kernel(size_x, size_y, groups, widths, control, diffusivity, *rest):
+def turns_in(groups):
+    return list(range(groups))
+
+
+def turns_out(groups, last):
+    near, far = list(range(groups // 2 - 1, 1, -1)), list(range(groups // 2, groups))
+    return [0, 1] + far + near if last else [0] + far + near + [1]
+
+
+def forward_kernel(size_x, size_y, groups, n_sooner, widths, control, diffusivity, *rest):
     *rest, flat, one, two, face_x, face_up, face_down = rest
-    diff_out, later, *sooner = rest[-groups - 2 :]
+    diff_out, later, *sooner = rest[-n_sooner - 2 :]
     face_refs = (face_x, face_up, face_down)
     columns = size_x * size_y
     part = later.shape[2]
@@ -134,15 +139,16 @@
             store(t, jnp.where(low, now, following))
             now = following
 
-    for d, turn in enumerate(turns_of(groups)):
+    for d, turn in enumerate(turns_in(groups)):
 
         def store_sooner(t, value):
-            sooner[d][:, t * LANES : (t + 1) * LANES] = value
+            target = sooner[d] if n_sooner == groups else sooner[0].at[d]
+            target[:, t * LANES : (t + 1) * LANES] = value
 
         def store_later(t, value):
             later[d, :, t * LANES : (t + 1) * LANES] = value
 
-        cut(jnp.bitwise_xor(me, turn), 0, store_sooner)
+        cut(jnp.bitwise_xor(me, turn) if n_sooner == groups else d, 0, store_sooner)
         cut(d, 1, store_later)
 
 
@@ -198,8 +204,9 @@
         send[...] = result
 
 
-def back_kernel(core, vfilter, perturb, adj_mine, adj_other, *rest):
-    *pieces, table = rest
+def back_kernel(n_adj, core, vfilter, perturb, *rest):
+    adj_mine, adj_other = rest[:n_adj], rest[n_adj : 2 * n_adj]
+    *pieces, table = rest[2 * n_adj :]
     levels = vfilter.shape[0]
     step = pl.program_id(0)
     blocks = pl.num_programs(0) // 2
@@ -212,7 +219,7 @@
         table[:levels, levels:] = low
         table[levels:, levels:] = jnp.zeros_like(low)
 
-    adj = jnp.where(step < blocks, adj_mine[...], adj_other[...])
+    adj = jnp.concatenate([jnp.where(step < blocks, a[...], b[...]) for a, b in zip(adj_mine, adj_other)], axis=0)
     both = jnp.concatenate(split2(perturb[0] * adj), axis=1)
     products = jnp.dot(both, table[...], preferred_element_type=F32)
     result = (products[:, :levels] + products[:, levels:]).T
@@ -223,7 +230,7 @@
         first += count
 
 
-def backward_kernel(size_x, size_y, groups, capacity, group, widths, diff, *rest):
+def backward_kernel(size_x, size_y, groups, capacity, group, last, widths, diff, *rest):
     *rest, staging, flat, one, two, face_x, face_up, face_down, sem = rest
     face_refs = (face_x, face_up, face_down)
     sooner, *later = rest[: groups + 1]
@@ -235,12 +242,10 @@
             sooner.at[:, pl.ds(group * GROUP, GROUP), :], staging.at[:, :, pl.ds(0, part)], sem.at[0]
         )
     ]
-    for d, turn in enumerate(turns_of(groups)):
-        copies.append(
-            pltpu.make_async_copy(
-                later[d], staging.at[jnp.bitwise_xor(me, turn), :, pl.ds(part, part)], sem.at[1 + d]
-            )
-        )
+    late = pl.ds(part, part)
+    targets = [staging.at[jnp.bitwise_xor(me, turn), :, late] for turn in turns_out(groups, last)]
+    for d in range(groups):
+        copies.append(pltpu.make_async_copy(later[d], targets[d], sem.at[1 + d]))
     for copy in copies:
         copy.start()
     faces(diff, *face_refs, size_x, size_y)
@@ -300,19 +305,22 @@
     flat_width = columns + capacity + LANES
     piece_shape = jax.ShapeDtypeStruct((GROUP, part), F32)
     pieces_shape = jax.ShapeDtypeStruct((groups, levels_here, part), F32)
+    group_shape = jax.ShapeDtypeStruct((groups, GROUP, part), F32)
     n_groups = levels_here // GROUP
     any_spec = pl.BlockSpec(memory_space=pl.ANY)
-    turns = turns_of(groups)
-
-    def permute(piece, d):
-        return lax.ppermute(piece, "lev", flip_pairs(groups, turns[d])) if d else piece
-
-    diffs, later, got = [], None, {}
-    widths = sub_widths
+
+    def exchange(pieces):
+        return lax.all_to_all(pieces, "lev", 0, 0, tiled=True)
+
+    def permute(piece, turn):
+        return lax.ppermute(piece, "lev", flip_pairs(groups, turn)) if turn else piece
+
+    diffs, later, got = [], None, []
     for group in range(n_groups):
         before = [] if later is None else [later]
+        n_sooner = groups if group else 1
         results = pl.pallas_call(
-            functools.partial(forward_kernel, size_x, size_y, groups),
+            functools.partial(forward_kernel, size_x, size_y, groups, n_sooner),
             grid=(1,),
             in_specs=[
                 smem,
@@ -324,27 +332,39 @@
                 pl.BlockSpec((size_x, GROUP, size_y), lambda g: (0, 0, 0)),
                 pl.BlockSpec((groups, GROUP, part), lambda g, group=group: (0, group, 0)),
             ]
-            + [pl.BlockSpec((GROUP, part), lambda g: (0, 0))] * groups,
-            out_shape=[jax.ShapeDtypeStruct((size_x, GROUP, size_y), F32), pieces_shape] + [piece_shape] * groups,
+            + (
+                [pl.BlockSpec((GROUP, part), lambda g: (0, 0))] * groups
+                if group
+                else [pl.BlockSpec((groups, GROUP, part), lambda g: (0, 0, 0))]
+            ),
+            out_shape=[jax.ShapeDtypeStruct((size_x, GROUP, size_y), F32), pieces_shape]
+            + ([piece_shape] * groups if group else [group_shape]),
             input_output_aliases={3: 1} if before else {},
             scratch_shapes=[pltpu.VMEM((GROUP, flat_width), F32)]
             + [pltpu.VMEM((size_x, GROUP, size_y), F32)] * 5,
             compiler_params=params,
             cost_estimate=pl.CostEstimate(flops=0, bytes_accessed=0, transcendentals=0),
             name="smooth_and_cut",
-        )(widths, control, diffusivity, *before)
+        )(sub_widths, control, diffusivity, *before)
         diffs.append(results[0])
         later = results[1]
-        for d in range(groups):
-            got[d, group] = permute(results[2 + d], d)
-        widths = after(sub_widths, got[7, group])
+        if group:
+            got += [permute(piece, turn) for piece, turn in zip(results[2:], turns_in(groups))]
+        else:
+            got.append(exchange(results[2]))
 
     width = sub_widths[me]
     live = jnp.arange(obs_cap, dtype=jnp.int32) < obs_counts[me]
     slots = jnp.where(live, obs_raw[0] % width, -1)[None, :]
 
-    order = jnp.bitwise_xor(me, jnp.array(turns, jnp.int32))
-    turned = vertical_filter.reshape(levels, groups, levels_here)[:, order, :].reshape(levels, levels)
+    by_group = vertical_filter.reshape(levels, groups, n_groups, GROUP)
+    def reordered(orders):
+        places = [jnp.bitwise_xor(me, jnp.array(order, jnp.int32)) if order else jnp.arange(groups) for order in orders]
+        return jnp.concatenate([by_group[:, at, g].reshape(levels, -1) for g, at in enumerate(places)], axis=1)
+
+    last = n_groups - 1
+    filter_in = reordered([turns_in(groups) if g else None for g in range(n_groups)])
+    filter_out = reordered([turns_out(groups, g == last) for g in range(n_groups)])
 
     width = half
     blocks = part // width
@@ -356,7 +376,8 @@
     square = pl.BlockSpec((levels, levels), lambda g, core: (0, 0))
     slab = pl.BlockSpec((groups, levels_here, width), lambda g, core: (0, 0, block_of(g, core)))
     strip = pl.BlockSpec((GROUP, width), lambda g, core: (0, block_of(g, core)))
-    n_strips = groups * n_groups
+    group_slab = pl.BlockSpec((groups, GROUP, width), lambda g, core: (0, 0, block_of(g, core)))
+    strips_in = [group_slab] + [strip] * (groups * (n_groups - 1))
     first_half = pl.BlockSpec((width, levels), lambda g, core: (jnp.minimum(g, some - 1), 0))
     second_half = pl.BlockSpec((width, levels), lambda g, core: (jnp.maximum(g - some, 0), 0))
     half_shape = jax.ShapeDtypeStruct((half, levels), F32)
@@ -390,7 +411,7 @@
             grid_spec=pltpu.PrefetchScalarGridSpec(
                 num_scalar_prefetch=1,
                 grid=(blocks,),
-                in_specs=[square, perturb_part(c)] + ([slab] if len(pieces) == 1 else [strip] * n_strips),
+                in_specs=[square, perturb_part(c)] + ([slab] if len(pieces) == 1 else strips_in),
                 out_specs=[first_half, second_half],
                 scratch_shapes=[table],
             ),
@@ -402,63 +423,60 @@
 
     def filter_backward(c, vfilter, adj_mine, adj_other, strips):
         return pl.pallas_call(
-            back_kernel,
+            functools.partial(back_kernel, len(adj_mine)),
             grid_spec=pltpu.PrefetchScalarGridSpec(
                 num_scalar_prefetch=1,
                 grid=(blocks,),
-                in_specs=[square, perturb_part(c), first_half, second_half],
-                out_specs=[strip] * n_strips if strips else [slab],
+                in_specs=[square, perturb_part(c)]
+                + [pl.BlockSpec(adj.shape, lambda g, core: (0, 0)) for adj in adj_mine + adj_other],
+                out_specs=[strip] * (groups * n_groups) if strips else [slab],
                 scratch_shapes=[table],
             ),
-            out_shape=[piece_shape] * n_strips if strips else [pieces_shape],
+            out_shape=[piece_shape] * (groups * n_groups) if strips else [pieces_shape],
             compiler_params=params,
             cost_estimate=cost,
             name="filter_backward",
-        )(core, vfilter, perturb, adj_mine, adj_other)
-
-    def exchange(pieces):
-        return lax.all_to_all(pieces, "lev", 0, 0, tiled=True)
-
-    def sum_members(keep, send):
-        total = keep + lax.ppermute(send, "mem", flip_pairs(n_mem, 1))
-        bit = 2
-        while bit < n_mem:
-            total = total + lax.ppermute(total, "mem", flip_pairs(n_mem, bit))
-            bit *= 2
-        return total
-
-    def adjoint(total, obs_weight):
-        mine = total * obs_weight
-        return mine, lax.ppermute(mine, "mem", flip_pairs(n_mem, 1))
-
-    in_order = [(d, group) for d in range(groups) for group in range(n_groups)]
-    slots = after(slots, got[1, 0])
+        )(core, vfilter, perturb, *adj_mine, *adj_other)
+
+    def member_sum(keep, send, obs_weight, pieces):
+        mine, other = [], []
+        for first in range(0, half, half // pieces):
+            here = slice(first, first + half // pieces)
+            total = keep[here] + lax.ppermute(send[here], "mem", flip_pairs(n_mem, 1))
+            bit = 2
+            while bit < n_mem:
+                total = total + lax.ppermute(total, "mem", flip_pairs(n_mem, bit))
+                bit *= 2
+            mine.append(total * obs_weight[here])
+            other.append(lax.ppermute(mine[-1], "mem", flip_pairs(n_mem, 1)))
+        return mine, other
+
+    slots = after(slots, got[1], filter_out)
     weight = [weights(c, slots) for c in range(PARTS)]
     got_later = exchange(later)
 
-    keep, send = filter_forward(0, turned, *[got[key] for key in in_order])
-    mine, other = adjoint(sum_members(keep, send), weight[0])
+    keep, send = filter_forward(0, filter_in, *got)
+    mine, other = member_sum(keep, send, weight[0], 1)
     pieces = filter_backward(0, vertical_filter, mine, other, False)[0]
     back_sooner = exchange(pieces)
 
     keep, send = filter_forward(1, after(vertical_filter, pieces), got_later)
-    mine, other = adjoint(sum_members(keep, send), weight[1])
-    pieces = filter_backward(1, turned, mine, other, True)
+    mine, other = member_sum(keep, send, weight[1], 2)
+    pieces = filter_backward(1, filter_out, mine, other, True)
     out = None
     for group in range(n_groups):
         before = [] if out is None else [out]
         back = []
-        for d in range(groups):
-            piece = pieces[in_order.index((d, group))]
-            back.append(permute(after(piece, out) if before and d in (6,) else piece, d))
+        for piece, turn in zip(pieces[group * groups :], turns_out(groups, group == last)):
+            back.append(permute(after(piece, out) if before and turn == 2 else piece, turn))
         out = pl.pallas_call(
-            functools.partial(backward_kernel, size_x, size_y, groups, capacity, group),
+            functools.partial(backward_kernel, size_x, size_y, groups, capacity, group, group == last),
             grid=(1,),
             in_specs=[smem, pl.BlockSpec((size_x, GROUP, size_y), lambda g: (0, 0, 0))]
-            + [any_spec] * (1 + groups + len(before)),
+            + [any_spec] * (1 + len(back) + len(before)),
             out_specs=pl.BlockSpec((1, GROUP, size_x, size_y), lambda g, group=group: (0, group, 0, 0)),
             out_shape=jax.ShapeDtypeStruct((members, levels_here, size_x, size_y), F32),
-            input_output_aliases={3 + groups: 0} if before else {},
+            input_output_aliases={3 + len(back): 0} if before else {},
             scratch_shapes=[
                 pltpu.VMEM((groups, GROUP, capacity), F32),
                 pltpu.VMEM((GROUP, flat_width), F32),

time: 196 us -> 194 us (0.990)
  waiting for transfers between devices: 52.1 us -> 48.9 us
  starting transfers between devices: 57.4 us -> 54.5 us
  other arithmetic: 5.85 us -> 8.31 us
    ppermute x34 -> x30, starting transfers between devices: 48.3 us -> 38.3 us  [the longest x21 33.4 us: permute(): lax.ppermute(piece, 'lev', flip_pairs(groups, turn))]
    all_to_all x2 -> x3, starting transfers between devices: 9.17 us -> 16.2 us  [exchange(): return lax.all_to_all(pieces, 'lev', 0, 0, tiled=True)]
    all_to_all x2 -> x3, waiting for transfers between devices: 7.22 us -> 4.22 us  [exchange(): return lax.all_to_all(pieces, 'lev', 0, 0, tiled=True)]
    unnamed x89 -> x85, local copies, waits for them, and re-layouts: 5.45 us -> 4.66 us
    ppermute x34 -> x30, waiting for transfers between devices: 44.9 us -> 44.7 us  [the longest x21 24.5 us: permute(): lax.ppermute(piece, 'lev', flip_pairs(groups, turn))]
  transfers between devices with their start and end apart: 36 -> 33, of which waited for: 13 -> 15; matrix products, arithmetic and copies ran while one was open for 4% -> 7% of each run, Pallas kernels for 23% -> 25%
where the time goes in v6:
time: 194 us
  Pallas kernels  70.2 us (36%)
  starting transfers between devices  54.5 us (28%)
  waiting for transfers between devices  48.9 us (25%)
  local copies, waits for them, and re-layouts  9.71 us (5%)
  other arithmetic  8.31 us (4%)
    ppermute x21, starting transfers between devices, permute(): lax.ppermute(piece, 'lev', flip_pairs(groups, turn))  33.4 us
    ppermute x21, waiting for transfers between devices, permute(): lax.ppermute(piece, 'lev', flip_pairs(groups, turn))  24.5 us
    pallas_call x2, Pallas kernels, body(): pl.pallas_call(functools.partial(forward_kernel, size_x, size_y, groups,...  19.7 us
    pallas_call x2, Pallas kernels, weights(): pl.pallas_call(functools.partial(observation_kernel, part, c, obs_cap), g...  18.2 us
    pallas_call x2, Pallas kernels, body(): pl.pallas_call(functools.partial(backward_kernel, size_x, size_y, groups,...  17.2 us
    all_to_all x3, starting transfers between devices, exchange(): return lax.all_to_all(pieces, 'lev', 0, 0, tiled=True)  16.2 us
    ppermute x3, waiting for transfers between devices, member_sum(): total = total + lax.ppermute(total, 'mem', flip_pairs(n_mem, bit))  14.3 us
    pallas_call x2, Pallas kernels, filter_forward(): pl.pallas_call(filter_kernel, grid_spec=pltpu.PrefetchScalarGridSpec(num_...  7.6 us
  transfers between devices with their start and end apart: 33, of which 15 were waited for; matrix products, arithmetic and copies ran while one was open for 7% of the time, Pallas kernels for 25%

profile of v6, /device:TPU:0, one launch (start us, length us, event | category | flops | bytes accessed | tf_op | source)
XLA Modules:
  0.0 193.5 jit_solution(6785460811328664017)
XLA Ops:
  0.0 9.8 %smooth_and_cut.2 = (f32[128,8,256]{2,1,0:T(8,128)}, f32[8,16,3072]{2,1,0:T(8,128)}, f32[8,8,3072]{2,1,0:T(8,128)}) custom-call(s32[8]{0:T(128)} %widths.7, f32[1,16,128,256]{3,2,1,0:T(8,128)} %control.3, f32[16,128,256]{2,1,0:T(8,128)} %diffusivity.3), custom_call_target="tpu_custom_call" | custom-call | tf_op jit(solution)/shard_map/smooth_and_cut/pallas_call | solution.py:322
  9.8 7.3 %all-to-all-start = ((f32[8,8,3072]{2,1,0:T(8,128)}), f32[8,8,3072]{2,1,0:T(8,128)S(1)}, u32[]{:S(2)}, u32[]{:S(2)}) async-start(f32[8,8,3072]{2,1,0:T(8,128)} %get-tuple-element.43), calls=%async_computation | async-start | bytes 1572864 | tf_op jit(solution)/shard_map/all_to_all | solution.py:313
  17.1 9.9 %smooth_and_cut.3 = (f32[128,8,256]{2,1,0:T(8,128)}, f32[8,16,3072]{2,1,0:T(8,128)}, f32[8,3072]{1,0:T(8,128)}, f32[8,3072]{1,0:T(8,128)}, f32[8,3072]{1,0:T(8,1...) custom-call(s32[8]{0:T(128)} %widths.7, ...), custom_call_target="tpu_custom_call", output_to_operand_aliasing={{1}: (3, {})} | custom-call | tf_op jit(solution)/shard_map/smooth_and_cut/pallas_call | solution.py:322
  36.4 3.3 %collective-permute-start.5 = (f32[8,3072]{1,0:T(8,128)S(1)}, f32[8,3072]{1,0:T(8,128)S(1)}, u32[]{:S(2)}, u32[]{:S(2)}) collective-permute-start(f32[8,3072]{1,0:T(8,128)S(1)} %copy-done.39), channel_id=1, source_target_pairs={{0,6},{1,7},{2,4},{3,5},{4,2},{5,3},{6,0},{7,1},{8,14},{9,15},{10,... | collective-permute-start | bytes 294920 | tf_op jit(solution)/shard_map/ppermute | solution.py:316
  40.6 8.6 %collective-permute-done.3.rest_5_ = f32[8,3072]{1,0:T(8,128)S(1)} collective-permute-done((f32[8,3072]{1,0:T(8,128)}, f32[8,3072]{1,0:T(8,128)S(1)}, u32[]{:S(2)}, u32[]{:S(2)}) %collective-permute-start.3) | collective-permute-done | bytes 98336 | tf_op jit(solution)/shard_map/ppermute | solution.py:316
  52.7 3.9 %filter_forward.2 = (f32[1536,128]{1,0:T(8,128)}, f32[1536,128]{1,0:T(8,128)}) custom-call(s32[1]{0:T(128)} %bitcast.core, f32[128,128]{1,0:T(8,128)} %pad_maximum_fusion.vfilter, f32[1,6144,128]{2,1,0:T(8,128)} %perturb.7, f32[8,8,3072]{2,1,0:T(8,128)} %copy-done.2, f32[8,3072]{1,0:T(8,128)} %get-tuple-element.44.rest_1_, f32[8,3072]{1,0:T(8,128)} %copy-done.19, ...), custom_call_target="tpu_custom_call" | custom-call | tf_op jit(solution)/shard_map/filter_forward/pallas_call | solution.py:409
  56.7 5.2 %all-to-all-start.2 = ((f32[8,16,3072]{2,1,0:T(8,128)}), f32[8,16,3072]{2,1,0:T(8,128)S(1)}, u32[]{:S(2)}, u32[]{:S(2)}) async-start(f32[8,16,3072]{2,1,0:T(8,128)} %get-tuple-element.56), calls=%async_computation.2 | async-start | bytes 3145728 | tf_op jit(solution)/shard_map/all_to_all | solution.py:313
  72.3 9.1 %observation_weights.2 = f32[1536,128]{1,0:T(8,128)} custom-call(s32[1,6144]{1,0:T(1,128)} %compare_select_fusion.slots, f32[1,6144,128]{2,1,0:T(8,128)} %rinv.3), custom_call_target="tpu_custom_call" | custom-call | tf_op jit(solution)/shard_map/observation_weights/pallas_call | solution.py:390
  81.4 5.9 %collective-permute-done.8 = f32[1536,128]{1,0:T(8,128)S(1)} collective-permute-done((f32[1536,128]{1,0:T(8,128)S(1)}, f32[1536,128]{1,0:T(8,128)S(1)}, u32[]{:S(2)}, u32[]{:S(2)}) %collective-permute-start.8) | collective-permute-done | bytes 786464 | tf_op jit(solution)/shard_map/ppermute | solution.py:448
  91.8 3.6 %filter_backward.2 = f32[8,16,3072]{2,1,0:T(8,128)} custom-call(s32[1]{0:T(128)} %bitcast.core, f32[128,128]{1,0:T(8,128)} %vfilter.2, f32[1,6144,128]{2,1,0:T(8,128)} %perturb.7, f32[1536,128]{1,0:T(8,128)} %copy-done.3, f32[1536,128]{1,0:T(8,128)} %copy-done.6), custom_call_target="tpu_custom_call" | custom-call | tf_op jit(solution)/shard_map/filter_backward/pallas_call | solution.py:425
  95.4 4.2 %all-to-all-done.2.rest_0_ = f32[8,16,3072]{2,1,0:T(8,128)S(1)} async-done(((f32[8,16,3072]{2,1,0:T(8,128)}), f32[8,16,3072]{2,1,0:T(8,128)S(1)}, u32[]{:S(2)}, u32[]{:S(2)}) %all-to-all-start.2) | async-done | bytes 1572896 | tf_op jit(solution)/shard_map/all_to_all | solution.py:313
  99.6 3.8 %all-to-all-start.1 = ((f32[8,16,3072]{2,1,0:T(8,128)}), f32[8,16,3072]{2,1,0:T(8,128)S(1)}, u32[]{:S(2)}, u32[]{:S(2)}) async-start(f32[8,16,3072]{2,1,0:T(8,128)} %filter_backward.2), calls=%async_computation.1 | async-start | bytes 3145728 | tf_op jit(solution)/shard_map/all_to_all | solution.py:313
  103.4 3.7 %filter_forward.3 = (f32[1536,128]{1,0:T(8,128)}, f32[1536,128]{1,0:T(8,128)}) custom-call(s32[1]{0:T(128)} %bitcast.core, f32[128,128]{1,0:T(8,128)} %vfilter.2, f32[1,6144,128]{2,1,0:T(8,128)} %perturb.7, f32[8,16,3072]{2,1,0:T(8,128)} %copy-done.1), custom_call_target="tpu_custom_call" | custom-call | tf_op jit(solution)/shard_map/filter_forward/pallas_call | solution.py:409
  112.9 9.1 %observation_weights.3 = f32[1536,128]{1,0:T(8,128)} custom-call(s32[1,6144]{1,0:T(1,128)} %compare_select_fusion.slots, f32[1,6144,128]{2,1,0:T(8,128)} %rinv.3), custom_call_target="tpu_custom_call" | custom-call | tf_op jit(solution)/shard_map/observation_weights/pallas_call | solution.py:390
  122.8 7.6 %collective-permute-done.13 = f32[768,128]{1,0:T(8,128)S(1)} collective-permute-done((f32[768,128]{1,0:T(8,128)S(1)}, f32[768,128]{1,0:T(8,128)S(1)}, u32[]{:S(2)}, u32[]{:S(2)}) %collective-permute-start.13) | collective-permute-done | bytes 393248 | tf_op jit(solution)/shard_map/ppermute | solution.py:448
  135.0 3.9 %filter_backward.3 = (f32[8,3072]{1,0:T(8,128)}, f32[8,3072]{1,0:T(8,128)}, f32[8,3072]{1,0:T(8,128)}, f32[8,3072]{1,0:T(8,128)}, f32[8,3072]{1,0:T(8,128)}, /*i...) custom-call(s32[1]{0:T(128)} %bitcast.core, ...), custom_call_target="tpu_custom_call" | custom-call | tf_op jit(solution)/shard_map/filter_backward/pallas_call | solution.py:425
  143.2 3.3 %collective-permute-start.24 = (f32[8,3072]{1,0:T(8,128)}, f32[8,3072]{1,0:T(8,128)S(1)}, u32[]{:S(2)}, u32[]{:S(2)}) collective-permute-start(f32[8,3072]{1,0:T(8,128)} %get-tuple-element.71), channel_id=1, source_target_pairs={{0,6},{1,7},{2,4},{3,5},{4,2},{5,3},{6,0},{7,1},{8,14},{9,15},{10,... | collective-permute-start | bytes 294920 | tf_op jit(solution)/shard_map/ppermute | solution.py:316
  147.6 6.4 %collective-permute-done.22.rest_2_ = f32[8,3072]{1,0:T(8,128)S(1)} collective-permute-done((f32[8,3072]{1,0:T(8,128)}, f32[8,3072]{1,0:T(8,128)S(1)}, u32[]{:S(2)}, u32[]{:S(2)}) %collective-permute-start.22) | collective-permute-done | bytes 98336 | tf_op jit(solution)/shard_map/ppermute | solution.py:316
  154.4 3.2 %collective-permute-done.23.rest_3_ = f32[8,3072]{1,0:T(8,128)S(1)} collective-permute-done((f32[8,3072]{1,0:T(8,128)}, f32[8,3072]{1,0:T(8,128)S(1)}, u32[]{:S(2)}, u32[]{:S(2)}) %collective-permute-start.23) | collective-permute-done | bytes 98336 | tf_op jit(solution)/shard_map/ppermute | solution.py:316
  159.6 3.9 %collective-permute-start.17 = (f32[8,3072]{1,0:T(8,128)}, f32[8,3072]{1,0:T(8,128)S(1)}, u32[]{:S(2)}, u32[]{:S(2)}) collective-permute-start(f32[8,3072]{1,0:T(8,128)} %get-tuple-element.61), channel_id=1, source_target_pairs={{0,4},{1,5},{2,6},{3,7},{4,0},{5,1},{6,2},{7,3},{8,12},{9,13},{10,... | collective-permute-start | bytes 294920 | tf_op jit(solution)/shard_map/ppermute | solution.py:316
  165.1 3.2 %collective-permute-start.20 = (f32[8,3072]{1,0:T(8,128)}, f32[8,3072]{1,0:T(8,128)S(1)}, u32[]{:S(2)}, u32[]{:S(2)}) collective-permute-start(f32[8,3072]{1,0:T(8,128)} %get-tuple-element.64), channel_id=1, source_target_pairs={{0,7},{1,6},{2,5},{3,4},{4,3},{5,2},{6,1},{7,0},{8,15},{9,14},{10,... | collective-permute-start | bytes 294920 | tf_op jit(solution)/shard_map/ppermute | solution.py:316
  169.4 8.6 %place_and_smooth.2.rest_9_ = f32[1,16,128,256]{3,2,1,0:T(8,128)} custom-call(s32[8]{0:T(128)} %widths.7, f32[128,8,256]{2,1,0:T(8,128)} %get-tuple-element.67.diff, f32[8,16,3072]{2,1,0:T(8,128)} %copy-done, f32[8,3072]{1,0:T(8,128)} %get-tuple-element.68.rest_1_, f32[8,3072]{1,0:T(8,128)} %copy-done.24, f32[8,3072]{1,0:T(8,128)} %copy-done.25, ...), custom_call_target="tpu_custom_call" | custom-call | tf_op jit(solution)/shard_map/place_and_smooth/pallas_call | solution.py:472
  180.3 3.6 %collective-permute-done.21.rest_7_ = f32[8,3072]{1,0:T(8,128)S(1)} collective-permute-done((f32[8,3072]{1,0:T(8,128)S(1)}, f32[8,3072]{1,0:T(8,128)S(1)}, u32[]{:S(2)}, u32[]{:S(2)}) %collective-permute-start.21) | collective-permute-done | bytes 98336 | tf_op jit(solution)/shard_map/ppermute | solution.py:316
  184.8 8.6 %place_and_smooth.3 = f32[1,16,128,256]{3,2,1,0:T(8,128)} custom-call(s32[8]{0:T(128)} %widths.7, f32[128,8,256]{2,1,0:T(8,128)} %get-tuple-element.42.diff, f32[8,16,3072]{2,1,0:T(8,128)} %copy-done, f32[8,3072]{1,0:T(8,128)} %get-tuple-element.59.rest_1_, f32[8,3072]{1,0:T(8,128)} %copy-done.12, ...), custom_call_target="tpu_custom_call", output_to_operand_aliasing={{}: (11, {})} | custom-call | tf_op jit(solution)/shard_map/place_and_smooth/pallas_call | solution.py:472
  (158 shorter events, 52.1 us)
Async XLA Ops:
  9.8 42.0 %all-to-all-start = ((f32[8,8,3072]{2,1,0:T(8,128)}), f32[8,8,3072]{2,1,0:T(8,128)S(1)}, u32[]{:S(2)}, u32[]{:S(2)}) async-start(f32[8,8,3072]{2,1,0:T(8,128)} %get-tuple-element.43), calls=%async_computation | async-start | bytes 1572864 | tf_op jit(solution)/shard_map/all_to_all | solution.py:313
  29.0 10.7 %collective-permute-start.1 = (f32[8,3072]{1,0:T(8,128)}, f32[8,3072]{1,0:T(8,128)S(1)}, u32[]{:S(2)}, u32[]{:S(2)}) collective-permute-start(f32[8,3072]{1,0:T(8,128)} %get-tuple-element.46), channel_id=1, source_target_pairs={{0,2},{1,3},{2,0},{3,1},{4,6},{5,7},{6,4},{7,5},{8,10},{9,11},{10,... | collective-permute-start | bytes 294920 | tf_op jit(solution)/shard_map/ppermute | solution.py:316
  30.5 10.1 %collective-permute-start.2 = (f32[8,3072]{1,0:T(8,128)}, f32[8,3072]{1,0:T(8,128)S(1)}, u32[]{:S(2)}, u32[]{:S(2)}) collective-permute-start(f32[8,3072]{1,0:T(8,128)} %get-tuple-element.47), channel_id=1, source_target_pairs={{0,3},{1,2},{2,1},{3,0},{4,7},{5,6},{6,5},{7,4},{8,11},{9,10},{10,... | collective-permute-start | bytes 294920 | tf_op jit(solution)/shard_map/ppermute | solution.py:316
  30.6 18.6 %collective-permute-start.3 = (f32[8,3072]{1,0:T(8,128)}, f32[8,3072]{1,0:T(8,128)S(1)}, u32[]{:S(2)}, u32[]{:S(2)}) collective-permute-start(f32[8,3072]{1,0:T(8,128)} %get-tuple-element.48), channel_id=1, source_target_pairs={{0,4},{1,5},{2,6},{3,7},{4,0},{5,1},{6,2},{7,3},{8,12},{9,13},{10,... | collective-permute-start | bytes 294920 | tf_op jit(solution)/shard_map/ppermute | solution.py:316
  33.4 18.3 %collective-permute-start.4 = (f32[8,3072]{1,0:T(8,128)}, f32[8,3072]{1,0:T(8,128)S(1)}, u32[]{:S(2)}, u32[]{:S(2)}) collective-permute-start(f32[8,3072]{1,0:T(8,128)} %get-tuple-element.49), channel_id=1, source_target_pairs={{0,5},{1,4},{2,7},{3,6},{4,1},{5,0},{6,3},{7,2},{8,13},{9,12},{10,... | collective-permute-start | bytes 294920 | tf_op jit(solution)/shard_map/ppermute | solution.py:316
  36.4 15.3 %collective-permute-start.5 = (f32[8,3072]{1,0:T(8,128)S(1)}, f32[8,3072]{1,0:T(8,128)S(1)}, u32[]{:S(2)}, u32[]{:S(2)}) collective-permute-start(f32[8,3072]{1,0:T(8,128)S(1)} %copy-done.39), channel_id=1, source_target_pairs={{0,6},{1,7},{2,4},{3,5},{4,2},{5,3},{6,0},{7,1},{8,14},{9,15},{10,... | collective-permute-start | bytes 294920 | tf_op jit(solution)/shard_map/ppermute | solution.py:316
  39.8 12.0 %collective-permute-start.6 = (f32[8,3072]{1,0:T(8,128)S(1)}, f32[8,3072]{1,0:T(8,128)S(1)}, u32[]{:S(2)}, u32[]{:S(2)}) collective-permute-start(f32[8,3072]{1,0:T(8,128)S(1)} %copy-done.38), channel_id=1, source_target_pairs={{0,7},{1,6},{2,5},{3,4},{4,3},{5,2},{6,1},{7,0},{8,15},{9,14},{10,... | collective-permute-start | bytes 294920 | tf_op jit(solution)/shard_map/ppermute | solution.py:316
  56.6 9.7 %collective-permute-start.7 = (f32[1536,128]{1,0:T(8,128)}, f32[1536,128]{1,0:T(8,128)}, u32[]{:S(2)}, u32[]{:S(2)}) collective-permute-start(f32[1536,128]{1,0:T(8,128)} %get-tuple-element.53), channel_id=1, source_target_pairs={{0,8},{8,0},{16,24},{24,16},{1,9},{9,1},{17,25},{25,17},{2,10},{10... | collective-permute-start | bytes 2359304 | tf_op jit(solution)/shard_map/ppermute | solution.py:445
  56.7 42.8 %all-to-all-start.2 = ((f32[8,16,3072]{2,1,0:T(8,128)}), f32[8,16,3072]{2,1,0:T(8,128)S(1)}, u32[]{:S(2)}, u32[]{:S(2)}) async-start(f32[8,16,3072]{2,1,0:T(8,128)} %get-tuple-element.56), calls=%async_computation.2 | async-start | bytes 3145728 | tf_op jit(solution)/shard_map/all_to_all | solution.py:313
  67.6 19.7 %collective-permute-start.8 = (f32[1536,128]{1,0:T(8,128)S(1)}, f32[1536,128]{1,0:T(8,128)S(1)}, u32[]{:S(2)}, u32[]{:S(2)}) collective-permute-start(f32[1536,128]{1,0:T(8,128)S(1)} %add.51), channel_id=1, source_target_pairs={{0,16},{8,24},{16,0},{24,8},{1,17},{9,25},{17,1},{25,9},{2,18},{10... | collective-permute-start | bytes 2359304 | tf_op jit(solution)/shard_map/ppermute | solution.py:448
  99.6 68.7 %all-to-all-start.1 = ((f32[8,16,3072]{2,1,0:T(8,128)}), f32[8,16,3072]{2,1,0:T(8,128)S(1)}, u32[]{:S(2)}, u32[]{:S(2)}) async-start(f32[8,16,3072]{2,1,0:T(8,128)} %filter_backward.2), calls=%async_computation.1 | async-start | bytes 3145728 | tf_op jit(solution)/shard_map/all_to_all | solution.py:313
  110.8 12.0 %collective-permute-start.11 = (f32[768,128]{1,0:T(8,128)S(1)}, f32[768,128]{1,0:T(8,128)S(1)}, u32[]{:S(2)}, u32[]{:S(2)}) collective-permute-start(f32[768,128]{1,0:T(8,128)S(1)} %get-tuple-element.80), channel_id=1, source_target_pairs={{0,16},{8,24},{16,0},{24,8},{1,17},{9,25},{17,1},{25,9},{2,18},{10... | collective-permute-start | bytes 1179656 | tf_op jit(solution)/shard_map/ppermute | solution.py:448
  112.4 18.1 %collective-permute-start.13 = (f32[768,128]{1,0:T(8,128)S(1)}, f32[768,128]{1,0:T(8,128)S(1)}, u32[]{:S(2)}, u32[]{:S(2)}) collective-permute-start(f32[768,128]{1,0:T(8,128)S(1)} %get-tuple-element.79), channel_id=1, source_target_pairs={{0,16},{8,24},{16,0},{24,8},{1,17},{9,25},{17,1},{25,9},{2,18},{10... | collective-permute-start | bytes 1179656 | tf_op jit(solution)/shard_map/ppermute | solution.py:448
  138.9 15.0 %collective-permute-start.22 = (f32[8,3072]{1,0:T(8,128)}, f32[8,3072]{1,0:T(8,128)S(1)}, u32[]{:S(2)}, u32[]{:S(2)}) collective-permute-start(f32[8,3072]{1,0:T(8,128)} %get-tuple-element.69), channel_id=1, source_target_pairs={{0,4},{1,5},{2,6},{3,7},{4,0},{5,1},{6,2},{7,3},{8,12},{9,13},{10,... | collective-permute-start | bytes 294920 | tf_op jit(solution)/shard_map/ppermute | solution.py:316
  141.7 15.9 %collective-permute-start.23 = (f32[8,3072]{1,0:T(8,128)}, f32[8,3072]{1,0:T(8,128)S(1)}, u32[]{:S(2)}, u32[]{:S(2)}) collective-permute-start(f32[8,3072]{1,0:T(8,128)} %get-tuple-element.70), channel_id=1, source_target_pairs={{0,5},{1,4},{2,7},{3,6},{4,1},{5,0},{6,3},{7,2},{8,13},{9,12},{10,... | collective-permute-start | bytes 294920 | tf_op jit(solution)/shard_map/ppermute | solution.py:316
  143.2 14.6 %collective-permute-start.24 = (f32[8,3072]{1,0:T(8,128)}, f32[8,3072]{1,0:T(8,128)S(1)}, u32[]{:S(2)}, u32[]{:S(2)}) collective-permute-start(f32[8,3072]{1,0:T(8,128)} %get-tuple-element.71), channel_id=1, source_target_pairs={{0,6},{1,7},{2,4},{3,5},{4,2},{5,3},{6,0},{7,1},{8,14},{9,15},{10,... | collective-permute-start | bytes 294920 | tf_op jit(solution)/shard_map/ppermute | solution.py:316
  146.4 13.2 %collective-permute-start.25 = (f32[8,3072]{1,0:T(8,128)}, f32[8,3072]{1,0:T(8,128)S(1)}, u32[]{:S(2)}, u32[]{:S(2)}) collective-permute-start(f32[8,3072]{1,0:T(8,128)} %get-tuple-element.72), channel_id=1, source_target_pairs={{0,7},{1,6},{2,5},{3,4},{4,3},{5,2},{6,1},{7,0},{8,15},{9,14},{10,... | collective-permute-start | bytes 294920 | tf_op jit(solution)/shard_map/ppermute | solution.py:316
  146.6 16.9 %collective-permute-start.26 = (f32[8,3072]{1,0:T(8,128)}, f32[8,3072]{1,0:T(8,128)S(1)}, u32[]{:S(2)}, u32[]{:S(2)}) collective-permute-start(f32[8,3072]{1,0:T(8,128)} %get-tuple-element.73), channel_id=1, source_target_pairs={{0,3},{1,2},{2,1},{3,0},{4,7},{5,6},{6,5},{7,4},{8,11},{9,10},{10,... | collective-permute-start | bytes 294920 | tf_op jit(solution)/shard_map/ppermute | solution.py:316
  153.9 9.6 %collective-permute-start.27 = (f32[8,3072]{1,0:T(8,128)}, f32[8,3072]{1,0:T(8,128)S(1)}, u32[]{:S(2)}, u32[]{:S(2)}) collective-permute-start(f32[8,3072]{1,0:T(8,128)} %get-tuple-element.74), channel_id=1, source_target_pairs={{0,2},{1,3},{2,0},{3,1},{4,6},{5,7},{6,4},{7,5},{8,10},{9,11},{10,... | collective-permute-start | bytes 294920 | tf_op jit(solution)/shard_map/ppermute | solution.py:316
  157.7 20.3 %collective-permute-start.16 = (f32[8,3072]{1,0:T(8,128)}, f32[8,3072]{1,0:T(8,128)S(1)}, u32[]{:S(2)}, u32[]{:S(2)}) collective-permute-start(f32[8,3072]{1,0:T(8,128)} %get-tuple-element.60), channel_id=1, source_target_pairs={{0,1},{1,0},{2,3},{3,2},{4,5},{5,4},{6,7},{7,6},{8,9},{9,8},{10,11... | collective-permute-start | bytes 294920 | tf_op jit(solution)/shard_map/ppermute | solution.py:316
  159.6 18.6 %collective-permute-start.17 = (f32[8,3072]{1,0:T(8,128)}, f32[8,3072]{1,0:T(8,128)S(1)}, u32[]{:S(2)}, u32[]{:S(2)}) collective-permute-start(f32[8,3072]{1,0:T(8,128)} %get-tuple-element.61), channel_id=1, source_target_pairs={{0,4},{1,5},{2,6},{3,7},{4,0},{5,1},{6,2},{7,3},{8,12},{9,13},{10,... | collective-permute-start | bytes 294920 | tf_op jit(solution)/shard_map/ppermute | solution.py:316
  163.5 16.8 %collective-permute-start.18 = (f32[8,3072]{1,0:T(8,128)}, f32[8,3072]{1,0:T(8,128)S(1)}, u32[]{:S(2)}, u32[]{:S(2)}) collective-permute-start(f32[8,3072]{1,0:T(8,128)} %get-tuple-element.62), channel_id=1, source_target_pairs={{0,5},{1,4},{2,7},{3,6},{4,1},{5,0},{6,3},{7,2},{8,13},{9,12},{10,... | collective-permute-start | bytes 294920 | tf_op jit(solution)/shard_map/ppermute | solution.py:316
  163.6 16.7 %collective-permute-start.19 = (f32[8,3072]{1,0:T(8,128)}, f32[8,3072]{1,0:T(8,128)S(1)}, u32[]{:S(2)}, u32[]{:S(2)}) collective-permute-start(f32[8,3072]{1,0:T(8,128)} %get-tuple-element.63), channel_id=1, source_target_pairs={{0,6},{1,7},{2,4},{3,5},{4,2},{5,3},{6,0},{7,1},{8,14},{9,15},{10,... | collective-permute-start | bytes 294920 | tf_op jit(solution)/shard_map/ppermute | solution.py:316
  165.1 15.2 %collective-permute-start.20 = (f32[8,3072]{1,0:T(8,128)}, f32[8,3072]{1,0:T(8,128)S(1)}, u32[]{:S(2)}, u32[]{:S(2)}) collective-permute-start(f32[8,3072]{1,0:T(8,128)} %get-tuple-element.64), channel_id=1, source_target_pairs={{0,7},{1,6},{2,5},{3,4},{4,3},{5,2},{6,1},{7,0},{8,15},{9,14},{10,... | collective-permute-start | bytes 294920 | tf_op jit(solution)/shard_map/ppermute | solution.py:316
  (51 other events, 293.5 us)

commit v7 on v6

--- a/solution.py
+++ b/solution.py
@@ -30,22 +30,22 @@
 
 def faces(diff, face_x, face_up, face_down, size_x, size_y):
     lane = lax.broadcasted_iota(jnp.int32, (1, GROUP, size_y), 2)
-    rows = 16
+    rows = 8
 
     def step(b, _):
         first = pl.multiple_of(b * rows, rows)
         here = diff[pl.ds(first, rows)]
         beyond = diff[pl.ds(jnp.minimum(first + rows, size_x - 1), 1)]
         ahead = jnp.concatenate([here[1:], beyond], axis=0)
-        row = first + lax.broadcasted_iota(jnp.int32, (rows, GROUP, size_y), 0)
-        face_x[pl.ds(first, rows)] = jnp.where(row < size_x - 1, 0.5 * (here + ahead), 0.0)
+        face_x[pl.ds(first, rows)] = 0.5 * (here + ahead)
         up = 0.5 * (here + pltpu.roll(here, size_y - 1, 2))
         face_up[pl.ds(first, rows)] = jnp.where(lane < size_y - 1, up, 0.0)
         down = 0.5 * (here + pltpu.roll(here, 1, 2))
         face_down[pl.ds(first, rows)] = jnp.where(lane > 0, down, 0.0)
         return 0
 
-    lax.fori_loop(0, size_x // rows, step, 0)
+    lax.fori_loop(0, size_x // rows, step, 0, unroll=16)
+    face_x[size_x - 1] = jnp.zeros((GROUP, size_y), F32)
 
 
 def sweep(read, write, face_x, face_up, face_down, size_x, size_y):
@@ -63,7 +63,7 @@
         write(first, rows, here + (flux_x - behind) + (flux_up - flux_down))
         return flux_x[-1:]
 
-    lax.fori_loop(0, size_x // rows, step, jnp.zeros((1, GROUP, size_y), F32), unroll=4)
+    lax.fori_loop(0, size_x // rows, step, jnp.zeros((1, GROUP, size_y), F32), unroll=16)
 
 
 def on_grid(grid):
@@ -100,7 +100,7 @@
 
 def turns_out(groups, last):
     near, far = list(range(groups // 2 - 1, 1, -1)), list(range(groups // 2, groups))
-    return [0, 1] + far + near if last else [0] + far + near + [1]
+    return [0] + near[:1] + far + near[1:] + [1] if last else [0] + far + near + [1]
 
 
 def forward_kernel(size_x, size_y, groups, n_sooner, widths, control, diffusivity, *rest):
@@ -468,7 +468,7 @@
         before = [] if out is None else [out]
         back = []
         for piece, turn in zip(pieces[group * groups :], turns_out(groups, group == last)):
-            back.append(permute(after(piece, out) if before and turn == 2 else piece, turn))
+            back.append(permute(after(piece, out) if before and turn == 1 else piece, turn))
         out = pl.pallas_call(
             functools.partial(backward_kernel, size_x, size_y, groups, capacity, group, group == last),
             grid=(1,),

time: 194 us -> 190 us (0.979)
  Pallas kernels: 70.2 us -> 65.2 us
    pallas_call x2, Pallas kernels: 19.7 us -> 16.6 us  [body(): pl.pallas_call(functools.partial(forward_kernel, size_x, size_y, groups,...]
    pallas_call x2, Pallas kernels: 17.2 us -> 15.2 us  [body(): pl.pallas_call(functools.partial(backward_kernel, size_x, size_y, groups,...]
  transfers between devices with their start and end apart: 33 -> 33, of which waited for: 15 -> 15; matrix products, arithmetic and copies ran while one was open for 7% -> 7% of each run, Pallas kernels for 25% -> 24%
where the time goes in v7:
time: 190 us; the launch traced here: 189 us
  Pallas kernels  65.2 us (34%)
  starting transfers between devices  53.5 us (28%)
  waiting for transfers between devices  50.2 us (26%)
  local copies, waits for them, and re-layouts  9.71 us (5%)
  other arithmetic  8.31 us (4%)
    ppermute x21, starting transfers between devices, permute(): lax.ppermute(piece, 'lev', flip_pairs(groups, turn))  32.4 us
    ppermute x21, waiting for transfers between devices, permute(): lax.ppermute(piece, 'lev', flip_pairs(groups, turn))  25.9 us
    pallas_call x2, Pallas kernels, weights(): pl.pallas_call(functools.partial(observation_kernel, part, c, obs_cap), g...  18.2 us
    pallas_call x2, Pallas kernels, body(): pl.pallas_call(functools.partial(forward_kernel, size_x, size_y, groups,...  16.6 us
    all_to_all x3, starting transfers between devices, exchange(): return lax.all_to_all(pieces, 'lev', 0, 0, tiled=True)  16.1 us
    pallas_call x2, Pallas kernels, body(): pl.pallas_call(functools.partial(backward_kernel, size_x, size_y, groups,...  15.2 us
    ppermute x3, waiting for transfers between devices, member_sum(): total = total + lax.ppermute(total, 'mem', flip_pairs(n_mem, bit))  14.3 us
    pallas_call x2, Pallas kernels, filter_forward(): pl.pallas_call(filter_kernel, grid_spec=pltpu.PrefetchScalarGridSpec(num_...  7.6 us
  transfers between devices with their start and end apart: 33, of which 15 were waited for; matrix products, arithmetic and copies ran while one was open for 7% of the time, Pallas kernels for 24%

profile of v7, /device:TPU:0, one launch (start us, length us, event | category | flops | bytes accessed | tf_op | source)
XLA Modules:
  0.0 188.8 jit_solution(15411093195554952118)
XLA Ops:
  0.0 8.3 %smooth_and_cut.2 = (f32[128,8,256]{2,1,0:T(8,128)}, f32[8,16,3072]{2,1,0:T(8,128)}, f32[8,8,3072]{2,1,0:T(8,128)}) custom-call(s32[8]{0:T(128)} %widths.7, f32[1,16,128,256]{3,2,1,0:T(8,128)} %control.3, f32[16,128,256]{2,1,0:T(8,128)} %diffusivity.3), custom_call_target="tpu_custom_call" | custom-call | tf_op jit(solution)/shard_map/smooth_and_cut/pallas_call | solution.py:322
  8.3 7.3 %all-to-all-start = ((f32[8,8,3072]{2,1,0:T(8,128)}), f32[8,8,3072]{2,1,0:T(8,128)S(1)}, u32[]{:S(2)}, u32[]{:S(2)}) async-start(f32[8,8,3072]{2,1,0:T(8,128)} %get-tuple-element.43), calls=%async_computation | async-start | bytes 1572864 | tf_op jit(solution)/shard_map/all_to_all | solution.py:313
  15.6 8.4 %smooth_and_cut.3 = (f32[128,8,256]{2,1,0:T(8,128)}, f32[8,16,3072]{2,1,0:T(8,128)}, f32[8,3072]{1,0:T(8,128)}, f32[8,3072]{1,0:T(8,128)}, f32[8,3072]{1,0:T(8,1...) custom-call(s32[8]{0:T(128)} %widths.7, ...), custom_call_target="tpu_custom_call", output_to_operand_aliasing={{1}: (3, {})} | custom-call | tf_op jit(solution)/shard_map/smooth_and_cut/pallas_call | solution.py:322
  33.4 3.3 %collective-permute-start.5 = (f32[8,3072]{1,0:T(8,128)S(1)}, f32[8,3072]{1,0:T(8,128)S(1)}, u32[]{:S(2)}, u32[]{:S(2)}) collective-permute-start(f32[8,3072]{1,0:T(8,128)S(1)} %copy-done.39), channel_id=1, source_target_pairs={{0,6},{1,7},{2,4},{3,5},{4,2},{5,3},{6,0},{7,1},{8,14},{9,15},{10,... | collective-permute-start | bytes 294920 | tf_op jit(solution)/shard_map/ppermute | solution.py:316
  37.6 10.1 %collective-permute-done.3.rest_5_ = f32[8,3072]{1,0:T(8,128)S(1)} collective-permute-done((f32[8,3072]{1,0:T(8,128)}, f32[8,3072]{1,0:T(8,128)S(1)}, u32[]{:S(2)}, u32[]{:S(2)}) %collective-permute-start.3) | collective-permute-done | bytes 98336 | tf_op jit(solution)/shard_map/ppermute | solution.py:316
  51.2 3.9 %filter_forward.2 = (f32[1536,128]{1,0:T(8,128)}, f32[1536,128]{1,0:T(8,128)}) custom-call(s32[1]{0:T(128)} %bitcast.core, f32[128,128]{1,0:T(8,128)} %pad_maximum_fusion.vfilter, f32[1,6144,128]{2,1,0:T(8,128)} %perturb.7, f32[8,8,3072]{2,1,0:T(8,128)} %copy-done.2, f32[8,3072]{1,0:T(8,128)} %get-tuple-element.44.rest_1_, f32[8,3072]{1,0:T(8,128)} %copy-done.19, ...), custom_call_target="tpu_custom_call" | custom-call | tf_op jit(solution)/shard_map/filter_forward/pallas_call | solution.py:409
  55.2 5.2 %all-to-all-start.2 = ((f32[8,16,3072]{2,1,0:T(8,128)}), f32[8,16,3072]{2,1,0:T(8,128)S(1)}, u32[]{:S(2)}, u32[]{:S(2)}) async-start(f32[8,16,3072]{2,1,0:T(8,128)} %get-tuple-element.56), calls=%async_computation.2 | async-start | bytes 3145728 | tf_op jit(solution)/shard_map/all_to_all | solution.py:313
  67.7 3.1 %compare_select_fusion.slots = s32[1,6144]{1,0:T(1,128)} fusion(pred[]{:T(512)S(6)} %lt.48, s32[1,6144]{1,0:T(1,128)S(1)} %copy-done.33, s32[]{:T(128)S(6)} %select_n.38, s32[]{:T(128)} %bitcast.6), kind=kLoop, calls=%fused_computation.10 | loop fusion | flops 55296 | bytes 49161 | tf_op jit(solution)/shard_map/jit(_where)/select_n | solution.py:358
  70.8 9.1 %observation_weights.2 = f32[1536,128]{1,0:T(8,128)} custom-call(s32[1,6144]{1,0:T(1,128)} %compare_select_fusion.slots, f32[1,6144,128]{2,1,0:T(8,128)} %rinv.3), custom_call_target="tpu_custom_call" | custom-call | tf_op jit(solution)/shard_map/observation_weights/pallas_call | solution.py:390
  79.9 5.9 %collective-permute-done.8 = f32[1536,128]{1,0:T(8,128)S(1)} collective-permute-done((f32[1536,128]{1,0:T(8,128)S(1)}, f32[1536,128]{1,0:T(8,128)S(1)}, u32[]{:S(2)}, u32[]{:S(2)}) %collective-permute-start.8) | collective-permute-done | bytes 786464 | tf_op jit(solution)/shard_map/ppermute | solution.py:448
  90.3 3.6 %filter_backward.2 = f32[8,16,3072]{2,1,0:T(8,128)} custom-call(s32[1]{0:T(128)} %bitcast.core, f32[128,128]{1,0:T(8,128)} %vfilter.2, f32[1,6144,128]{2,1,0:T(8,128)} %perturb.7, f32[1536,128]{1,0:T(8,128)} %copy-done.3, f32[1536,128]{1,0:T(8,128)} %copy-done.6), custom_call_target="tpu_custom_call" | custom-call | tf_op jit(solution)/shard_map/filter_backward/pallas_call | solution.py:425
  93.9 4.2 %all-to-all-done.2.rest_0_ = f32[8,16,3072]{2,1,0:T(8,128)S(1)} async-done(((f32[8,16,3072]{2,1,0:T(8,128)}), f32[8,16,3072]{2,1,0:T(8,128)S(1)}, u32[]{:S(2)}, u32[]{:S(2)}) %all-to-all-start.2) | async-done | bytes 1572896 | tf_op jit(solution)/shard_map/all_to_all | solution.py:313
  98.1 3.6 %all-to-all-start.1 = ((f32[8,16,3072]{2,1,0:T(8,128)}), f32[8,16,3072]{2,1,0:T(8,128)S(1)}, u32[]{:S(2)}, u32[]{:S(2)}) async-start(f32[8,16,3072]{2,1,0:T(8,128)} %filter_backward.2), calls=%async_computation.1 | async-start | bytes 3145728 | tf_op jit(solution)/shard_map/all_to_all | solution.py:313
  101.7 3.7 %filter_forward.3 = (f32[1536,128]{1,0:T(8,128)}, f32[1536,128]{1,0:T(8,128)}) custom-call(s32[1]{0:T(128)} %bitcast.core, f32[128,128]{1,0:T(8,128)} %vfilter.2, f32[1,6144,128]{2,1,0:T(8,128)} %perturb.7, f32[8,16,3072]{2,1,0:T(8,128)} %copy-done.1), custom_call_target="tpu_custom_call" | custom-call | tf_op jit(solution)/shard_map/filter_forward/pallas_call | solution.py:409
  111.2 9.1 %observation_weights.3 = f32[1536,128]{1,0:T(8,128)} custom-call(s32[1,6144]{1,0:T(1,128)} %compare_select_fusion.slots, f32[1,6144,128]{2,1,0:T(8,128)} %rinv.3), custom_call_target="tpu_custom_call" | custom-call | tf_op jit(solution)/shard_map/observation_weights/pallas_call | solution.py:390
  121.2 7.6 %collective-permute-done.13 = f32[768,128]{1,0:T(8,128)S(1)} collective-permute-done((f32[768,128]{1,0:T(8,128)S(1)}, f32[768,128]{1,0:T(8,128)S(1)}, u32[]{:S(2)}, u32[]{:S(2)}) %collective-permute-start.13) | collective-permute-done | bytes 393248 | tf_op jit(solution)/shard_map/ppermute | solution.py:448
  133.3 3.9 %filter_backward.3 = (f32[8,3072]{1,0:T(8,128)}, f32[8,3072]{1,0:T(8,128)}, f32[8,3072]{1,0:T(8,128)}, f32[8,3072]{1,0:T(8,128)}, f32[8,3072]{1,0:T(8,128)}, /*i...) custom-call(s32[1]{0:T(128)} %bitcast.core, ...), custom_call_target="tpu_custom_call" | custom-call | tf_op jit(solution)/shard_map/filter_backward/pallas_call | solution.py:425
  141.7 3.3 %collective-permute-start.24 = (f32[8,3072]{1,0:T(8,128)}, f32[8,3072]{1,0:T(8,128)S(1)}, u32[]{:S(2)}, u32[]{:S(2)}) collective-permute-start(f32[8,3072]{1,0:T(8,128)} %get-tuple-element.71), channel_id=1, source_target_pairs={{0,6},{1,7},{2,4},{3,5},{4,2},{5,3},{6,0},{7,1},{8,14},{9,15},{10,... | collective-permute-start | bytes 294920 | tf_op jit(solution)/shard_map/ppermute | solution.py:316
  146.1 6.0 %collective-permute-done.22.rest_2_ = f32[8,3072]{1,0:T(8,128)S(1)} collective-permute-done((f32[8,3072]{1,0:T(8,128)}, f32[8,3072]{1,0:T(8,128)S(1)}, u32[]{:S(2)}, u32[]{:S(2)}) %collective-permute-start.22) | collective-permute-done | bytes 98336 | tf_op jit(solution)/shard_map/ppermute | solution.py:316
  152.9 3.2 %collective-permute-done.23.rest_3_ = f32[8,3072]{1,0:T(8,128)S(1)} collective-permute-done((f32[8,3072]{1,0:T(8,128)}, f32[8,3072]{1,0:T(8,128)S(1)}, u32[]{:S(2)}, u32[]{:S(2)}) %collective-permute-start.23) | collective-permute-done | bytes 98336 | tf_op jit(solution)/shard_map/ppermute | solution.py:316
  158.7 3.2 %collective-permute-start.17 = (f32[8,3072]{1,0:T(8,128)}, f32[8,3072]{1,0:T(8,128)S(1)}, u32[]{:S(2)}, u32[]{:S(2)}) collective-permute-start(f32[8,3072]{1,0:T(8,128)} %get-tuple-element.61), channel_id=1, source_target_pairs={{0,4},{1,5},{2,6},{3,7},{4,0},{5,1},{6,2},{7,3},{8,12},{9,13},{10,... | collective-permute-start | bytes 294920 | tf_op jit(solution)/shard_map/ppermute | solution.py:316
  167.9 7.6 %place_and_smooth.2.rest_9_ = f32[1,16,128,256]{3,2,1,0:T(8,128)} custom-call(s32[8]{0:T(128)} %widths.7, f32[128,8,256]{2,1,0:T(8,128)} %get-tuple-element.67.diff, f32[8,16,3072]{2,1,0:T(8,128)} %copy-done, f32[8,3072]{1,0:T(8,128)} %get-tuple-element.68.rest_1_, f32[8,3072]{1,0:T(8,128)} %copy-done.24, f32[8,3072]{1,0:T(8,128)} %copy-done.25, ...), custom_call_target="tpu_custom_call" | custom-call | tf_op jit(solution)/shard_map/place_and_smooth/pallas_call | solution.py:472
  176.4 3.9 %collective-permute-done.21.rest_7_ = f32[8,3072]{1,0:T(8,128)S(1)} collective-permute-done((f32[8,3072]{1,0:T(8,128)S(1)}, f32[8,3072]{1,0:T(8,128)S(1)}, u32[]{:S(2)}, u32[]{:S(2)}) %collective-permute-start.21) | collective-permute-done | bytes 98336 | tf_op jit(solution)/shard_map/ppermute | solution.py:316
  181.0 7.6 %place_and_smooth.3 = f32[1,16,128,256]{3,2,1,0:T(8,128)} custom-call(s32[8]{0:T(128)} %widths.7, f32[128,8,256]{2,1,0:T(8,128)} %get-tuple-element.42.diff, f32[8,16,3072]{2,1,0:T(8,128)} %copy-done, f32[8,3072]{1,0:T(8,128)} %get-tuple-element.59.rest_1_, f32[8,3072]{1,0:T(8,128)} %copy-done.12, ...), custom_call_target="tpu_custom_call", output_to_operand_aliasing={{}: (11, {})} | custom-call | tf_op jit(solution)/shard_map/place_and_smooth/pallas_call | solution.py:472
  (158 shorter events, 51.8 us)
Async XLA Ops:
  8.3 42.0 %all-to-all-start = ((f32[8,8,3072]{2,1,0:T(8,128)}), f32[8,8,3072]{2,1,0:T(8,128)S(1)}, u32[]{:S(2)}, u32[]{:S(2)}) async-start(f32[8,8,3072]{2,1,0:T(8,128)} %get-tuple-element.43), calls=%async_computation | async-start | bytes 1572864 | tf_op jit(solution)/shard_map/all_to_all | solution.py:313
  26.0 10.7 %collective-permute-start.1 = (f32[8,3072]{1,0:T(8,128)}, f32[8,3072]{1,0:T(8,128)S(1)}, u32[]{:S(2)}, u32[]{:S(2)}) collective-permute-start(f32[8,3072]{1,0:T(8,128)} %get-tuple-element.46), channel_id=1, source_target_pairs={{0,2},{1,3},{2,0},{3,1},{4,6},{5,7},{6,4},{7,5},{8,10},{9,11},{10,... | collective-permute-start | bytes 294920 | tf_op jit(solution)/shard_map/ppermute | solution.py:316
  27.5 10.1 %collective-permute-start.2 = (f32[8,3072]{1,0:T(8,128)}, f32[8,3072]{1,0:T(8,128)S(1)}, u32[]{:S(2)}, u32[]{:S(2)}) collective-permute-start(f32[8,3072]{1,0:T(8,128)} %get-tuple-element.47), channel_id=1, source_target_pairs={{0,3},{1,2},{2,1},{3,0},{4,7},{5,6},{6,5},{7,4},{8,11},{9,10},{10,... | collective-permute-start | bytes 294920 | tf_op jit(solution)/shard_map/ppermute | solution.py:316
  27.6 20.1 %collective-permute-start.3 = (f32[8,3072]{1,0:T(8,128)}, f32[8,3072]{1,0:T(8,128)S(1)}, u32[]{:S(2)}, u32[]{:S(2)}) collective-permute-start(f32[8,3072]{1,0:T(8,128)} %get-tuple-element.48), channel_id=1, source_target_pairs={{0,4},{1,5},{2,6},{3,7},{4,0},{5,1},{6,2},{7,3},{8,12},{9,13},{10,... | collective-permute-start | bytes 294920 | tf_op jit(solution)/shard_map/ppermute | solution.py:316
  30.4 19.8 %collective-permute-start.4 = (f32[8,3072]{1,0:T(8,128)}, f32[8,3072]{1,0:T(8,128)S(1)}, u32[]{:S(2)}, u32[]{:S(2)}) collective-permute-start(f32[8,3072]{1,0:T(8,128)} %get-tuple-element.49), channel_id=1, source_target_pairs={{0,5},{1,4},{2,7},{3,6},{4,1},{5,0},{6,3},{7,2},{8,13},{9,12},{10,... | collective-permute-start | bytes 294920 | tf_op jit(solution)/shard_map/ppermute | solution.py:316
  33.4 16.8 %collective-permute-start.5 = (f32[8,3072]{1,0:T(8,128)S(1)}, f32[8,3072]{1,0:T(8,128)S(1)}, u32[]{:S(2)}, u32[]{:S(2)}) collective-permute-start(f32[8,3072]{1,0:T(8,128)S(1)} %copy-done.39), channel_id=1, source_target_pairs={{0,6},{1,7},{2,4},{3,5},{4,2},{5,3},{6,0},{7,1},{8,14},{9,15},{10,... | collective-permute-start | bytes 294920 | tf_op jit(solution)/shard_map/ppermute | solution.py:316
  36.7 13.5 %collective-permute-start.6 = (f32[8,3072]{1,0:T(8,128)S(1)}, f32[8,3072]{1,0:T(8,128)S(1)}, u32[]{:S(2)}, u32[]{:S(2)}) collective-permute-start(f32[8,3072]{1,0:T(8,128)S(1)} %copy-done.38), channel_id=1, source_target_pairs={{0,7},{1,6},{2,5},{3,4},{4,3},{5,2},{6,1},{7,0},{8,15},{9,14},{10,... | collective-permute-start | bytes 294920 | tf_op jit(solution)/shard_map/ppermute | solution.py:316
  55.1 9.7 %collective-permute-start.7 = (f32[1536,128]{1,0:T(8,128)}, f32[1536,128]{1,0:T(8,128)}, u32[]{:S(2)}, u32[]{:S(2)}) collective-permute-start(f32[1536,128]{1,0:T(8,128)} %get-tuple-element.53), channel_id=1, source_target_pairs={{0,8},{8,0},{16,24},{24,16},{1,9},{9,1},{17,25},{25,17},{2,10},{10... | collective-permute-start | bytes 2359304 | tf_op jit(solution)/shard_map/ppermute | solution.py:445
  55.2 42.8 %all-to-all-start.2 = ((f32[8,16,3072]{2,1,0:T(8,128)}), f32[8,16,3072]{2,1,0:T(8,128)S(1)}, u32[]{:S(2)}, u32[]{:S(2)}) async-start(f32[8,16,3072]{2,1,0:T(8,128)} %get-tuple-element.56), calls=%async_computation.2 | async-start | bytes 3145728 | tf_op jit(solution)/shard_map/all_to_all | solution.py:313
  66.1 19.7 %collective-permute-start.8 = (f32[1536,128]{1,0:T(8,128)S(1)}, f32[1536,128]{1,0:T(8,128)S(1)}, u32[]{:S(2)}, u32[]{:S(2)}) collective-permute-start(f32[1536,128]{1,0:T(8,128)S(1)} %add.51), channel_id=1, source_target_pairs={{0,16},{8,24},{16,0},{24,8},{1,17},{9,25},{17,1},{25,9},{2,18},{10... | collective-permute-start | bytes 2359304 | tf_op jit(solution)/shard_map/ppermute | solution.py:448
  98.1 68.7 %all-to-all-start.1 = ((f32[8,16,3072]{2,1,0:T(8,128)}), f32[8,16,3072]{2,1,0:T(8,128)S(1)}, u32[]{:S(2)}, u32[]{:S(2)}) async-start(f32[8,16,3072]{2,1,0:T(8,128)} %filter_backward.2), calls=%async_computation.1 | async-start | bytes 3145728 | tf_op jit(solution)/shard_map/all_to_all | solution.py:313
  109.1 12.0 %collective-permute-start.11 = (f32[768,128]{1,0:T(8,128)S(1)}, f32[768,128]{1,0:T(8,128)S(1)}, u32[]{:S(2)}, u32[]{:S(2)}) collective-permute-start(f32[768,128]{1,0:T(8,128)S(1)} %get-tuple-element.80), channel_id=1, source_target_pairs={{0,16},{8,24},{16,0},{24,8},{1,17},{9,25},{17,1},{25,9},{2,18},{10... | collective-permute-start | bytes 1179656 | tf_op jit(solution)/shard_map/ppermute | solution.py:448
  110.7 18.1 %collective-permute-start.13 = (f32[768,128]{1,0:T(8,128)S(1)}, f32[768,128]{1,0:T(8,128)S(1)}, u32[]{:S(2)}, u32[]{:S(2)}) collective-permute-start(f32[768,128]{1,0:T(8,128)S(1)} %get-tuple-element.79), channel_id=1, source_target_pairs={{0,16},{8,24},{16,0},{24,8},{1,17},{9,25},{17,1},{25,9},{2,18},{10... | collective-permute-start | bytes 1179656 | tf_op jit(solution)/shard_map/ppermute | solution.py:448
  137.2 14.8 %collective-permute-start.22 = (f32[8,3072]{1,0:T(8,128)}, f32[8,3072]{1,0:T(8,128)S(1)}, u32[]{:S(2)}, u32[]{:S(2)}) collective-permute-start(f32[8,3072]{1,0:T(8,128)} %get-tuple-element.69), channel_id=1, source_target_pairs={{0,4},{1,5},{2,6},{3,7},{4,0},{5,1},{6,2},{7,3},{8,12},{9,13},{10,... | collective-permute-start | bytes 294920 | tf_op jit(solution)/shard_map/ppermute | solution.py:316
  140.2 15.9 %collective-permute-start.23 = (f32[8,3072]{1,0:T(8,128)}, f32[8,3072]{1,0:T(8,128)S(1)}, u32[]{:S(2)}, u32[]{:S(2)}) collective-permute-start(f32[8,3072]{1,0:T(8,128)} %get-tuple-element.70), channel_id=1, source_target_pairs={{0,5},{1,4},{2,7},{3,6},{4,1},{5,0},{6,3},{7,2},{8,13},{9,12},{10,... | collective-permute-start | bytes 294920 | tf_op jit(solution)/shard_map/ppermute | solution.py:316
  141.7 14.4 %collective-permute-start.24 = (f32[8,3072]{1,0:T(8,128)}, f32[8,3072]{1,0:T(8,128)S(1)}, u32[]{:S(2)}, u32[]{:S(2)}) collective-permute-start(f32[8,3072]{1,0:T(8,128)} %get-tuple-element.71), channel_id=1, source_target_pairs={{0,6},{1,7},{2,4},{3,5},{4,2},{5,3},{6,0},{7,1},{8,14},{9,15},{10,... | collective-permute-start | bytes 294920 | tf_op jit(solution)/shard_map/ppermute | solution.py:316
  144.9 13.8 %collective-permute-start.25 = (f32[8,3072]{1,0:T(8,128)}, f32[8,3072]{1,0:T(8,128)S(1)}, u32[]{:S(2)}, u32[]{:S(2)}) collective-permute-start(f32[8,3072]{1,0:T(8,128)} %get-tuple-element.72), channel_id=1, source_target_pairs={{0,7},{1,6},{2,5},{3,4},{4,3},{5,2},{6,1},{7,0},{8,15},{9,14},{10,... | collective-permute-start | bytes 294920 | tf_op jit(solution)/shard_map/ppermute | solution.py:316
  145.0 17.0 %collective-permute-start.26 = (f32[8,3072]{1,0:T(8,128)}, f32[8,3072]{1,0:T(8,128)S(1)}, u32[]{:S(2)}, u32[]{:S(2)}) collective-permute-start(f32[8,3072]{1,0:T(8,128)} %get-tuple-element.73), channel_id=1, source_target_pairs={{0,3},{1,2},{2,1},{3,0},{4,7},{5,6},{6,5},{7,4},{8,11},{9,10},{10,... | collective-permute-start | bytes 294920 | tf_op jit(solution)/shard_map/ppermute | solution.py:316
  152.1 10.0 %collective-permute-start.27 = (f32[8,3072]{1,0:T(8,128)}, f32[8,3072]{1,0:T(8,128)S(1)}, u32[]{:S(2)}, u32[]{:S(2)}) collective-permute-start(f32[8,3072]{1,0:T(8,128)} %get-tuple-element.74), channel_id=1, source_target_pairs={{0,2},{1,3},{2,0},{3,1},{4,6},{5,7},{6,4},{7,5},{8,10},{9,11},{10,... | collective-permute-start | bytes 294920 | tf_op jit(solution)/shard_map/ppermute | solution.py:316
  156.1 19.5 %collective-permute-start.16 = (f32[8,3072]{1,0:T(8,128)}, f32[8,3072]{1,0:T(8,128)S(1)}, u32[]{:S(2)}, u32[]{:S(2)}) collective-permute-start(f32[8,3072]{1,0:T(8,128)} %get-tuple-element.60), channel_id=1, source_target_pairs={{0,3},{1,2},{2,1},{3,0},{4,7},{5,6},{6,5},{7,4},{8,11},{9,10},{10,... | collective-permute-start | bytes 294920 | tf_op jit(solution)/shard_map/ppermute | solution.py:316
  158.7 17.0 %collective-permute-start.17 = (f32[8,3072]{1,0:T(8,128)}, f32[8,3072]{1,0:T(8,128)S(1)}, u32[]{:S(2)}, u32[]{:S(2)}) collective-permute-start(f32[8,3072]{1,0:T(8,128)} %get-tuple-element.61), channel_id=1, source_target_pairs={{0,4},{1,5},{2,6},{3,7},{4,0},{5,1},{6,2},{7,3},{8,12},{9,13},{10,... | collective-permute-start | bytes 294920 | tf_op jit(solution)/shard_map/ppermute | solution.py:316
  162.0 14.4 %collective-permute-start.18 = (f32[8,3072]{1,0:T(8,128)}, f32[8,3072]{1,0:T(8,128)S(1)}, u32[]{:S(2)}, u32[]{:S(2)}) collective-permute-start(f32[8,3072]{1,0:T(8,128)} %get-tuple-element.62), channel_id=1, source_target_pairs={{0,5},{1,4},{2,7},{3,6},{4,1},{5,0},{6,3},{7,2},{8,13},{9,12},{10,... | collective-permute-start | bytes 294920 | tf_op jit(solution)/shard_map/ppermute | solution.py:316
  162.1 14.3 %collective-permute-start.19 = (f32[8,3072]{1,0:T(8,128)}, f32[8,3072]{1,0:T(8,128)S(1)}, u32[]{:S(2)}, u32[]{:S(2)}) collective-permute-start(f32[8,3072]{1,0:T(8,128)} %get-tuple-element.63), channel_id=1, source_target_pairs={{0,6},{1,7},{2,4},{3,5},{4,2},{5,3},{6,0},{7,1},{8,14},{9,15},{10,... | collective-permute-start | bytes 294920 | tf_op jit(solution)/shard_map/ppermute | solution.py:316
  164.2 12.1 %collective-permute-start.20 = (f32[8,3072]{1,0:T(8,128)}, f32[8,3072]{1,0:T(8,128)S(1)}, u32[]{:S(2)}, u32[]{:S(2)}) collective-permute-start(f32[8,3072]{1,0:T(8,128)} %get-tuple-element.64), channel_id=1, source_target_pairs={{0,7},{1,6},{2,5},{3,4},{4,3},{5,2},{6,1},{7,0},{8,15},{9,14},{10,... | collective-permute-start | bytes 294920 | tf_op jit(solution)/shard_map/ppermute | solution.py:316
  (51 other events, 288.5 us)

commit v8 on v7

--- a/solution.py
+++ b/solution.py
@@ -25,7 +25,7 @@
         dst[pl.ds(first, 8)] = jnp.swapaxes(src[:, pl.ds(first, 8), :], 0, 1)
         return 0
 
-    lax.fori_loop(0, size_x // 8, step, 0, unroll=2)
+    lax.fori_loop(0, size_x // 8, step, 0, unroll=8)
 
 
 def faces(diff, face_x, face_up, face_down, size_x, size_y):
@@ -461,7 +461,7 @@
     back_sooner = exchange(pieces)
 
     keep, send = filter_forward(1, after(vertical_filter, pieces), got_later)
-    mine, other = member_sum(keep, send, weight[1], 2)
+    mine, other = member_sum(keep, send, weight[1], 3)
     pieces = filter_backward(1, filter_out, mine, other, True)
     out = None
     for group in range(n_groups):

time: 190 us -> 190 us (level)
  waiting for transfers between devices: 50.2 us -> 48.2 us
    ppermute x3 -> x4, waiting for transfers between devices: 14.3 us -> 12.7 us  [member_sum(): total = total + lax.ppermute(total, 'mem', flip_pairs(n_mem, bit))]
    ppermute x3 -> x4, starting transfers between devices: 3.66 us -> 5.17 us  [member_sum(): total = total + lax.ppermute(total, 'mem', flip_pairs(n_mem, bit))]
    unnamed x85 -> x89, local copies, waits for them, and re-layouts: 4.66 us -> 4.75 us
    ppermute x3 -> x4, waiting for transfers between devices: 4.04 us -> 3.96 us  [member_sum(): other.append(lax.ppermute(mine[-1], 'mem', flip_pairs(n_mem, 1)))]
  transfers between devices with their start and end apart: 33 -> 36, of which waited for: 15 -> 17; matrix products, arithmetic and copies ran while one was open for 7% -> 7% of each run, Pallas kernels for 24% -> 24%
where the time goes in v8:
time: 190 us; the launch traced here: 189 us
  Pallas kernels  65 us (34%)
  starting transfers between devices  55 us (29%)
  waiting for transfers between devices  48.2 us (25%)
  local copies, waits for them, and re-layouts  9.96 us (5%)
  other arithmetic  8.41 us (4%)
  between operations  2.14 us (1%)
    ppermute x21, starting transfers between devices, permute(): lax.ppermute(piece, 'lev', flip_pairs(groups, turn))  32.3 us
    ppermute x21, waiting for transfers between devices, permute(): lax.ppermute(piece, 'lev', flip_pairs(groups, turn))  26 us
    pallas_call x2, Pallas kernels, weights(): pl.pallas_call(functools.partial(observation_kernel, part, c, obs_cap), g...  18.2 us
    pallas_call x2, Pallas kernels, body(): pl.pallas_call(functools.partial(forward_kernel, size_x, size_y, groups,...  16.4 us
    all_to_all x3, starting transfers between devices, exchange(): return lax.all_to_all(pieces, 'lev', 0, 0, tiled=True)  16.1 us
    pallas_call x2, Pallas kernels, body(): pl.pallas_call(functools.partial(backward_kernel, size_x, size_y, groups,...  15.2 us
    ppermute x4, waiting for transfers between devices, member_sum(): total = total + lax.ppermute(total, 'mem', flip_pairs(n_mem, bit))  12.7 us
    pallas_call x2, Pallas kernels, filter_forward(): pl.pallas_call(filter_kernel, grid_spec=pltpu.PrefetchScalarGridSpec(num_...  7.63 us
  transfers between devices with their start and end apart: 36, of which 17 were waited for; matrix products, arithmetic and copies ran while one was open for 7% of the time, Pallas kernels for 24%

profile of v8, /device:TPU:0, one launch (start us, length us, event | category | flops | bytes accessed | tf_op | source)
XLA Modules:
  0.0 188.8 jit_solution(15606595256110970996)
XLA Ops:
  0.0 8.2 %smooth_and_cut.2 = (f32[128,8,256]{2,1,0:T(8,128)}, f32[8,16,3072]{2,1,0:T(8,128)}, f32[8,8,3072]{2,1,0:T(8,128)}) custom-call(s32[8]{0:T(128)} %widths.7, f32[1,16,128,256]{3,2,1,0:T(8,128)} %control.3, f32[16,128,256]{2,1,0:T(8,128)} %diffusivity.3), custom_call_target="tpu_custom_call" | custom-call | tf_op jit(solution)/shard_map/smooth_and_cut/pallas_call | solution.py:322
  8.2 7.3 %all-to-all-start = ((f32[8,8,3072]{2,1,0:T(8,128)}), f32[8,8,3072]{2,1,0:T(8,128)S(1)}, u32[]{:S(2)}, u32[]{:S(2)}) async-start(f32[8,8,3072]{2,1,0:T(8,128)} %get-tuple-element.43), calls=%async_computation | async-start | bytes 1572864 | tf_op jit(solution)/shard_map/all_to_all | solution.py:313
  15.5 8.3 %smooth_and_cut.3 = (f32[128,8,256]{2,1,0:T(8,128)}, f32[8,16,3072]{2,1,0:T(8,128)}, f32[8,3072]{1,0:T(8,128)}, f32[8,3072]{1,0:T(8,128)}, f32[8,3072]{1,0:T(8,1...) custom-call(s32[8]{0:T(128)} %widths.7, ...), custom_call_target="tpu_custom_call", output_to_operand_aliasing={{1}: (3, {})} | custom-call | tf_op jit(solution)/shard_map/smooth_and_cut/pallas_call | solution.py:322
  33.2 3.3 %collective-permute-start.5 = (f32[8,3072]{1,0:T(8,128)S(1)}, f32[8,3072]{1,0:T(8,128)S(1)}, u32[]{:S(2)}, u32[]{:S(2)}) collective-permute-start(f32[8,3072]{1,0:T(8,128)S(1)} %copy-done.41), channel_id=1, source_target_pairs={{0,6},{1,7},{2,4},{3,5},{4,2},{5,3},{6,0},{7,1},{8,14},{9,15},{10,... | collective-permute-start | bytes 294920 | tf_op jit(solution)/shard_map/ppermute | solution.py:316
  37.4 10.2 %collective-permute-done.3.rest_5_ = f32[8,3072]{1,0:T(8,128)S(1)} collective-permute-done((f32[8,3072]{1,0:T(8,128)}, f32[8,3072]{1,0:T(8,128)S(1)}, u32[]{:S(2)}, u32[]{:S(2)}) %collective-permute-start.3) | collective-permute-done | bytes 98336 | tf_op jit(solution)/shard_map/ppermute | solution.py:316
  51.1 3.9 %filter_forward.2 = (f32[1536,128]{1,0:T(8,128)}, f32[1536,128]{1,0:T(8,128)}) custom-call(s32[1]{0:T(128)} %bitcast.core, f32[128,128]{1,0:T(8,128)} %pad_maximum_fusion.vfilter, f32[1,6144,128]{2,1,0:T(8,128)} %perturb.7, f32[8,8,3072]{2,1,0:T(8,128)} %copy-done.2, f32[8,3072]{1,0:T(8,128)} %get-tuple-element.44.rest_1_, f32[8,3072]{1,0:T(8,128)} %copy-done.21, ...), custom_call_target="tpu_custom_call" | custom-call | tf_op jit(solution)/shard_map/filter_forward/pallas_call | solution.py:409
  55.2 5.2 %all-to-all-start.2 = ((f32[8,16,3072]{2,1,0:T(8,128)}), f32[8,16,3072]{2,1,0:T(8,128)S(1)}, u32[]{:S(2)}, u32[]{:S(2)}) async-start(f32[8,16,3072]{2,1,0:T(8,128)} %get-tuple-element.56), calls=%async_computation.2 | async-start | bytes 3145728 | tf_op jit(solution)/shard_map/all_to_all | solution.py:313
  68.0 3.2 %compare_select_fusion.slots = s32[1,6144]{1,0:T(1,128)} fusion(pred[]{:T(512)S(6)} %lt.48, s32[1,6144]{1,0:T(1,128)S(1)} %copy-done.35, s32[]{:T(128)S(6)} %select_n.38, s32[]{:T(128)} %bitcast.6), kind=kLoop, calls=%fused_computation.12 | loop fusion | flops 55296 | bytes 49161 | tf_op jit(solution)/shard_map/jit(_where)/select_n | solution.py:358
  71.2 9.1 %observation_weights.2 = f32[1536,128]{1,0:T(8,128)} custom-call(s32[1,6144]{1,0:T(1,128)} %compare_select_fusion.slots, f32[1,6144,128]{2,1,0:T(8,128)} %rinv.3), custom_call_target="tpu_custom_call" | custom-call | tf_op jit(solution)/shard_map/observation_weights/pallas_call | solution.py:390
  80.3 5.8 %collective-permute-done.8 = f32[1536,128]{1,0:T(8,128)S(1)} collective-permute-done((f32[1536,128]{1,0:T(8,128)S(1)}, f32[1536,128]{1,0:T(8,128)S(1)}, u32[]{:S(2)}, u32[]{:S(2)}) %collective-permute-start.8) | collective-permute-done | bytes 786464 | tf_op jit(solution)/shard_map/ppermute | solution.py:448
  90.6 3.5 %filter_backward.2 = f32[8,16,3072]{2,1,0:T(8,128)} custom-call(s32[1]{0:T(128)} %bitcast.core, f32[128,128]{1,0:T(8,128)} %vfilter.2, f32[1,6144,128]{2,1,0:T(8,128)} %perturb.7, f32[1536,128]{1,0:T(8,128)} %copy-done.3, f32[1536,128]{1,0:T(8,128)} %copy-done.7), custom_call_target="tpu_custom_call" | custom-call | tf_op jit(solution)/shard_map/filter_backward/pallas_call | solution.py:425
  94.2 3.8 %all-to-all-done.2.rest_0_ = f32[8,16,3072]{2,1,0:T(8,128)S(1)} async-done(((f32[8,16,3072]{2,1,0:T(8,128)}), f32[8,16,3072]{2,1,0:T(8,128)S(1)}, u32[]{:S(2)}, u32[]{:S(2)}) %all-to-all-start.2) | async-done | bytes 1572896 | tf_op jit(solution)/shard_map/all_to_all | solution.py:313
  98.0 3.6 %all-to-all-start.1 = ((f32[8,16,3072]{2,1,0:T(8,128)}), f32[8,16,3072]{2,1,0:T(8,128)S(1)}, u32[]{:S(2)}, u32[]{:S(2)}) async-start(f32[8,16,3072]{2,1,0:T(8,128)} %filter_backward.2), calls=%async_computation.1 | async-start | bytes 3145728 | tf_op jit(solution)/shard_map/all_to_all | solution.py:313
  101.6 3.7 %filter_forward.3 = (f32[1536,128]{1,0:T(8,128)}, f32[1536,128]{1,0:T(8,128)}) custom-call(s32[1]{0:T(128)} %bitcast.core, f32[128,128]{1,0:T(8,128)} %vfilter.2, f32[1,6144,128]{2,1,0:T(8,128)} %perturb.7, f32[8,16,3072]{2,1,0:T(8,128)} %copy-done.1), custom_call_target="tpu_custom_call" | custom-call | tf_op jit(solution)/shard_map/filter_forward/pallas_call | solution.py:409
  112.7 9.1 %observation_weights.3 = f32[1536,128]{1,0:T(8,128)} custom-call(s32[1,6144]{1,0:T(1,128)} %compare_select_fusion.slots, f32[1,6144,128]{2,1,0:T(8,128)} %rinv.3), custom_call_target="tpu_custom_call" | custom-call | tf_op jit(solution)/shard_map/observation_weights/pallas_call | solution.py:390
  123.9 4.8 %collective-permute-done.15 = f32[512,128]{1,0:T(8,128)S(1)} collective-permute-done((f32[512,128]{1,0:T(8,128)S(1)}, f32[512,128]{1,0:T(8,128)S(1)}, u32[]{:S(2)}, u32[]{:S(2)}) %collective-permute-start.15) | collective-permute-done | bytes 262176 | tf_op jit(solution)/shard_map/ppermute | solution.py:448
  133.3 3.9 %filter_backward.3 = (f32[8,3072]{1,0:T(8,128)}, f32[8,3072]{1,0:T(8,128)}, f32[8,3072]{1,0:T(8,128)}, f32[8,3072]{1,0:T(8,128)}, f32[8,3072]{1,0:T(8,128)}, /*i...) custom-call(s32[1]{0:T(128)} %bitcast.core, ...), custom_call_target="tpu_custom_call" | custom-call | tf_op jit(solution)/shard_map/filter_backward/pallas_call | solution.py:425
  141.7 3.3 %collective-permute-start.27 = (f32[8,3072]{1,0:T(8,128)}, f32[8,3072]{1,0:T(8,128)S(1)}, u32[]{:S(2)}, u32[]{:S(2)}) collective-permute-start(f32[8,3072]{1,0:T(8,128)} %get-tuple-element.71), channel_id=1, source_target_pairs={{0,6},{1,7},{2,4},{3,5},{4,2},{5,3},{6,0},{7,1},{8,14},{9,15},{10,... | collective-permute-start | bytes 294920 | tf_op jit(solution)/shard_map/ppermute | solution.py:316
  146.1 6.1 %collective-permute-done.25.rest_2_ = f32[8,3072]{1,0:T(8,128)S(1)} collective-permute-done((f32[8,3072]{1,0:T(8,128)}, f32[8,3072]{1,0:T(8,128)S(1)}, u32[]{:S(2)}, u32[]{:S(2)}) %collective-permute-start.25) | collective-permute-done | bytes 98336 | tf_op jit(solution)/shard_map/ppermute | solution.py:316
  152.9 3.2 %collective-permute-done.26.rest_3_ = f32[8,3072]{1,0:T(8,128)S(1)} collective-permute-done((f32[8,3072]{1,0:T(8,128)}, f32[8,3072]{1,0:T(8,128)S(1)}, u32[]{:S(2)}, u32[]{:S(2)}) %collective-permute-start.26) | collective-permute-done | bytes 98336 | tf_op jit(solution)/shard_map/ppermute | solution.py:316
  158.7 3.2 %collective-permute-start.20 = (f32[8,3072]{1,0:T(8,128)}, f32[8,3072]{1,0:T(8,128)S(1)}, u32[]{:S(2)}, u32[]{:S(2)}) collective-permute-start(f32[8,3072]{1,0:T(8,128)} %get-tuple-element.61), channel_id=1, source_target_pairs={{0,4},{1,5},{2,6},{3,7},{4,0},{5,1},{6,2},{7,3},{8,12},{9,13},{10,... | collective-permute-start | bytes 294920 | tf_op jit(solution)/shard_map/ppermute | solution.py:316
  167.9 7.6 %place_and_smooth.2.rest_9_ = f32[1,16,128,256]{3,2,1,0:T(8,128)} custom-call(s32[8]{0:T(128)} %widths.7, f32[128,8,256]{2,1,0:T(8,128)} %get-tuple-element.67.diff, f32[8,16,3072]{2,1,0:T(8,128)} %copy-done, f32[8,3072]{1,0:T(8,128)} %get-tuple-element.68.rest_1_, f32[8,3072]{1,0:T(8,128)} %copy-done.26, f32[8,3072]{1,0:T(8,128)} %copy-done.27, ...), custom_call_target="tpu_custom_call" | custom-call | tf_op jit(solution)/shard_map/place_and_smooth/pallas_call | solution.py:472
  176.4 3.9 %collective-permute-done.24.rest_7_ = f32[8,3072]{1,0:T(8,128)S(1)} collective-permute-done((f32[8,3072]{1,0:T(8,128)S(1)}, f32[8,3072]{1,0:T(8,128)S(1)}, u32[]{:S(2)}, u32[]{:S(2)}) %collective-permute-start.24) | collective-permute-done | bytes 98336 | tf_op jit(solution)/shard_map/ppermute | solution.py:316
  181.0 7.6 %place_and_smooth.3 = f32[1,16,128,256]{3,2,1,0:T(8,128)} custom-call(s32[8]{0:T(128)} %widths.7, f32[128,8,256]{2,1,0:T(8,128)} %get-tuple-element.42.diff, f32[8,16,3072]{2,1,0:T(8,128)} %copy-done, f32[8,3072]{1,0:T(8,128)} %get-tuple-element.59.rest_1_, f32[8,3072]{1,0:T(8,128)} %copy-done.14, ...), custom_call_target="tpu_custom_call", output_to_operand_aliasing={{}: (11, {})} | custom-call | tf_op jit(solution)/shard_map/place_and_smooth/pallas_call | solution.py:472
  (168 shorter events, 54.8 us)
Async XLA Ops:
  8.2 42.0 %all-to-all-start = ((f32[8,8,3072]{2,1,0:T(8,128)}), f32[8,8,3072]{2,1,0:T(8,128)S(1)}, u32[]{:S(2)}, u32[]{:S(2)}) async-start(f32[8,8,3072]{2,1,0:T(8,128)} %get-tuple-element.43), calls=%async_computation | async-start | bytes 1572864 | tf_op jit(solution)/shard_map/all_to_all | solution.py:313
  25.8 10.7 %collective-permute-start.1 = (f32[8,3072]{1,0:T(8,128)}, f32[8,3072]{1,0:T(8,128)S(1)}, u32[]{:S(2)}, u32[]{:S(2)}) collective-permute-start(f32[8,3072]{1,0:T(8,128)} %get-tuple-element.46), channel_id=1, source_target_pairs={{0,2},{1,3},{2,0},{3,1},{4,6},{5,7},{6,4},{7,5},{8,10},{9,11},{10,... | collective-permute-start | bytes 294920 | tf_op jit(solution)/shard_map/ppermute | solution.py:316
  27.3 10.1 %collective-permute-start.2 = (f32[8,3072]{1,0:T(8,128)}, f32[8,3072]{1,0:T(8,128)S(1)}, u32[]{:S(2)}, u32[]{:S(2)}) collective-permute-start(f32[8,3072]{1,0:T(8,128)} %get-tuple-element.47), channel_id=1, source_target_pairs={{0,3},{1,2},{2,1},{3,0},{4,7},{5,6},{6,5},{7,4},{8,11},{9,10},{10,... | collective-permute-start | bytes 294920 | tf_op jit(solution)/shard_map/ppermute | solution.py:316
  27.4 20.2 %collective-permute-start.3 = (f32[8,3072]{1,0:T(8,128)}, f32[8,3072]{1,0:T(8,128)S(1)}, u32[]{:S(2)}, u32[]{:S(2)}) collective-permute-start(f32[8,3072]{1,0:T(8,128)} %get-tuple-element.48), channel_id=1, source_target_pairs={{0,4},{1,5},{2,6},{3,7},{4,0},{5,1},{6,2},{7,3},{8,12},{9,13},{10,... | collective-permute-start | bytes 294920 | tf_op jit(solution)/shard_map/ppermute | solution.py:316
  30.2 19.9 %collective-permute-start.4 = (f32[8,3072]{1,0:T(8,128)}, f32[8,3072]{1,0:T(8,128)S(1)}, u32[]{:S(2)}, u32[]{:S(2)}) collective-permute-start(f32[8,3072]{1,0:T(8,128)} %get-tuple-element.49), channel_id=1, source_target_pairs={{0,5},{1,4},{2,7},{3,6},{4,1},{5,0},{6,3},{7,2},{8,13},{9,12},{10,... | collective-permute-start | bytes 294920 | tf_op jit(solution)/shard_map/ppermute | solution.py:316
  33.2 16.9 %collective-permute-start.5 = (f32[8,3072]{1,0:T(8,128)S(1)}, f32[8,3072]{1,0:T(8,128)S(1)}, u32[]{:S(2)}, u32[]{:S(2)}) collective-permute-start(f32[8,3072]{1,0:T(8,128)S(1)} %copy-done.41), channel_id=1, source_target_pairs={{0,6},{1,7},{2,4},{3,5},{4,2},{5,3},{6,0},{7,1},{8,14},{9,15},{10,... | collective-permute-start | bytes 294920 | tf_op jit(solution)/shard_map/ppermute | solution.py:316
  36.5 13.6 %collective-permute-start.6 = (f32[8,3072]{1,0:T(8,128)S(1)}, f32[8,3072]{1,0:T(8,128)S(1)}, u32[]{:S(2)}, u32[]{:S(2)}) collective-permute-start(f32[8,3072]{1,0:T(8,128)S(1)} %copy-done.40), channel_id=1, source_target_pairs={{0,7},{1,6},{2,5},{3,4},{4,3},{5,2},{6,1},{7,0},{8,15},{9,14},{10,... | collective-permute-start | bytes 294920 | tf_op jit(solution)/shard_map/ppermute | solution.py:316
  55.1 10.1 %collective-permute-start.7 = (f32[1536,128]{1,0:T(8,128)}, f32[1536,128]{1,0:T(8,128)}, u32[]{:S(2)}, u32[]{:S(2)}) collective-permute-start(f32[1536,128]{1,0:T(8,128)} %get-tuple-element.53), channel_id=1, source_target_pairs={{0,8},{8,0},{16,24},{24,16},{1,9},{9,1},{17,25},{25,17},{2,10},{10... | collective-permute-start | bytes 2359304 | tf_op jit(solution)/shard_map/ppermute | solution.py:445
  55.2 42.8 %all-to-all-start.2 = ((f32[8,16,3072]{2,1,0:T(8,128)}), f32[8,16,3072]{2,1,0:T(8,128)S(1)}, u32[]{:S(2)}, u32[]{:S(2)}) async-start(f32[8,16,3072]{2,1,0:T(8,128)} %get-tuple-element.56), calls=%async_computation.2 | async-start | bytes 3145728 | tf_op jit(solution)/shard_map/all_to_all | solution.py:313
  66.4 19.7 %collective-permute-start.8 = (f32[1536,128]{1,0:T(8,128)S(1)}, f32[1536,128]{1,0:T(8,128)S(1)}, u32[]{:S(2)}, u32[]{:S(2)}) collective-permute-start(f32[1536,128]{1,0:T(8,128)S(1)} %add.57), channel_id=1, source_target_pairs={{0,16},{8,24},{16,0},{24,8},{1,17},{9,25},{17,1},{25,9},{2,18},{10... | collective-permute-start | bytes 2359304 | tf_op jit(solution)/shard_map/ppermute | solution.py:448
  98.0 68.8 %all-to-all-start.1 = ((f32[8,16,3072]{2,1,0:T(8,128)}), f32[8,16,3072]{2,1,0:T(8,128)S(1)}, u32[]{:S(2)}, u32[]{:S(2)}) async-start(f32[8,16,3072]{2,1,0:T(8,128)} %filter_backward.2), calls=%async_computation.1 | async-start | bytes 3145728 | tf_op jit(solution)/shard_map/all_to_all | solution.py:313
  109.0 12.7 %collective-permute-start.11 = (f32[512,128]{1,0:T(8,128)S(1)}, f32[512,128]{1,0:T(8,128)S(1)}, u32[]{:S(2)}, u32[]{:S(2)}) collective-permute-start(f32[512,128]{1,0:T(8,128)S(1)} %get-tuple-element.82), channel_id=1, source_target_pairs={{0,16},{8,24},{16,0},{24,8},{1,17},{9,25},{17,1},{25,9},{2,18},{10... | collective-permute-start | bytes 786440 | tf_op jit(solution)/shard_map/ppermute | solution.py:448
  110.6 13.2 %collective-permute-start.13 = (f32[512,128]{1,0:T(8,128)S(1)}, f32[512,128]{1,0:T(8,128)S(1)}, u32[]{:S(2)}, u32[]{:S(2)}) collective-permute-start(f32[512,128]{1,0:T(8,128)S(1)} %get-tuple-element.81), channel_id=1, source_target_pairs={{0,16},{8,24},{16,0},{24,8},{1,17},{9,25},{17,1},{25,9},{2,18},{10... | collective-permute-start | bytes 786440 | tf_op jit(solution)/shard_map/ppermute | solution.py:448
  111.1 17.6 %collective-permute-start.15 = (f32[512,128]{1,0:T(8,128)S(1)}, f32[512,128]{1,0:T(8,128)S(1)}, u32[]{:S(2)}, u32[]{:S(2)}) collective-permute-start(f32[512,128]{1,0:T(8,128)S(1)} %get-tuple-element.80), channel_id=1, source_target_pairs={{0,16},{8,24},{16,0},{24,8},{1,17},{9,25},{17,1},{25,9},{2,18},{10... | collective-permute-start | bytes 786440 | tf_op jit(solution)/shard_map/ppermute | solution.py:448
  137.2 14.9 %collective-permute-start.25 = (f32[8,3072]{1,0:T(8,128)}, f32[8,3072]{1,0:T(8,128)S(1)}, u32[]{:S(2)}, u32[]{:S(2)}) collective-permute-start(f32[8,3072]{1,0:T(8,128)} %get-tuple-element.69), channel_id=1, source_target_pairs={{0,4},{1,5},{2,6},{3,7},{4,0},{5,1},{6,2},{7,3},{8,12},{9,13},{10,... | collective-permute-start | bytes 294920 | tf_op jit(solution)/shard_map/ppermute | solution.py:316
  140.2 15.9 %collective-permute-start.26 = (f32[8,3072]{1,0:T(8,128)}, f32[8,3072]{1,0:T(8,128)S(1)}, u32[]{:S(2)}, u32[]{:S(2)}) collective-permute-start(f32[8,3072]{1,0:T(8,128)} %get-tuple-element.70), channel_id=1, source_target_pairs={{0,5},{1,4},{2,7},{3,6},{4,1},{5,0},{6,3},{7,2},{8,13},{9,12},{10,... | collective-permute-start | bytes 294920 | tf_op jit(solution)/shard_map/ppermute | solution.py:316
  141.7 14.4 %collective-permute-start.27 = (f32[8,3072]{1,0:T(8,128)}, f32[8,3072]{1,0:T(8,128)S(1)}, u32[]{:S(2)}, u32[]{:S(2)}) collective-permute-start(f32[8,3072]{1,0:T(8,128)} %get-tuple-element.71), channel_id=1, source_target_pairs={{0,6},{1,7},{2,4},{3,5},{4,2},{5,3},{6,0},{7,1},{8,14},{9,15},{10,... | collective-permute-start | bytes 294920 | tf_op jit(solution)/shard_map/ppermute | solution.py:316
  144.9 13.8 %collective-permute-start.28 = (f32[8,3072]{1,0:T(8,128)}, f32[8,3072]{1,0:T(8,128)S(1)}, u32[]{:S(2)}, u32[]{:S(2)}) collective-permute-start(f32[8,3072]{1,0:T(8,128)} %get-tuple-element.72), channel_id=1, source_target_pairs={{0,7},{1,6},{2,5},{3,4},{4,3},{5,2},{6,1},{7,0},{8,15},{9,14},{10,... | collective-permute-start | bytes 294920 | tf_op jit(solution)/shard_map/ppermute | solution.py:316
  145.0 16.9 %collective-permute-start.29 = (f32[8,3072]{1,0:T(8,128)}, f32[8,3072]{1,0:T(8,128)S(1)}, u32[]{:S(2)}, u32[]{:S(2)}) collective-permute-start(f32[8,3072]{1,0:T(8,128)} %get-tuple-element.73), channel_id=1, source_target_pairs={{0,3},{1,2},{2,1},{3,0},{4,7},{5,6},{6,5},{7,4},{8,11},{9,10},{10,... | collective-permute-start | bytes 294920 | tf_op jit(solution)/shard_map/ppermute | solution.py:316
  156.1 19.5 %collective-permute-start.19 = (f32[8,3072]{1,0:T(8,128)}, f32[8,3072]{1,0:T(8,128)S(1)}, u32[]{:S(2)}, u32[]{:S(2)}) collective-permute-start(f32[8,3072]{1,0:T(8,128)} %get-tuple-element.60), channel_id=1, source_target_pairs={{0,3},{1,2},{2,1},{3,0},{4,7},{5,6},{6,5},{7,4},{8,11},{9,10},{10,... | collective-permute-start | bytes 294920 | tf_op jit(solution)/shard_map/ppermute | solution.py:316
  158.7 16.9 %collective-permute-start.20 = (f32[8,3072]{1,0:T(8,128)}, f32[8,3072]{1,0:T(8,128)S(1)}, u32[]{:S(2)}, u32[]{:S(2)}) collective-permute-start(f32[8,3072]{1,0:T(8,128)} %get-tuple-element.61), channel_id=1, source_target_pairs={{0,4},{1,5},{2,6},{3,7},{4,0},{5,1},{6,2},{7,3},{8,12},{9,13},{10,... | collective-permute-start | bytes 294920 | tf_op jit(solution)/shard_map/ppermute | solution.py:316
  161.9 14.4 %collective-permute-start.21 = (f32[8,3072]{1,0:T(8,128)}, f32[8,3072]{1,0:T(8,128)S(1)}, u32[]{:S(2)}, u32[]{:S(2)}) collective-permute-start(f32[8,3072]{1,0:T(8,128)} %get-tuple-element.62), channel_id=1, source_target_pairs={{0,5},{1,4},{2,7},{3,6},{4,1},{5,0},{6,3},{7,2},{8,13},{9,12},{10,... | collective-permute-start | bytes 294920 | tf_op jit(solution)/shard_map/ppermute | solution.py:316
  162.0 14.3 %collective-permute-start.22 = (f32[8,3072]{1,0:T(8,128)}, f32[8,3072]{1,0:T(8,128)S(1)}, u32[]{:S(2)}, u32[]{:S(2)}) collective-permute-start(f32[8,3072]{1,0:T(8,128)} %get-tuple-element.63), channel_id=1, source_target_pairs={{0,6},{1,7},{2,4},{3,5},{4,2},{5,3},{6,0},{7,1},{8,14},{9,15},{10,... | collective-permute-start | bytes 294920 | tf_op jit(solution)/shard_map/ppermute | solution.py:316
  164.2 12.1 %collective-permute-start.23 = (f32[8,3072]{1,0:T(8,128)}, f32[8,3072]{1,0:T(8,128)S(1)}, u32[]{:S(2)}, u32[]{:S(2)}) collective-permute-start(f32[8,3072]{1,0:T(8,128)} %get-tuple-element.64), channel_id=1, source_target_pairs={{0,7},{1,6},{2,5},{3,4},{4,3},{5,2},{6,1},{7,0},{8,15},{9,14},{10,... | collective-permute-start | bytes 294920 | tf_op jit(solution)/shard_map/ppermute | solution.py:316
  (56 other events, 304.8 us)
